TPU v7x, 256 devices: a whole 4x4x8 slice. The times are simulated.
256 devices in a mesh: section: 8 (over y, core), dp: 32 (over z, x).
Axes of the slice: x: 4, y: 4, z: 8, core: 2. Of those that a mesh axis runs over, the one named last changes fastest.
Arguments:
- hidden_in: bfloat16 [8, 4096, 5120], P('section', 'dp'), may hold values from -400 to 400
- norm_gain: bfloat16 [8, 5120], P('section', 'dp'), may hold values from 0.5 to 1.5
- key_weight: bfloat16 [8, 5120, 512], P('section', 'dp'), may hold values from -0.078125 to 0.078125
- value_weight: bfloat16 [8, 5120, 512], P('section', 'dp'), may hold values from -0.078125 to 0.078125
- queries: bfloat16 [8, 4096, 4096], P('section', 'dp'), may hold values from -100 to 100
- stashed_keys: bfloat16 [8, 4096, 512], P('section', 'dp'), may hold values from -5 to 5
- stashed_values: bfloat16 [8, 4096, 512], P('section', 'dp'), may hold values from -6 to 6
- out_cotangent: bfloat16 [8, 4096, 4096], P('section', 'dp'), may hold values from -6 to 6
- logprob_grad: bfloat16 [4096, 5120], P('dp'), may hold values from -2 to 2
- new_logprob: float32 [4096], P('dp'), may hold values from -5 to 0.5
- old_logprob: float32 [4096], P('dp'), may hold values from -5 to 0.5
- advantages: float32 [32, 4], P('dp'), may hold values from -3 to 3
- segment_ids: int32 [32, 128], P('dp'), may hold values from 0 to 3, never falling along the last dimension, each value on 1 to 96 neighbouring positions
Outputs:
- hidden_cotangent: bfloat16 [8, 4096, 5120], P('section', 'dp')
- key_weight_grad: float32 [8, 5120, 512], P('section', 'dp')
- value_weight_grad: float32 [8, 5120, 512], P('section', 'dp')
Inputs may be any that keep to these rules, and one draw needn't show every extreme that they name: `segment_ids`: within each block the ids never fall, every rollout has 1 to 96 rows, and one has exactly 96.
All inputs are finite; a program needn't handle non-finite values.
Results may differ from a plain program's by a relative error of at most 0.023.
Values may be sent and summed in bfloat16 or wider, within the bound.
No kernel may reach another device: no remote copies, remote signals or barrier semaphores. Data moves between devices by JAX's collectives and lax.ppermute only.
A program may use at most 128 MiB of HBM per device.

v0:
```python
import math

import jax
import jax.numpy as jnp
from jax import lax
from jax.sharding import PartitionSpec as P

HD = 128
KVH = 4
GROUP = 8
KVW = 512


EPSILON = 1e-06


def carried_in(shard, axis, join, neutral):
    count = lax.axis_size(axis)
    place = lax.axis_index(axis)
    ahead = count - 1 - place
    gathered = lax.all_gather(shard.astype(jnp.bfloat16), axis)
    state = jnp.zeros_like(shard) + jnp.asarray(neutral, shard.dtype)

    def one(turn, state):
        source = count - 1 - turn
        return join(state, lax.dynamic_index_in_dim(gathered, source, 0, False).astype(shard.dtype))

    return lax.fori_loop(0, ahead, one, state)


def attend_back(queries, stashed_keys, stashed_values, out_cotangent, segments):
    row_count = queries.shape[0]
    score_scale = 1.0 / math.sqrt(HD)
    query_half = queries.reshape(row_count, KVH, GROUP, HD)
    key_half = stashed_keys.reshape(row_count, KVH, HD)
    value_half = stashed_values.reshape(row_count, KVH, HD)
    cot_half = out_cotangent.reshape(row_count, KVH, GROUP, HD)
    position = jnp.arange(row_count)
    allowed = (segments[:, None] == segments[None, :]) & (position[None, :] <= position[:, None])
    scores = (
        jnp.einsum("igne,jge->gnij", query_half, key_half, preferred_element_type=jnp.float32)
        * score_scale
    )
    scores = jnp.where(allowed[None, None], scores, -jnp.inf)
    highest = jnp.max(scores, axis=-1, keepdims=True)
    exp_scores = jnp.exp(scores - highest)
    probs_full = exp_scores / jnp.sum(exp_scores, axis=-1, keepdims=True)
    probs_half = probs_full.astype(jnp.bfloat16)
    attended = jnp.einsum(
        "gnij,jge->igne", probs_half, value_half, preferred_element_type=jnp.float32
    )
    row_delta = jnp.sum(cot_half.astype(jnp.float32) * attended, axis=-1)
    prob_cot = jnp.einsum(
        "igne,jge->gnij", cot_half, value_half, preferred_element_type=jnp.float32
    )
    score_cot = (probs_full * (prob_cot - jnp.transpose(row_delta, (1, 2, 0))[..., None])).astype(
        jnp.bfloat16
    )
    key_cot = (
        jnp.einsum("gnij,igne->jge", score_cot, query_half, preferred_element_type=jnp.float32)
        * score_scale
    )
    value_cot = jnp.einsum(
        "gnij,igne->jge", probs_half, cot_half, preferred_element_type=jnp.float32
    )
    return (
        key_cot.astype(jnp.bfloat16).reshape(row_count, KVW),
        value_cot.astype(jnp.bfloat16).reshape(row_count, KVW),
    )


def add_terms(first_term, second_term):
    return first_term + second_term


def local(
    hidden_in,
    norm_gain,
    key_weight,
    value_weight,
    queries,
    stashed_keys,
    stashed_values,
    out_cotangent,
    logprob_grad,
    new_logprob,
    old_logprob,
    advantages,
    segment_ids,
):
    kv_width = stashed_keys.shape[2]
    stream = hidden_in[0].astype(jnp.float32)
    inv_rms = lax.rsqrt(jnp.mean(stream * stream, axis=-1, keepdims=True) + EPSILON)
    normed = stream * inv_rms
    segments = segment_ids[0]
    key_cot, value_cot = attend_back(
        queries[0], stashed_keys[0], stashed_values[0], out_cotangent[0], segments
    )
    kv_cot = jnp.concatenate([key_cot, value_cot], axis=1)
    key_full, value_full, gain_half = (
        lax.all_gather(key_weight[0], "dp", axis=0, tiled=True),
        lax.all_gather(value_weight[0], "dp", axis=0, tiled=True),
        lax.all_gather(norm_gain[0], "dp", axis=0, tiled=True),
    )
    gain_full = gain_half.astype(jnp.float32)
    scaled = (normed * gain_full).astype(jnp.bfloat16)
    weight_pair = jnp.concatenate([key_full, value_full], axis=1)
    scaled_cot = (
        lax.dot_general(
            kv_cot, weight_pair, (((1,), (1,)), ((), ())), preferred_element_type=jnp.float32
        )
        * gain_full
    )
    weight_grad = lax.psum_scatter(
        lax.dot_general(
            scaled, kv_cot, (((0,), (0,)), ((), ())), preferred_element_type=jnp.float32
        ).astype(jnp.bfloat16),
        "dp",
        scatter_dimension=0,
        tiled=True,
    ).astype(jnp.float32)
    local_term = inv_rms * (
        scaled_cot - normed * jnp.mean(scaled_cot * normed, axis=-1, keepdims=True)
    )
    upper_sum = carried_in(local_term, "section", add_terms, jnp.zeros_like(local_term))
    rollout_index = jnp.arange(advantages.shape[1])
    row_adv = jnp.sum(
        jnp.where(segments[:, None] == rollout_index[None, :], advantages[0][None, :], 0.0), axis=1
    )
    ratio = jnp.exp(new_logprob - old_logprob)
    coefficient = -jnp.clip(ratio, 0.8, 1.28) * row_adv
    top_term = coefficient[:, None] * logprob_grad.astype(jnp.float32)
    hidden_cotangent = (top_term + upper_sum + local_term).astype(jnp.bfloat16)
    return (
        hidden_cotangent[None],
        weight_grad[:, :kv_width][None],
        weight_grad[:, kv_width:][None],
    )


def solution(mesh):
    return jax.shard_map(
        local,
        mesh=mesh,
        in_specs=(
            P("section", "dp", None),
            P("section", "dp"),
            P("section", "dp", None),
            P("section", "dp", None),
            P("section", "dp", None),
            P("section", "dp", None),
            P("section", "dp", None),
            P("section", "dp", None),
            P("dp", None),
            P("dp"),
            P("dp"),
            P("dp", None),
            P("dp", None),
        ),
        out_specs=(P("section", "dp", None), P("section", "dp", None), P("section", "dp", None)),
        check_vma=False,
    )
```

profile of v0, /device:TPU:1, one launch (start us, length us, event | category | flops | bytes accessed | tf_op | source)
XLA Modules:
  0.0 505.1 jit_solution(5553301425859973452)
XLA Ops:
  7.2 0.0 copy-start.3
  7.2 0.0 all-gather.8.cloned.1.call-start
  7.2 0.7 all-gather.8.cloned.1.call-update
  7.9 0.0 all-gather.10.cloned.1.call-start
  8.0 0.7 all-gather.10.cloned.1.call-update
  8.7 0.0 reduce-scatter.2.cloned.1.call-start
  8.7 1.3 dynamic-slice
  10.6 0.7 reduce
  11.3 0.2 dynamic-update-slice
  11.6 119.4 %all-reduce = bf16[5120]{0:T(1024)(128)(2,1)S(1)} all-reduce(bf16[5120]{0:T(1024)(128)(2,1)S(1)} %dynamic-update-slice), channel_id=4, replica_groups=mesh['section'=8,'dp'=32] {'dp'}, use_global_device_ids=true, to_apply=%add | all-reduce | flops 5120 | bytes 20480
  131.0 0.6 convert_element_type.76
  131.6 0.9 reshape_squeeze.14
  132.5 0.0 copy-start.5
  132.5 1.0 reshape_squeeze.12
  133.5 1.6 copy.50
  135.1 0.0 copy-start.4
  135.2 0.0 copy-start.8
  135.2 0.0 copy-done.3
  135.2 0.2 copy.51
  135.4 1.7 copy.39
  137.1 0.0 copy-done.8
  137.1 0.1 fusion.46
  137.2 2.1 fusion.53
  139.3 0.0 copy-done.4
  139.3 1.8 fusion.35
  141.2 0.0 copy-start
  141.2 1.7 copy.33
  142.9 0.0 copy-done.5
  142.9 2.8 fusion.16
  145.7 1.7 copy.35
  147.4 0.0 copy-done
  147.4 0.3 fusion.15
  147.7 0.5 add_rsqrt_fusion
  148.3 1.7 fusion.30
  149.9 0.0 copy-done.2
  149.9 0.0 copy-start.6
  150.0 0.0 copy-start.7
  150.0 2.7 fusion.29
  152.7 0.0 copy-done.6
  152.7 0.0 copy-done.7
  152.7 5.6 %convolution_convert_fusion = bf16[5120,1024]{1,0:T(8,128)(2,1)} fusion(bf16[1,128,5120]{2,1,0:T(8,128)(2,1)S(1)} %copy-done, f32[5120]{0:T(1024)S(1)} %copy-done.6, f32[128]{0:T(128)S(1)} %copy-done.7, bf16[128,512]{0,1:T(8,128)(2,1)S(1)} %bitcast.94, bf16[128,512]{0,1:T(8,128)(2,1)S(1)} %bitcast.97), kind=kOutput, calls=%fused_computation.6 | convolution fusion | flops 1350565888 | bytes 12079616 | tf_op jit(solution)/shard_map/dot_general | solution.py:115
  158.3 0.0 reduce-scatter.2.cloned.1.call-update
  158.4 0.0 all-gather.12.cloned.1.call-start
  158.4 0.6 copy-done.9
  159.0 0.0 copy-done.12
  159.0 0.1 select_reduce_fusion
  159.1 23.3 %all-gather.10.cloned.1.call-done = bf16[1,5120,512]{2,1,0:T(8,128)(2,1)} async-done(((bf16[1,160,512]{2,1,0:T(8,128)(2,1)}), bf16[1,5120,512]{2,1,0:T(8,128)(2,1)}) %all-gather.10.cloned.1.call-update) | async-done | bytes 5242896 | tf_op jit(solution)/shard_map/all_gather | solution.py:102
  182.4 6.5 %fusion.11 = (f32[128]{0:T(128)S(1)}, f32[128,5120]{1,0:T(8,128)S(1)}) fusion(bf16[1,128,5120]{2,1,0:T(8,128)(2,1)S(1)} %copy-done, f32[128]{0:T(128)S(1)} %copy-done.7, f32[5120]{0:T(1024)S(1)} %copy-done.6, bf16[5120,512]{1,0:T(8,128)(2,1)} %bitcast.103, bf16[5120,512]{1,0:T(8,128)(2,1)} %bitcast.102, bf16[128,512]{0,1:T(8,128)(2,1)S(1)} %bitcast.95, ...), kind=kOutput, calls=%fused_computation.13 | convolution fusion | flops 1366949760 | bytes 14701568 | tf_op jit(solution)/shard_map/dot_general | solution.py:109
  189.0 1.5 copy-done.1
  190.4 1.6 fusion.21
  192.1 0.0 all-gather.12.cloned.1.call-update
  192.1 223.7 %reduce-scatter.2.cloned.1.call-done = bf16[160,1024]{1,0:T(8,128)(2,1)} async-done(((bf16[5120,1024]{1,0:T(8,128)(2,1)}), bf16[160,1024]{1,0:T(8,128)(2,1)}) %reduce-scatter.2.cloned.1.call-update) | async-done | bytes 327696 | tf_op jit(solution)/shard_map/reduce_scatter | solution.py:114
  415.8 1.0 convert_element_type.72
  416.9 0.9 slice_bitcast_fusion
  417.8 64.5 %all-gather.12.cloned.1.call-done = bf16[1024,5120]{1,0:T(8,128)(2,1)} async-done(((bf16[128,5120]{1,0:T(8,128)(2,1)}), bf16[1024,5120]{1,0:T(8,128)(2,1)}) %all-gather.12.cloned.1.call-update) | async-done | bytes 10485776 | tf_op jit(solution)/shard_map/all_gather | solution.py:21
  482.2 0.2 broadcast_in_dim.53
  482.5 11.6 %while.12 = (s32[]{:T(128)}, f32[128,5120]{1,0:T(8,128)S(1)}, s32[]{:T(128)}, bf16[8,128,5120]{2,1,0:T(8,128)(2,1)}, s32[]{:T(128)}, /*index=5*/s32[]{:T(128)}, s32[]{:T(128)}, s32[]{:T(128)}) while((s32[]{:T(128)}, f32[128,5120]{1,0:T(8,128)S(1)}, s32[]{:T(128)}, bf16[8,128,5120]{2,1,0:T(8,128)(2,1)}, s32[]{:T(128)}, /*index=5*/s32[]{:T(128)}, ...), condition=%wide.region_7.8_spmd, body=%wide.region_6.7_spmd.sunk | while | flops 1310726 | bytes 6553743 | solution.py:28
  482.5 1.9 convert_add_fusion.2
  484.4 1.9 convert_add_fusion.2
  486.3 1.9 convert_add_fusion.2
  488.3 1.9 convert_add_fusion.2
  490.2 1.9 convert_add_fusion.2
  492.1 1.9 convert_add_fusion.2
  494.0 4.6 fusion.22
  (11 shorter events, 0.0 us)
Async XLA Ops:
  7.2 128.0 %copy-start.3 = (bf16[1,128,4096]{2,1,0:T(8,128)(2,1)S(1)}, bf16[1,128,4096]{2,1,0:T(8,128)(2,1)}, u32[]{:S(2)}) copy-start(bf16[1,128,4096]{2,1,0:T(8,128)(2,1)} %param.22) | copy-start | bytes 3145732
  7.2 151.9 %all-gather.8.cloned.1.call-start = ((), (), s32[]{:S(2)}) async-start(), calls=%async_computation.2 | async-start | bytes 5406720 | tf_op jit(solution)/shard_map/all_gather | solution.py:101
  7.9 174.5 %all-gather.10.cloned.1.call-start = ((), (), s32[]{:S(2)}) async-start(), calls=%async_computation.3 | async-start | bytes 5406720 | tf_op jit(solution)/shard_map/all_gather | solution.py:102
  8.7 407.2 %reduce-scatter.2.cloned.1.call-start = ((), (), s32[]{:S(2)}) async-start(), calls=%async_computation.1 | async-start | bytes 10813440 | tf_op jit(solution)/shard_map/reduce_scatter | solution.py:114
  132.5 10.4 %copy-start.5 = (bf16[128,4,128]{2,1,0:T(4,128)(2,1)}, bf16[128,4,128]{2,1,0:T(4,128)(2,1)S(1)}, u32[]{:S(2)}) copy-start(bf16[128,4,128]{2,1,0:T(4,128)(2,1)S(1)} %reshape_squeeze.14) | copy-start | bytes 393220
  135.1 4.2 copy-start.4
  135.2 2.0 copy-start.8
  141.2 6.2 %copy-start = (bf16[1,128,5120]{2,1,0:T(8,128)(2,1)S(1)}, bf16[1,128,5120]{2,1,0:T(8,128)(2,1)}, u32[]{:S(2)}) copy-start(bf16[1,128,5120]{2,1,0:T(8,128)(2,1)} %param.15) | copy-start | bytes 3932164
  145.7 4.3 copy-start.2
  149.9 2.7 copy-start.6
  150.0 2.7 copy-start.7
  158.3 0.7 copy-start.9
  158.3 0.7 copy-start.12
  158.4 323.9 %all-gather.12.cloned.1.call-start = ((), (), s32[]{:S(2)}) async-start(), calls=%async_computation.4 | async-start | bytes 11796480 | tf_op jit(solution)/shard_map/all_gather | solution.py:21
  182.4 6.5 %copy-start.10 = (f32[128]{0:T(128)S(1)}, f32[128]{0:T(128)}, u32[]{:S(2)}) copy-start(f32[128]{0:T(128)} %param.24) | copy-start | bytes 1540
  182.4 6.5 %copy-start.11 = (f32[128]{0:T(128)S(1)}, f32[128]{0:T(128)}, u32[]{:S(2)}) copy-start(f32[128]{0:T(128)} %param.25) | copy-start | bytes 1540
  188.9 1.5 copy-start.1
Sparse Core Ops, SparseCore 0:
  10.6 87.1 all-gather.7
  100.4 81.9 all-gather.9
  186.5 229.3 reduce-scatter.1
  418.3 63.9 all-gather.11
where the time goes:
time: 506 us; the launch traced here: 505 us
  waiting for transfers between devices  313 us (62%)
  blocking collectives  119 us (24%)
  other arithmetic  22.9 us (5%)
  matrix products  21.3 us (4%)
  between operations  14.6 us (3%)
  local copies, waits for them, and re-layouts  13.7 us (3%)
    reduce_scatter x1, waiting for transfers between devices, local(): lax.psum_scatter(lax.dot_general(scaled, kv_cot, (((0,), (0,)), ((), ()))...  224 us
    unnamed x1, blocking collectives  119 us
    all_gather x1, waiting for transfers between devices, carried_in(): gathered = lax.all_gather(shard.astype(jnp.bfloat16), axis)  64.5 us
    all_gather x1, waiting for transfers between devices, local(): lax.all_gather(value_weight[0], 'dp', axis=0, tiled=True)  23.3 us
    add x6, other arithmetic, add_terms(): return first_term + second_term  11.4 us
  transfers between devices with their start and end apart: 4, of which 3 were waited for; matrix products, arithmetic and copies ran while one was open for 8% of the time, Pallas kernels for 0%

commit v1 on v0

v1 whole, which is shorter than its diff:
```python
import functools
import math

import jax
import jax.numpy as jnp
from jax import lax
from jax.experimental import pallas as pl
from jax.experimental.pallas import tpu as pltpu
from jax.sharding import PartitionSpec as P

D = 5120
HD = 128
KVH = 4
GROUP = 8
KVW = 512
ROWS = 128
NZ = 8
NX = 4
NY = 4
SLAB = D // (NZ * NX)
EPSILON = 1e-06
VMEM = pltpu.CompilerParams(vmem_limit_bytes=48 * 1024 * 1024)
NT = (((1,), (1,)), ((), ()))

Z_FIRST = (0, 1, 7, 2, 6)
Z_LAST = (3, 5, 4)


def shape_of(shape, dtype=jnp.bfloat16):
    return jax.ShapeDtypeStruct(shape, dtype)


def whole(count):
    return [pl.BlockSpec(memory_space=pltpu.VMEM)] * count


def fetched(*shapes):
    return [pl.BlockSpec(shape, lambda *_, n=len(shape): (0,) * n) for shape in shapes]


def after(values, *first):
    return lax.optimization_barrier((values, first))[0]


def cost(flops, moved, exps=0):
    return pl.CostEstimate(flops=flops, bytes_accessed=moved, transcendentals=exps)


def shift_z(value, step):
    pairs = [(z * NX + x, ((z + step) % NZ) * NX + x) for z in range(NZ) for x in range(NX)]
    return lax.ppermute(value, "dp", pairs)


def shift_x(value, step):
    pairs = [(z * NX + x, z * NX + (x + step) % NX) for z in range(NZ) for x in range(NX)]
    return lax.ppermute(value, "dp", pairs)


def swap_core(value):
    return lax.ppermute(value, "section", [(s, s ^ 1) for s in range(2 * NY)])


def send_y(value, routes):
    pairs = [(2 * a + c, 2 * b + c) for a, b in routes for c in range(2)]
    return lax.ppermute(value, "section", pairs)


def place():
    own = lax.axis_index("dp")
    layer = lax.axis_index("section")
    return own // NX, own % NX, layer // 2, layer % 2


def turn_kernel(h_ref, o0, o1, o2, o3, held):
    z, x, _, _ = place()
    for tile in range(D // 128):
        turned = h_ref[:, tile * 128 : (tile + 1) * 128].T
        for piece in range(4):
            unit = tile * 4 + piece
            slab, part = unit // 5, unit % 5
            k = lax.rem(slab // NX - z + NZ, NZ)
            d = lax.rem(slab % NX - x + NX, NX)
            held[d, k, part * 32 : (part + 1) * 32, :] = turned[piece * 32 : (piece + 1) * 32, :]
    for d, out in enumerate((o0, o1, o2, o3)):
        out[...] = held[d]


def turn(hidden):
    return pl.pallas_call(
        turn_kernel,
        out_shape=[shape_of((NZ, SLAB, ROWS))] * NX,
        in_specs=fetched((ROWS, D)),
        out_specs=whole(NX),
        scratch_shapes=[pltpu.VMEM((NX, NZ, SLAB, ROWS), jnp.bfloat16)],
        compiler_params=VMEM,
        cost_estimate=cost(0, 4 * D * ROWS),
        name="turn",
    )(hidden)


def attend_kernel(q_ref, k_ref, v_ref, o_ref, row_ref, h_ref, out_ref):
    squares = jnp.zeros((ROWS, 128), jnp.float32)
    for tile in range(D // 128):
        part = h_ref[:, tile * 128 : (tile + 1) * 128].astype(jnp.float32)
        squares = squares + part * part
    inv_rms = lax.rsqrt(jnp.sum(squares, axis=1, keepdims=True) * (1.0 / D) + EPSILON)
    j_place = lax.broadcasted_iota(jnp.int32, (ROWS, ROWS), 0)
    i_place = lax.broadcasted_iota(jnp.int32, (ROWS, ROWS), 1)
    segment = jnp.broadcast_to(row_ref[...].astype(jnp.float32), (ROWS, ROWS))
    allowed = (segment.T == segment) & (j_place <= i_place)
    scale = 1.0 / math.sqrt(HD)
    for g in range(KVH):
        key = k_ref[:, g * HD : (g + 1) * HD]
        value = v_ref[:, g * HD : (g + 1) * HD]
        heads = range(g * GROUP, (g + 1) * GROUP)
        query = jnp.concatenate([q_ref[:, n * HD : (n + 1) * HD] for n in heads], axis=0)
        cot = jnp.concatenate([o_ref[:, n * HD : (n + 1) * HD] for n in heads], axis=0)
        scores = lax.dot_general(key, query, NT, preferred_element_type=jnp.float32) * scale
        prob_cot = lax.dot_general(value, cot, NT, preferred_element_type=jnp.float32)
        halves, cots = [], []
        for n in range(GROUP):
            span = slice(n * ROWS, (n + 1) * ROWS)
            score = jnp.where(allowed, scores[:, span], -jnp.inf)
            high = jnp.max(score, axis=0, keepdims=True)
            grown = jnp.exp(score - high)
            probs = grown * (1.0 / jnp.sum(grown, axis=0, keepdims=True))
            half = probs.astype(jnp.bfloat16)
            pulled = prob_cot[:, span]
            delta = jnp.sum(half.astype(jnp.float32) * pulled, axis=0, keepdims=True)
            halves.append(half)
            cots.append((probs * (pulled - delta)).astype(jnp.bfloat16))
        key_cot = jnp.dot(jnp.concatenate(cots, axis=1), query, preferred_element_type=jnp.float32)
        value_cot = jnp.dot(jnp.concatenate(halves, axis=1), cot, preferred_element_type=jnp.float32)
        key_cot = (key_cot * scale).astype(jnp.bfloat16).astype(jnp.float32)
        value_cot = value_cot.astype(jnp.bfloat16).astype(jnp.float32)
        out_ref[:, g * HD : (g + 1) * HD] = (key_cot * inv_rms).astype(jnp.bfloat16)
        out_ref[:, KVW + g * HD : KVW + (g + 1) * HD] = (value_cot * inv_rms).astype(jnp.bfloat16)


def attend(queries, keys, values, cotangent, row, hidden):
    return pl.pallas_call(
        attend_kernel,
        out_shape=shape_of((ROWS, 2 * KVW)),
        in_specs=fetched(
            (ROWS, KVH * GROUP * HD), (ROWS, KVW), (ROWS, KVW), (ROWS, KVH * GROUP * HD), (1, ROWS), (ROWS, D)
        ),
        out_specs=pl.BlockSpec(memory_space=pltpu.VMEM),
        compiler_params=VMEM,
        cost_estimate=cost(4 * 32 * 2 * 128**3, 4 * 2**20, 32 * 128 * 128),
        name="attend",
    )(queries, keys, values, cotangent, row, hidden)


def grad_kernel(*refs):
    turned, cots, outs = refs[:NX], refs[NX : 2 * NX], refs[2 * NX : 2 * NX + NZ]
    left = jnp.concatenate([ref[...].reshape(NZ * SLAB, ROWS) for ref in turned], axis=1)
    right = jnp.concatenate([ref[...] for ref in cots], axis=0)
    for k in range(NZ):
        outs[k][...] = jnp.dot(
            left[k * SLAB : (k + 1) * SLAB], right, preferred_element_type=jnp.float32
        ).astype(jnp.bfloat16)


def weight_terms(turned, cots):
    return pl.pallas_call(
        grad_kernel,
        out_shape=[shape_of((SLAB, 2 * KVW))] * NZ,
        in_specs=whole(2 * NX),
        out_specs=whole(NZ),
        compiler_params=VMEM,
        cost_estimate=cost(2 * 512 * 1280 * 1024, 6 * 2**20),
        name="weight_terms",
    )(*turned, *cots)


def back_kernel(slabs, *refs):
    weights, cots, outs = refs[: len(slabs)], refs[len(slabs) : len(slabs) + NX], refs[len(slabs) + NX :]
    right = jnp.concatenate([ref[...] for ref in cots], axis=0)
    for place_k, weight in enumerate(weights):
        full = lax.dot_general(weight[...], right, NT, preferred_element_type=jnp.float32)
        for d in range(NX):
            outs[d][place_k] = full[:, d * ROWS : (d + 1) * ROWS].astype(jnp.bfloat16)


def back(weights, cots):
    count = len(weights)
    return pl.pallas_call(
        functools.partial(back_kernel, tuple(range(count))),
        out_shape=[shape_of((count, SLAB, ROWS))] * NX,
        in_specs=whole(count + NX),
        out_specs=whole(NX),
        compiler_params=VMEM,
        cost_estimate=cost(2 * 512 * 160 * count * 1024, 2**20 * 3),
        name="back",
    )(*weights, *cots)


def local_kernel(*refs):
    firsts, lasts, turned = refs[:NX], refs[NX : 2 * NX], refs[2 * NX : 3 * NX]
    mine, other = refs[3 * NX : 3 * NX + 2], refs[3 * NX + 2 : 3 * NX + 4]
    held = refs[3 * NX + 4]
    _, _, _, core = place()
    squares = jnp.zeros((SLAB, ROWS), jnp.float32)
    along = jnp.zeros((SLAB, ROWS), jnp.float32)
    order = [(firsts, place_k, k) for place_k, k in enumerate(Z_FIRST)]
    order += [(lasts, place_k, k) for place_k, k in enumerate(Z_LAST)]
    for d in range(NX):
        for source, place_k, k in order:
            stream = turned[d][k].astype(jnp.float32)
            squares = squares + stream * stream
            along = along + stream * source[d][place_k].astype(jnp.float32)
    inv_rms = lax.rsqrt(jnp.sum(squares, axis=0, keepdims=True) * (1.0 / D) + EPSILON)
    pull = inv_rms * inv_rms * (jnp.sum(along, axis=0, keepdims=True) * (1.0 / D))
    for d in range(NX):
        for source, place_k, k in order:
            stream = turned[d][k].astype(jnp.float32)
            term = source[d][place_k].astype(jnp.float32) - stream * pull
            held[k // 4, k % 4, d] = term.astype(jnp.bfloat16)
    for chunk in range(2):
        mine[chunk][...] = held[core, 2 * chunk : 2 * chunk + 2]
        other[chunk][...] = held[1 - core, 2 * chunk : 2 * chunk + 2]


def local_terms(firsts, lasts, turned):
    return pl.pallas_call(
        local_kernel,
        out_shape=[shape_of((2, NX, SLAB, ROWS))] * 4,
        in_specs=whole(3 * NX),
        out_specs=whole(4),
        scratch_shapes=[pltpu.VMEM((2, 4, NX, SLAB, ROWS), jnp.bfloat16)],
        compiler_params=VMEM,
        cost_estimate=cost(0, 4 * 2**20),
        name="local_terms",
    )(*firsts, *lasts, *turned)


FINISH_STEPS = 5
FINISH_WIDE = D // FINISH_STEPS


def finish_kernel(*refs):
    pieces, (top_ref, new_ref, old_ref, adv_ref, row_ref) = refs[:14], refs[14:19]
    out_ref, total, coef = refs[19:]
    z, x, _, core = place()
    below = (1 - core).astype(jnp.float32)
    step = pl.program_id(0)

    @pl.when(step == 0)
    def _():
        for chunk in range(2):
            mine, met, down, wrap, swap, other, back_in = pieces[chunk * 7 : chunk * 7 + 7]
            for a in range(2):
                for d in range(NX):
                    own = mine[a, d].astype(jnp.float32) + below * met[a, d].astype(jnp.float32)
                    upper = down[a, d].astype(jnp.float32) + wrap[a, d].astype(jnp.float32)
                    own = own + (upper + swap[a, d].astype(jnp.float32))
                    rest = other[a, d].astype(jnp.float32) + back_in[a, d].astype(jnp.float32)
                    column = lax.rem(x + d, NX)
                    for value, half in ((own, core), (rest, 1 - core)):
                        k = half * 4 + (2 * chunk + a)
                        slab = lax.rem(z + k, NZ) * NX + column
                        total[pl.ds(pl.multiple_of(slab * SLAB, 32), SLAB), :] = value
        rollout = row_ref[...]
        advantage = jnp.zeros((1, ROWS), jnp.float32)
        for index in range(4):
            advantage = advantage + jnp.where(rollout == index, adv_ref[0, index], 0.0)
        ratio = jnp.exp(new_ref[...] - old_ref[...])
        across = -jnp.clip(ratio, 0.8, 1.28) * advantage
        coef[...] = jnp.broadcast_to(across, (ROWS, ROWS)).T

    coefficient = coef[...]
    for tile in range(FINISH_WIDE // 128):
        span = slice(tile * 128, (tile + 1) * 128)
        first = pl.multiple_of(step * FINISH_WIDE + tile * 128, 128)
        turned = total[pl.ds(first, 128), :].T
        top = coefficient * top_ref[:, span].astype(jnp.float32)
        out_ref[:, span] = (top + turned).astype(jnp.bfloat16)


def finish(pieces, top, new_logprob, old_logprob, advantages, segments):
    return pl.pallas_call(
        finish_kernel,
        grid=(FINISH_STEPS,),
        out_shape=shape_of((ROWS, D)),
        in_specs=whole(14)
        + [pl.BlockSpec((ROWS, FINISH_WIDE), lambda step: (0, step))]
        + fetched((1, ROWS), (1, ROWS))
        + [pl.BlockSpec(memory_space=pltpu.SMEM)]
        + fetched((1, ROWS)),
        out_specs=pl.BlockSpec((ROWS, FINISH_WIDE), lambda step: (0, step)),
        scratch_shapes=[pltpu.VMEM((D, ROWS), jnp.float32), pltpu.VMEM((ROWS, ROWS), jnp.float32)],
        compiler_params=VMEM,
        cost_estimate=cost(0, 8 * 2**20),
        name="finish",
    )(*pieces, top, new_logprob, old_logprob, advantages, segments)


def scatter_z(terms):
    half = SLAB // 2
    wide = jnp.float32

    def add(first, second):
        return (first.astype(wide) + second.astype(wide)).astype(jnp.bfloat16)

    far_up, far_down = shift_z(terms[4][:half], 1), shift_z(terms[4][half:], -1)
    up = jnp.concatenate([add(terms[3][:half], far_up), terms[3][half:]], axis=0)
    down = jnp.concatenate([terms[5][:half], add(terms[5][half:], far_down)], axis=0)
    up, down = shift_z(up, 1), shift_z(down, -1)
    up, down = add(terms[2], up), add(terms[6], down)
    up, down = shift_z(up, 1), shift_z(down, -1)
    up, down = add(terms[1], up), add(terms[7], down)
    up, down = shift_z(up, 1), shift_z(down, -1)
    return terms[0].astype(wide) + (up.astype(wide) + down.astype(wide))


def local(
    hidden_in,
    norm_gain,
    key_weight,
    value_weight,
    queries,
    stashed_keys,
    stashed_values,
    out_cotangent,
    logprob_grad,
    new_logprob,
    old_logprob,
    advantages,
    segment_ids,
):
    wide = jnp.float32
    _, _, y, core = place()
    hidden = hidden_in[0]
    gain = norm_gain[0].astype(wide)[:, None]
    weight_pair = jnp.concatenate([key_weight[0], value_weight[0]], axis=1).astype(wide)
    own = (weight_pair * gain).astype(jnp.bfloat16)
    half = SLAB // 2
    up_1, down_1 = shift_z(own, 1), shift_z(own, -1)

    turned = turn(hidden)
    met_turned = [turned[0]] + [shift_x(turned[d], d) for d in (1, 2, 3)]
    cots = attend(
        queries[0],
        stashed_keys[0],
        stashed_values[0],
        out_cotangent[0],
        after(segment_ids, *turned),
        hidden,
    )
    up_1, down_1 = after((up_1, down_1), cots)
    cots = after(cots, up_1, down_1, *met_turned)
    up_2, down_2 = shift_z(up_1, 1), shift_z(down_1, -1)
    met_cots = [cots] + [shift_x(cots, d) for d in (1, 2, 3)]
    up_3, down_3 = shift_z(up_2, 1), shift_z(down_2, -1)
    met_cots = after(met_cots, up_2, down_2)
    firsts = back([own, down_1, up_1, down_2, up_2], met_cots)
    firsts = [firsts[0]] + [shift_x(firsts[d], -d) for d in (1, 2, 3)]
    up_4, down_4 = shift_z(up_3[:half], 1), shift_z(down_3[half:], -1)
    met_turned = after(met_turned, up_3, down_3)
    terms = weight_terms(met_turned, met_cots)
    opposite = jnp.concatenate([up_4, down_4], axis=0)
    lasts = back([down_3, up_3, opposite], met_cots)
    lasts = [lasts[0]] + [shift_x(lasts[d], -d) for d in (1, 2, 3)]
    weight_grad = gain * scatter_z(after(terms, up_4, down_4))

    mine_a, mine_b, other_a, other_b = local_terms(firsts, lasts, turned)
    pieces, gate = [], ()
    for mine, other in ((mine_a, other_a), (mine_b, other_b)):
        met = swap_core(other)
        pair = (mine.astype(wide) + met.astype(wide)).astype(jnp.bfloat16)
        pair = after(pair, *gate)
        down = send_y(pair, [(3, 2), (2, 1)])
        wrap = send_y(pair, [(3, 0)])
        gate = (down, wrap)
        onward = jnp.where(y == 0, wrap.astype(wide), pair.astype(wide) + down.astype(wide))
        swap = send_y(onward.astype(jnp.bfloat16), [(0, 1), (1, 0)])
        upper = down.astype(wide) + wrap.astype(wide) + swap.astype(wide)
        upper = upper + jnp.where(core == 1, mine.astype(wide), 0.0)
        back_in = swap_core(upper.astype(jnp.bfloat16))
        pieces += [mine, met, down, wrap, swap, other, back_in]

    hidden_cotangent = finish(
        pieces, logprob_grad, new_logprob[None], old_logprob[None], advantages, segment_ids
    )
    return (
        hidden_cotangent[None],
        weight_grad[:, :KVW][None],
        weight_grad[:, KVW:][None],
    )


def solution(mesh):
    return jax.shard_map(
        local,
        mesh=mesh,
        in_specs=(
            P("section", "dp", None),
            P("section", "dp"),
            P("section", "dp", None),
            P("section", "dp", None),
            P("section", "dp", None),
            P("section", "dp", None),
            P("section", "dp", None),
            P("section", "dp", None),
            P("dp", None),
            P("dp"),
            P("dp"),
            P("dp", None),
            P("dp", None),
        ),
        out_specs=(P("section", "dp", None), P("section", "dp", None), P("section", "dp", None)),
        check_vma=False,
    )
```

time: 506 us -> 133 us (0.26)
  waiting for transfers between devices: 313 us -> 40.9 us
  blocking collectives: 119 us -> 0 us
  starting transfers between devices: 0.16 us -> 60.1 us
  matrix products: 21.3 us -> 0 us
  other arithmetic: 22.9 us -> 4.27 us
  Pallas kernels: 0 us -> 15.1 us
  between operations: 14.6 us -> 1.1 us
    reduce_scatter x1 -> x0, waiting for transfers between devices: 224 us -> none  [local(): lax.psum_scatter(lax.dot_general(scaled, kv_cot, (((0,), (0,)), ((), ()))...]
    unnamed x1 -> x0, blocking collectives: 119 us -> none
    all_gather x3 -> x0, waiting for transfers between devices: 87.8 us -> none  [the longest x1 64.5 us: carried_in(): gathered = lax.all_gather(shard.astype(jnp.bfloat16), axis)]
    ppermute x0 -> x38, starting transfers between devices: none -> 60.1 us  [the longest x16 22.5 us: shift_z(): return lax.ppermute(value, 'dp', pairs)]
    ppermute x0 -> x38, waiting for transfers between devices: none -> 40.9 us  [the longest x12 22.5 us: shift_x(): return lax.ppermute(value, 'dp', pairs)]
    dot_general x5 -> x0, matrix products: 19.3 us -> none  [the longest x1 6.51 us: local(): lax.dot_general(kv_cot, weight_pair, (((1,), (1,)), ((), ())), preferred_...]
    pallas_call x0 -> x7, Pallas kernels: none -> 15.1 us  [the longest x2 4.49 us: back(): pl.pallas_call(functools.partial(back_kernel, tuple(range(count))), out_s...]
    add x6 -> x0, other arithmetic: 11.4 us -> none  [add_terms(): return first_term + second_term]
  transfers between devices with their start and end apart: 4 -> 38, of which waited for: 3 -> 12; matrix products, arithmetic and copies ran while one was open for 8% -> 3% of each run, Pallas kernels for 0% -> 8%
where the time goes in v1:
time: 133 us
  starting transfers between devices  60.1 us (45%)
  waiting for transfers between devices  40.9 us (31%)
  Pallas kernels  15.1 us (11%)
  local copies, waits for them, and re-layouts  11.1 us (8%)
  other arithmetic  4.27 us (3%)
    ppermute x16, starting transfers between devices, shift_z(): return lax.ppermute(value, 'dp', pairs)  22.5 us
    ppermute x12, waiting for transfers between devices, shift_x(): return lax.ppermute(value, 'dp', pairs)  22.5 us
    ppermute x12, starting transfers between devices, shift_x(): return lax.ppermute(value, 'dp', pairs)  19.2 us
    ppermute x6, waiting for transfers between devices, send_y(): return lax.ppermute(value, 'section', pairs)  11.2 us
    ppermute x4, starting transfers between devices, swap_core(): return lax.ppermute(value, 'section', [(s, s ^ 1) for s in range(2 * NY)])  10.6 us
    unnamed x38, local copies, waits for them, and re-layouts  9.38 us
    ppermute x6, starting transfers between devices, send_y(): return lax.ppermute(value, 'section', pairs)  7.78 us
    ppermute x16, waiting for transfers between devices, shift_z(): return lax.ppermute(value, 'dp', pairs)  7 us
  transfers between devices with their start and end apart: 38, of which 12 were waited for; matrix products, arithmetic and copies ran while one was open for 3% of the time, Pallas kernels for 8%

profile of v1, /device:TPU:1, one launch (start us, length us, event | category | flops | bytes accessed | tf_op | source)
XLA Modules:
  0.0 132.6 jit_solution(14400787814507657869)
XLA Ops:
  0.7 0.7 convert_element_type.182
  1.4 1.1 multiply_convert_fusion.refs_0_
  2.5 2.5 %collective-permute-start = (bf16[160,1024]{1,0:T(8,128)(2,1)S(1)}, bf16[160,1024]{1,0:T(8,128)(2,1)S(1)}, u32[]{:S(2)}, u32[]{:S(2)}) collective-permute-start(bf16[160,1024]{1,0:T(8,128)(2,1)S(1)} %multiply_convert_fusion.refs_0_), channel_id=1, source_target_pairs={{0,4},{1,5},{2,6},{3,7},{4,8},{5,9},{6,10},{7,11},{8,12},{9,13},{1... | collective-permute-start | bytes 983048 | tf_op jit(solution)/shard_map/ppermute | solution.py:51
  5.0 4.0 %collective-permute-start.1 = (bf16[160,1024]{1,0:T(8,128)(2,1)S(1)}, bf16[160,1024]{1,0:T(8,128)(2,1)S(1)}, u32[]{:S(2)}, u32[]{:S(2)}) collective-permute-start(bf16[160,1024]{1,0:T(8,128)(2,1)S(1)} %multiply_convert_fusion.refs_0_), channel_id=1, source_target_pairs={{0,28},{1,29},{2,30},{3,31},{4,0},{5,1},{6,2},{7,3},{8,4},{9,5},{1... | collective-permute-start | bytes 983048 | tf_op jit(solution)/shard_map/ppermute | solution.py:51
  9.1 1.3 copy-done
  10.4 0.5 turn.1
  10.9 0.8 copy-done.1
  11.7 1.2 copy-done.3
  12.9 1.2 copy-done.4
  14.2 2.4 %attend.1.refs_5_.refs_3_.refs_4_ = bf16[128,1024]{1,0:T(8,128)(2,1)S(1)} custom-call(bf16[128,4096]{1,0:T(8,128)(2,1)S(1)} %bitcast.17, bf16[128,512]{1,0:T(8,128)(2,1)S(1)} %bitcast.19, bf16[128,512]{1,0:T(8,128)(2,1)S(1)} %bitcast.20, bf16[128,4096]{1,0:T(8,128)(2,1)S(1)} %bitcast.18, s32[1,128]{1,0:T(1,128)S(1)} %copy-done.15, bf16[128,5120]{1,0:T(8,128)(2,1)S(1)} %bitcast.16), custom_call_target="tpu_custom_call" | custom-call | flops 536870912 | bytes 4194304 | tf_op jit(solution)/shard_map/attend/pallas_call | solution.py:141
  16.7 2.7 %collective-permute-start.2 = (bf16[160,1024]{1,0:T(8,128)(2,1)S(1)}, bf16[160,1024]{1,0:T(8,128)(2,1)S(1)}, u32[]{:S(2)}, u32[]{:S(2)}) collective-permute-start(bf16[160,1024]{1,0:T(8,128)(2,1)S(1)} %collective-permute-done.1.refs_1_), channel_id=1, source_target_pairs={{0,28},{1,29},{2,30},{3,31},{4,0},{5,1},{6,2},{7,3},{8,4},{9,5},{1... | collective-permute-start | bytes 983048 | tf_op jit(solution)/shard_map/ppermute | solution.py:51
  19.3 1.2 collective-permute-start.4
  20.5 2.5 %collective-permute-start.5 = (bf16[8,160,128]{2,1,0:T(8,128)(2,1)S(1)}, bf16[8,160,128]{2,1,0:T(8,128)(2,1)S(1)}, u32[]{:S(2)}, u32[]{:S(2)}) collective-permute-start(bf16[8,160,128]{2,1,0:T(8,128)(2,1)S(1)} %get-tuple-element.50.refs_10_), channel_id=1, source_target_pairs={{0,2},{1,3},{2,0},{3,1},{4,6},{5,7},{6,4},{7,5},{8,10},{9,11},{10,... | collective-permute-start | bytes 983048 | tf_op jit(solution)/shard_map/ppermute | solution.py:56
  23.0 1.2 collective-permute-start.6
  24.2 1.9 %collective-permute-done.3.refs_4_ = bf16[160,1024]{1,0:T(8,128)(2,1)S(1)} collective-permute-done((bf16[160,1024]{1,0:T(8,128)(2,1)S(1)}, bf16[160,1024]{1,0:T(8,128)(2,1)S(1)}, u32[]{:S(2)}, u32[]{:S(2)}) %collective-permute-start.3) | collective-permute-done | bytes 327712 | tf_op jit(solution)/shard_map/ppermute | solution.py:51
  26.1 2.7 %collective-permute-start.13 = (bf16[160,1024]{1,0:T(8,128)(2,1)S(1)}, bf16[160,1024]{1,0:T(8,128)(2,1)S(1)}, u32[]{:S(2)}, u32[]{:S(2)}) collective-permute-start(bf16[160,1024]{1,0:T(8,128)(2,1)S(1)} %collective-permute-done.2.refs_3_), channel_id=1, source_target_pairs={{0,28},{1,29},{2,30},{3,31},{4,0},{5,1},{6,2},{7,3},{8,4},{9,5},{1... | collective-permute-start | bytes 983048 | tf_op jit(solution)/shard_map/ppermute | solution.py:51
  28.7 7.4 %collective-permute-done.5.refs_2_ = bf16[8,160,128]{2,1,0:T(8,128)(2,1)S(1)} collective-permute-done((bf16[8,160,128]{2,1,0:T(8,128)(2,1)S(1)}, bf16[8,160,128]{2,1,0:T(8,128)(2,1)S(1)}, u32[]{:S(2)}, u32[]{:S(2)}) %collective-permute-start.5) | collective-permute-done | bytes 327712 | tf_op jit(solution)/shard_map/ppermute | solution.py:56
  36.2 0.6 collective-permute-done.6.refs_3_
  36.8 1.7 %collective-permute-start.7 = (bf16[128,1024]{1,0:T(8,128)(2,1)S(1)}, bf16[128,1024]{1,0:T(8,128)(2,1)S(1)}, u32[]{:S(2)}, u32[]{:S(2)}) collective-permute-start(bf16[128,1024]{1,0:T(8,128)(2,1)S(1)} %attend.1.refs_5_.refs_3_.refs_4_), channel_id=1, source_target_pairs={{0,1},{1,2},{2,3},{3,0},{4,5},{5,6},{6,7},{7,4},{8,9},{9,10},{10,1... | collective-permute-start | bytes 786440 | tf_op jit(solution)/shard_map/ppermute | solution.py:56
  38.5 2.9 %collective-permute-start.8 = (bf16[128,1024]{1,0:T(8,128)(2,1)S(1)}, bf16[128,1024]{1,0:T(8,128)(2,1)S(1)}, u32[]{:S(2)}, u32[]{:S(2)}) collective-permute-start(bf16[128,1024]{1,0:T(8,128)(2,1)S(1)} %attend.1.refs_5_.refs_3_.refs_4_), channel_id=1, source_target_pairs={{0,2},{1,3},{2,0},{3,1},{4,6},{5,7},{6,4},{7,5},{8,10},{9,11},{10,... | collective-permute-start | bytes 786440 | tf_op jit(solution)/shard_map/ppermute | solution.py:56
  41.4 4.0 %collective-permute-done.7.refs_6_.refs_4_.refs_5_ = bf16[128,1024]{1,0:T(8,128)(2,1)S(1)} collective-permute-done((bf16[128,1024]{1,0:T(8,128)(2,1)S(1)}, bf16[128,1024]{1,0:T(8,128)(2,1)S(1)}, u32[]{:S(2)}, u32[]{:S(2)}) %collective-permute-start.7) | collective-permute-done | bytes 262176 | tf_op jit(solution)/shard_map/ppermute | solution.py:56
  45.3 7.6 %collective-permute-done.8.refs_7_.refs_5_.refs_6_ = bf16[128,1024]{1,0:T(8,128)(2,1)S(1)} collective-permute-done((bf16[128,1024]{1,0:T(8,128)(2,1)S(1)}, bf16[128,1024]{1,0:T(8,128)(2,1)S(1)}, u32[]{:S(2)}, u32[]{:S(2)}) %collective-permute-start.8) | collective-permute-done | bytes 262176 | tf_op jit(solution)/shard_map/ppermute | solution.py:56
  52.9 0.3 collective-permute-start.15
  53.2 2.7 %collective-permute-start.16 = (bf16[80,1024]{1,0:T(8,128)(2,1)S(1)}, bf16[80,1024]{1,0:T(8,128)(2,1)S(1)}, u32[]{:S(2)}, u32[]{:S(2)}) collective-permute-start(bf16[80,1024]{1,0:T(8,128)(2,1)S(1)} %slice.41), channel_id=1, source_target_pairs={{0,28},{1,29},{2,30},{3,31},{4,0},{5,1},{6,2},{7,3},{8,4},{9,5},{1... | collective-permute-start | bytes 491528 | tf_op jit(solution)/shard_map/ppermute | solution.py:51
  55.9 2.6 %back.2 = (bf16[5,160,128]{2,1,0:T(8,128)(2,1)S(1)}, bf16[5,160,128]{2,1,0:T(8,128)(2,1)S(1)}, bf16[5,160,128]{2,1,0:T(8,128)(2,1)S(1)}, bf16[5,160,128]{2,1,0:T(8,128)(2,1)}) custom-call(bf16[160,1024]{1,0:T(8,128)(2,1)S(1)} %multiply_convert_fusion.refs_0_, bf16[160,1024]{1,0:T(8,128)(2,1)S(1)} %collective-permute-done.1.refs_1_, ...), custom_call_target="tpu_custom_call" | custom-call | flops 838860800 | bytes 3145728 | tf_op jit(solution)/shard_map/back/pallas_call | solution.py:187
  58.5 2.6 %collective-permute-start.10 = (bf16[5,160,128]{2,1,0:T(8,128)(2,1)S(1)}, bf16[5,160,128]{2,1,0:T(8,128)(2,1)S(1)}, u32[]{:S(2)}, u32[]{:S(2)}) collective-permute-start(bf16[5,160,128]{2,1,0:T(8,128)(2,1)S(1)} %get-tuple-element.61), channel_id=1, source_target_pairs={{0,3},{1,0},{2,1},{3,2},{4,7},{5,4},{6,5},{7,6},{8,11},{9,8},{10,9... | collective-permute-start | bytes 614408 | tf_op jit(solution)/shard_map/ppermute | solution.py:56
  61.2 0.5 collective-permute-start.12
  61.7 1.5 %weight_terms.1 = (bf16[160,1024]{1,0:T(8,128)(2,1)S(1)}, bf16[160,1024]{1,0:T(8,128)(2,1)S(1)}, bf16[160,1024]{1,0:T(8,128)(2,1)S(1)}, bf16[160,1024]{1,0:T(8,1...) custom-call(bf16[8,160,128]{2,1,0:T(8,128)(2,1)S(1)} %get-tuple-elem, ...), custom_call_target="tpu_custom_call" | custom-call | flops 1342177280 | bytes 6291456 | tf_op jit(solution)/shard_map/weight_terms/pallas_call | solution.py:165
  63.3 0.8 fusion.10
  64.1 1.9 %back.3 = (bf16[3,160,128]{2,1,0:T(8,128)(2,1)S(1)}, bf16[3,160,128]{2,1,0:T(8,128)(2,1)}, bf16[3,160,128]{2,1,0:T(8,128)(2,1)}, bf16[3,160,128]{2,1,0:T(8,128)(2,1)}) custom-call(bf16[160,1024]{1,0:T(8,128)(2,1)S(1)} %collective-permute-done.13.refs_0_, bf16[160,1024]{1,0:T(8,128)(2,1)S(1)} %collective-permute-done.14.refs_1_, ...), custom_call_target="tpu_custom_call" | custom-call | flops 503316480 | bytes 3145728 | tf_op jit(solution)/shard_map/back/pallas_call | solution.py:187
  66.1 0.6 copy-done.13
  66.7 2.1 %collective-permute-start.17 = (bf16[3,160,128]{2,1,0:T(8,128)(2,1)}, bf16[3,160,128]{2,1,0:T(8,128)(2,1)}, u32[]{:S(2)}, u32[]{:S(2)}) collective-permute-start(bf16[3,160,128]{2,1,0:T(8,128)(2,1)} %get-tuple-element.65), channel_id=1, source_target_pairs={{0,3},{1,0},{2,1},{3,2},{4,7},{5,4},{6,5},{7,6},{8,11},{9,8},{10,9... | collective-permute-start | bytes 368648 | tf_op jit(solution)/shard_map/ppermute | solution.py:56
  68.8 0.7 copy-done.7
  69.5 1.7 %collective-permute-start.18 = (bf16[3,160,128]{2,1,0:T(8,128)(2,1)}, bf16[3,160,128]{2,1,0:T(8,128)(2,1)}, u32[]{:S(2)}, u32[]{:S(2)}) collective-permute-start(bf16[3,160,128]{2,1,0:T(8,128)(2,1)} %get-tuple-element.66), channel_id=1, source_target_pairs={{0,2},{1,3},{2,0},{3,1},{4,6},{5,7},{6,4},{7,5},{8,10},{9,11},{10,... | collective-permute-start | bytes 368648 | tf_op jit(solution)/shard_map/ppermute | solution.py:56
  71.2 0.7 copy-done.9
  71.9 2.8 %collective-permute-start.19 = (bf16[3,160,128]{2,1,0:T(8,128)(2,1)}, bf16[3,160,128]{2,1,0:T(8,128)(2,1)}, u32[]{:S(2)}, u32[]{:S(2)}) collective-permute-start(bf16[3,160,128]{2,1,0:T(8,128)(2,1)} %get-tuple-element.67), channel_id=1, source_target_pairs={{0,1},{1,2},{2,3},{3,0},{4,5},{5,6},{6,7},{7,4},{8,9},{9,10},{10,1... | collective-permute-start | bytes 368648 | tf_op jit(solution)/shard_map/ppermute | solution.py:56
  74.9 0.4 collective-permute-done.18.refs_6_
  75.3 2.5 %collective-permute-done.19.refs_7_ = bf16[3,160,128]{2,1,0:T(8,128)(2,1)} collective-permute-done((bf16[3,160,128]{2,1,0:T(8,128)(2,1)}, bf16[3,160,128]{2,1,0:T(8,128)(2,1)}, u32[]{:S(2)}, u32[]{:S(2)}) %collective-permute-start.19) | collective-permute-done | bytes 122912 | tf_op jit(solution)/shard_map/ppermute | solution.py:56
  77.8 0.9 copy-done.8
  78.7 0.9 copy-done.10
  79.6 0.9 copy-done.14
  80.5 2.1 %local_terms.1 = (bf16[2,4,160,128]{3,2,1,0:T(8,128)(2,1)S(1)}, bf16[2,4,160,128]{3,2,1,0:T(8,128)(2,1)S(1)}, bf16[2,4,160,128]{3,2,1,0:T(8,128)(2,1)S(1)}, bf16[2,4,160,128]{3,2,1,0:T(8,128)(2,1)S(1)}) custom-call(bf16[5,160,128]{2,1,0:T(8,128)(2,1)S(1)} %get-tuple-element.60.refs_0_, bf16[5,160,128]{2,1,0:T(8,128)(2,1)S(1)} %copy-done.8, ...), custom_call_target="tpu_custom_call" | custom-call | bytes 4194304 | tf_op jit(solution)/shard_map/local_terms/pallas_call | solution.py:225
  82.6 3.5 %collective-permute-start.25 = (bf16[2,4,160,128]{3,2,1,0:T(8,128)(2,1)S(1)}, bf16[2,4,160,128]{3,2,1,0:T(8,128)(2,1)S(1)}, u32[]{:S(2)}, u32[]{:S(2)}) collective-permute-start(bf16[2,4,160,128]{3,2,1,0:T(8,128)(2,1)S(1)} %get-tuple-element.71.refs_12_), channel_id=1, source_target_pairs={{0,32},{32,0},{64,96},{96,64},{128,160},{160,128},{192,224},{224,1... | collective-permute-start | bytes 983048 | tf_op jit(solution)/shard_map/ppermute | solution.py:60
  86.2 1.0 add_convert_fusion.5
  87.2 0.3 collective-permute-start.31
  87.6 2.7 %collective-permute-start.35 = (bf16[160,1024]{1,0:T(8,128)(2,1)S(1)}, bf16[160,1024]{1,0:T(8,128)(2,1)S(1)}, u32[]{:S(2)}, u32[]{:S(2)}) collective-permute-start(bf16[160,1024]{1,0:T(8,128)(2,1)S(1)} %pad_maximum_fusion.2), channel_id=1, source_target_pairs={{0,28},{1,29},{2,30},{3,31},{4,0},{5,1},{6,2},{7,3},{8,4},{9,5},{1... | collective-permute-start | bytes 983048 | tf_op jit(solution)/shard_map/ppermute | solution.py:51
  90.4 0.7 collective-permute-start.21
  91.1 1.3 collective-permute-start.22
  92.5 5.1 %collective-permute-done.31 = bf16[160,1024]{1,0:T(8,128)(2,1)S(1)} collective-permute-done((bf16[160,1024]{1,0:T(8,128)(2,1)S(1)}, bf16[160,1024]{1,0:T(8,128)(2,1)S(1)}, u32[]{:S(2)}, u32[]{:S(2)}) %collective-permute-start.31) | collective-permute-done | bytes 327712 | tf_op jit(solution)/shard_map/ppermute | solution.py:51
  97.9 2.7 %collective-permute-start.36 = (bf16[160,1024]{1,0:T(8,128)(2,1)S(1)}, bf16[160,1024]{1,0:T(8,128)(2,1)S(1)}, u32[]{:S(2)}, u32[]{:S(2)}) collective-permute-start(bf16[160,1024]{1,0:T(8,128)(2,1)S(1)} %add_convert_fusion.1), channel_id=1, source_target_pairs={{0,28},{1,29},{2,30},{3,31},{4,0},{5,1},{6,2},{7,3},{8,4},{9,5},{1... | collective-permute-start | bytes 983048 | tf_op jit(solution)/shard_map/ppermute | solution.py:51
  100.6 3.0 %collective-permute-done.22.refs_3_ = bf16[2,4,160,128]{3,2,1,0:T(8,128)(2,1)S(1)} collective-permute-done((bf16[2,4,160,128]{3,2,1,0:T(8,128)(2,1)S(1)}, bf16[2,4,160,128]{3,2,1,0:T(8,128)(2,1)S(1)}, u32[]{:S(2)}, u32[]{:S(2)}) %collective-permute-start.22) | collective-permute-done | bytes 327712 | tf_op jit(solution)/shard_map/ppermute | solution.py:65
  103.6 0.7 collective-permute-start.26
  104.3 1.3 collective-permute-start.27
  105.7 1.9 %collective-permute-start.23 = (bf16[2,4,160,128]{3,2,1,0:T(8,128)(2,1)S(1)}, bf16[2,4,160,128]{3,2,1,0:T(8,128)(2,1)S(1)}, u32[]{:S(2)}, u32[]{:S(2)}) collective-permute-start(bf16[2,4,160,128]{3,2,1,0:T(8,128)(2,1)S(1)} %fusion.3), channel_id=1, source_target_pairs={{0,64},{32,96},{64,0},{96,32},{1,65},{33,97},{65,1},{97,33},{2,66}... | collective-permute-start | bytes 983048 | tf_op jit(solution)/shard_map/ppermute | solution.py:65
  107.9 6.8 %collective-permute-done.27.refs_10_ = bf16[2,4,160,128]{3,2,1,0:T(8,128)(2,1)S(1)} collective-permute-done((bf16[2,4,160,128]{3,2,1,0:T(8,128)(2,1)S(1)}, bf16[2,4,160,128]{3,2,1,0:T(8,128)(2,1)S(1)}, u32[]{:S(2)}, u32[]{:S(2)}) %collective-permute-start.27) | collective-permute-done | bytes 327712 | tf_op jit(solution)/shard_map/ppermute | solution.py:65
  114.8 1.9 %collective-permute-start.28 = (bf16[2,4,160,128]{3,2,1,0:T(8,128)(2,1)S(1)}, bf16[2,4,160,128]{3,2,1,0:T(8,128)(2,1)S(1)}, u32[]{:S(2)}, u32[]{:S(2)}) collective-permute-start(bf16[2,4,160,128]{3,2,1,0:T(8,128)(2,1)S(1)} %fusion.8), channel_id=1, source_target_pairs={{0,64},{32,96},{64,0},{96,32},{1,65},{33,97},{65,1},{97,33},{2,66}... | collective-permute-start | bytes 983048 | tf_op jit(solution)/shard_map/ppermute | solution.py:65
  116.9 1.5 %collective-permute-start.37 = (bf16[160,1024]{1,0:T(8,128)(2,1)S(1)}, bf16[160,1024]{1,0:T(8,128)(2,1)S(1)}, u32[]{:S(2)}, u32[]{:S(2)}) collective-permute-start(bf16[160,1024]{1,0:T(8,128)(2,1)S(1)} %add_convert_fusion), channel_id=1, source_target_pairs={{0,28},{1,29},{2,30},{3,31},{4,0},{5,1},{6,2},{7,3},{8,4},{9,5},{1... | collective-permute-start | bytes 983048 | tf_op jit(solution)/shard_map/ppermute | solution.py:51
  118.3 0.2 fusion.2
  118.5 3.2 %collective-permute-start.24 = (bf16[2,4,160,128]{3,2,1,0:T(8,128)(2,1)S(1)}, bf16[2,4,160,128]{3,2,1,0:T(8,128)(2,1)S(1)}, u32[]{:S(2)}, u32[]{:S(2)}) collective-permute-start(bf16[2,4,160,128]{3,2,1,0:T(8,128)(2,1)S(1)} %fusion.2), channel_id=1, source_target_pairs={{0,32},{32,0},{64,96},{96,64},{128,160},{160,128},{192,224},{224,1... | collective-permute-start | bytes 983048 | tf_op jit(solution)/shard_map/ppermute | solution.py:60
  121.7 1.4 %collective-permute-done.28.refs_11_ = bf16[2,4,160,128]{3,2,1,0:T(8,128)(2,1)S(1)} collective-permute-done((bf16[2,4,160,128]{3,2,1,0:T(8,128)(2,1)S(1)}, bf16[2,4,160,128]{3,2,1,0:T(8,128)(2,1)S(1)}, u32[]{:S(2)}, u32[]{:S(2)}) %collective-permute-start.28) | collective-permute-done | bytes 327712 | tf_op jit(solution)/shard_map/ppermute | solution.py:65
  123.4 3.8 %collective-permute-start.29 = (bf16[2,4,160,128]{3,2,1,0:T(8,128)(2,1)S(1)}, bf16[2,4,160,128]{3,2,1,0:T(8,128)(2,1)S(1)}, u32[]{:S(2)}, u32[]{:S(2)}) collective-permute-start(bf16[2,4,160,128]{3,2,1,0:T(8,128)(2,1)S(1)} %fusion.7), channel_id=1, source_target_pairs={{0,32},{32,0},{64,96},{96,64},{128,160},{160,128},{192,224},{224,1... | collective-permute-start | bytes 983048 | tf_op jit(solution)/shard_map/ppermute | solution.py:60
  127.3 0.9 slice_bitcast_fusion
  128.2 0.2 collective-permute-done.29.refs_13_
  128.5 4.1 %finish.1 = bf16[128,5120]{1,0:T(8,128)(2,1)} custom-call(bf16[2,4,160,128]{3,2,1,0:T(8,128)(2,1)S(1)} %get-tuple-element.68.refs_0_, bf16[2,4,160,128]{3,2,1,0:T(8,128)(2,1)S(1)} %collective-permute-done.20.refs_1_, bf16[2,4,160,128]{3,2,1,0:T(8,128)(2,1)S(1)} %collective-permute-done.21.refs_2_, ...), custom_call_target="tpu_custom_call" | custom-call | bytes 8388608 | tf_op jit(solution)/shard_map/finish/pallas_call | solution.py:281
  (81 shorter events, 2.0 us)
Async XLA Ops:
  0.6 10.3 %copy-start.15 = (s32[1,128]{1,0:T(1,128)S(1)}, s32[1,128]{1,0:T(1,128)}, u32[]{:S(2)}) copy-start(s32[1,128]{1,0:T(1,128)} %refs_18_.1) | copy-start | bytes 1540
  0.6 10.3 %copy-start.11 = (bf16[1,128,512]{2,1,0:T(8,128)(2,1)S(1)}, bf16[1,128,512]{2,1,0:T(8,128)(2,1)}, u32[]{:S(2)}) copy-start(bf16[1,128,512]{2,1,0:T(8,128)(2,1)} %param.18) | copy-start | bytes 393220
  0.7 10.3 %copy-start.12 = (bf16[1,128,512]{2,1,0:T(8,128)(2,1)S(1)}, bf16[1,128,512]{2,1,0:T(8,128)(2,1)}, u32[]{:S(2)}) copy-start(bf16[1,128,512]{2,1,0:T(8,128)(2,1)} %param.19) | copy-start | bytes 393220
  2.5 14.1 %collective-permute-start = (bf16[160,1024]{1,0:T(8,128)(2,1)S(1)}, bf16[160,1024]{1,0:T(8,128)(2,1)S(1)}, u32[]{:S(2)}, u32[]{:S(2)}) collective-permute-start(bf16[160,1024]{1,0:T(8,128)(2,1)S(1)} %multiply_convert_fusion.refs_0_), channel_id=1, source_target_pairs={{0,4},{1,5},{2,6},{3,7},{4,8},{5,9},{6,10},{7,11},{8,12},{9,13},{1... | collective-permute-start | bytes 983048 | tf_op jit(solution)/shard_map/ppermute | solution.py:51
  5.0 11.5 %collective-permute-start.1 = (bf16[160,1024]{1,0:T(8,128)(2,1)S(1)}, bf16[160,1024]{1,0:T(8,128)(2,1)S(1)}, u32[]{:S(2)}, u32[]{:S(2)}) collective-permute-start(bf16[160,1024]{1,0:T(8,128)(2,1)S(1)} %multiply_convert_fusion.refs_0_), channel_id=1, source_target_pairs={{0,28},{1,29},{2,30},{3,31},{4,0},{5,1},{6,2},{7,3},{8,4},{9,5},{1... | collective-permute-start | bytes 983048 | tf_op jit(solution)/shard_map/ppermute | solution.py:51
  9.1 1.3 copy-start
  10.4 1.3 copy-start.1
  11.7 1.2 copy-start.3
  12.9 1.2 copy-start.4
  16.6 9.5 %collective-permute-start.3 = (bf16[160,1024]{1,0:T(8,128)(2,1)S(1)}, bf16[160,1024]{1,0:T(8,128)(2,1)S(1)}, u32[]{:S(2)}, u32[]{:S(2)}) collective-permute-start(bf16[160,1024]{1,0:T(8,128)(2,1)S(1)} %collective-permute-done.refs_2_), channel_id=1, source_target_pairs={{0,4},{1,5},{2,6},{3,7},{4,8},{5,9},{6,10},{7,11},{8,12},{9,13},{1... | collective-permute-start | bytes 983048 | tf_op jit(solution)/shard_map/ppermute | solution.py:51
  16.7 9.4 %collective-permute-start.2 = (bf16[160,1024]{1,0:T(8,128)(2,1)S(1)}, bf16[160,1024]{1,0:T(8,128)(2,1)S(1)}, u32[]{:S(2)}, u32[]{:S(2)}) collective-permute-start(bf16[160,1024]{1,0:T(8,128)(2,1)S(1)} %collective-permute-done.1.refs_1_), channel_id=1, source_target_pairs={{0,28},{1,29},{2,30},{3,31},{4,0},{5,1},{6,2},{7,3},{8,4},{9,5},{1... | collective-permute-start | bytes 983048 | tf_op jit(solution)/shard_map/ppermute | solution.py:51
  19.3 9.4 %collective-permute-start.4 = (bf16[8,160,128]{2,1,0:T(8,128)(2,1)S(1)}, bf16[8,160,128]{2,1,0:T(8,128)(2,1)S(1)}, u32[]{:S(2)}, u32[]{:S(2)}) collective-permute-start(bf16[8,160,128]{2,1,0:T(8,128)(2,1)S(1)} %get-tuple-element.49.refs_9_), channel_id=1, source_target_pairs={{0,1},{1,2},{2,3},{3,0},{4,5},{5,6},{6,7},{7,4},{8,9},{9,10},{10,1... | collective-permute-start | bytes 983048 | tf_op jit(solution)/shard_map/ppermute | solution.py:56
  20.5 15.6 %collective-permute-start.5 = (bf16[8,160,128]{2,1,0:T(8,128)(2,1)S(1)}, bf16[8,160,128]{2,1,0:T(8,128)(2,1)S(1)}, u32[]{:S(2)}, u32[]{:S(2)}) collective-permute-start(bf16[8,160,128]{2,1,0:T(8,128)(2,1)S(1)} %get-tuple-element.50.refs_10_), channel_id=1, source_target_pairs={{0,2},{1,3},{2,0},{3,1},{4,6},{5,7},{6,4},{7,5},{8,10},{9,11},{10,... | collective-permute-start | bytes 983048 | tf_op jit(solution)/shard_map/ppermute | solution.py:56
  23.0 13.8 %collective-permute-start.6 = (bf16[8,160,128]{2,1,0:T(8,128)(2,1)S(1)}, bf16[8,160,128]{2,1,0:T(8,128)(2,1)S(1)}, u32[]{:S(2)}, u32[]{:S(2)}) collective-permute-start(bf16[8,160,128]{2,1,0:T(8,128)(2,1)S(1)} %get-tuple-element.51.refs_11_), channel_id=1, source_target_pairs={{0,3},{1,0},{2,1},{3,2},{4,7},{5,4},{6,5},{7,6},{8,11},{9,8},{10,9... | collective-permute-start | bytes 983048 | tf_op jit(solution)/shard_map/ppermute | solution.py:56
  26.1 26.8 %collective-permute-start.14 = (bf16[160,1024]{1,0:T(8,128)(2,1)S(1)}, bf16[160,1024]{1,0:T(8,128)(2,1)S(1)}, u32[]{:S(2)}, u32[]{:S(2)}) collective-permute-start(bf16[160,1024]{1,0:T(8,128)(2,1)S(1)} %collective-permute-done.3.refs_4_), channel_id=1, source_target_pairs={{0,4},{1,5},{2,6},{3,7},{4,8},{5,9},{6,10},{7,11},{8,12},{9,13},{1... | collective-permute-start | bytes 983048 | tf_op jit(solution)/shard_map/ppermute | solution.py:51
  26.1 27.1 %collective-permute-start.13 = (bf16[160,1024]{1,0:T(8,128)(2,1)S(1)}, bf16[160,1024]{1,0:T(8,128)(2,1)S(1)}, u32[]{:S(2)}, u32[]{:S(2)}) collective-permute-start(bf16[160,1024]{1,0:T(8,128)(2,1)S(1)} %collective-permute-done.2.refs_3_), channel_id=1, source_target_pairs={{0,28},{1,29},{2,30},{3,31},{4,0},{5,1},{6,2},{7,3},{8,4},{9,5},{1... | collective-permute-start | bytes 983048 | tf_op jit(solution)/shard_map/ppermute | solution.py:51
  36.8 8.6 %collective-permute-start.7 = (bf16[128,1024]{1,0:T(8,128)(2,1)S(1)}, bf16[128,1024]{1,0:T(8,128)(2,1)S(1)}, u32[]{:S(2)}, u32[]{:S(2)}) collective-permute-start(bf16[128,1024]{1,0:T(8,128)(2,1)S(1)} %attend.1.refs_5_.refs_3_.refs_4_), channel_id=1, source_target_pairs={{0,1},{1,2},{2,3},{3,0},{4,5},{5,6},{6,7},{7,4},{8,9},{9,10},{10,1... | collective-permute-start | bytes 786440 | tf_op jit(solution)/shard_map/ppermute | solution.py:56
  38.5 14.4 %collective-permute-start.8 = (bf16[128,1024]{1,0:T(8,128)(2,1)S(1)}, bf16[128,1024]{1,0:T(8,128)(2,1)S(1)}, u32[]{:S(2)}, u32[]{:S(2)}) collective-permute-start(bf16[128,1024]{1,0:T(8,128)(2,1)S(1)} %attend.1.refs_5_.refs_3_.refs_4_), channel_id=1, source_target_pairs={{0,2},{1,3},{2,0},{3,1},{4,6},{5,7},{6,4},{7,5},{8,10},{9,11},{10,... | collective-permute-start | bytes 786440 | tf_op jit(solution)/shard_map/ppermute | solution.py:56
  41.3 11.5 %collective-permute-start.9 = (bf16[128,1024]{1,0:T(8,128)(2,1)S(1)}, bf16[128,1024]{1,0:T(8,128)(2,1)S(1)}, u32[]{:S(2)}, u32[]{:S(2)}) collective-permute-start(bf16[128,1024]{1,0:T(8,128)(2,1)S(1)} %attend.1.refs_5_.refs_3_.refs_4_), channel_id=1, source_target_pairs={{0,3},{1,0},{2,1},{3,2},{4,7},{5,4},{6,5},{7,6},{8,11},{9,8},{10,9... | collective-permute-start | bytes 786440 | tf_op jit(solution)/shard_map/ppermute | solution.py:56
  52.9 10.4 %collective-permute-start.15 = (bf16[80,1024]{1,0:T(8,128)(2,1)S(1)}, bf16[80,1024]{1,0:T(8,128)(2,1)S(1)}, u32[]{:S(2)}, u32[]{:S(2)}) collective-permute-start(bf16[80,1024]{1,0:T(8,128)(2,1)S(1)} %slice.40), channel_id=1, source_target_pairs={{0,4},{1,5},{2,6},{3,7},{4,8},{5,9},{6,10},{7,11},{8,12},{9,13},{1... | collective-permute-start | bytes 491528 | tf_op jit(solution)/shard_map/ppermute | solution.py:51
  53.2 10.1 %collective-permute-start.16 = (bf16[80,1024]{1,0:T(8,128)(2,1)S(1)}, bf16[80,1024]{1,0:T(8,128)(2,1)S(1)}, u32[]{:S(2)}, u32[]{:S(2)}) collective-permute-start(bf16[80,1024]{1,0:T(8,128)(2,1)S(1)} %slice.41), channel_id=1, source_target_pairs={{0,28},{1,29},{2,30},{3,31},{4,0},{5,1},{6,2},{7,3},{8,4},{9,5},{1... | collective-permute-start | bytes 491528 | tf_op jit(solution)/shard_map/ppermute | solution.py:51
  58.5 10.3 %collective-permute-start.10 = (bf16[5,160,128]{2,1,0:T(8,128)(2,1)S(1)}, bf16[5,160,128]{2,1,0:T(8,128)(2,1)S(1)}, u32[]{:S(2)}, u32[]{:S(2)}) collective-permute-start(bf16[5,160,128]{2,1,0:T(8,128)(2,1)S(1)} %get-tuple-element.61), channel_id=1, source_target_pairs={{0,3},{1,0},{2,1},{3,2},{4,7},{5,4},{6,5},{7,6},{8,11},{9,8},{10,9... | collective-permute-start | bytes 614408 | tf_op jit(solution)/shard_map/ppermute | solution.py:56
  61.1 10.1 %collective-permute-start.11 = (bf16[5,160,128]{2,1,0:T(8,128)(2,1)S(1)}, bf16[5,160,128]{2,1,0:T(8,128)(2,1)S(1)}, u32[]{:S(2)}, u32[]{:S(2)}) collective-permute-start(bf16[5,160,128]{2,1,0:T(8,128)(2,1)S(1)} %get-tuple-element.62), channel_id=1, source_target_pairs={{0,2},{1,3},{2,0},{3,1},{4,6},{5,7},{6,4},{7,5},{8,10},{9,11},{10,... | collective-permute-start | bytes 614408 | tf_op jit(solution)/shard_map/ppermute | solution.py:56
  61.2 13.5 %collective-permute-start.12 = (bf16[5,160,128]{2,1,0:T(8,128)(2,1)}, bf16[5,160,128]{2,1,0:T(8,128)(2,1)}, u32[]{:S(2)}, u32[]{:S(2)}) collective-permute-start(bf16[5,160,128]{2,1,0:T(8,128)(2,1)} %get-tuple-element.63), channel_id=1, source_target_pairs={{0,1},{1,2},{2,3},{3,0},{4,5},{5,6},{6,7},{7,4},{8,9},{9,10},{10,1... | collective-permute-start | bytes 614408 | tf_op jit(solution)/shard_map/ppermute | solution.py:56
  63.3 0.8 copy-start.5
  64.1 22.1 %collective-permute-start.30 = (bf16[80,1024]{1,0:T(8,128)(2,1)}, bf16[80,1024]{1,0:T(8,128)(2,1)}, u32[]{:S(2)}, u32[]{:S(2)}) collective-permute-start(bf16[80,1024]{1,0:T(8,128)(2,1)} %get-tuple-element.95), channel_id=1, source_target_pairs={{0,4},{1,5},{2,6},{3,7},{4,8},{5,9},{6,10},{7,11},{8,12},{9,13},{1... | collective-permute-start | bytes 491528 | tf_op jit(solution)/shard_map/ppermute | solution.py:51
  66.1 0.6 copy-start.13
  66.7 8.2 %collective-permute-start.17 = (bf16[3,160,128]{2,1,0:T(8,128)(2,1)}, bf16[3,160,128]{2,1,0:T(8,128)(2,1)}, u32[]{:S(2)}, u32[]{:S(2)}) collective-permute-start(bf16[3,160,128]{2,1,0:T(8,128)(2,1)} %get-tuple-element.65), channel_id=1, source_target_pairs={{0,3},{1,0},{2,1},{3,2},{4,7},{5,4},{6,5},{7,6},{8,11},{9,8},{10,9... | collective-permute-start | bytes 368648 | tf_op jit(solution)/shard_map/ppermute | solution.py:56
  68.8 0.7 copy-start.7
  69.5 5.8 %collective-permute-start.18 = (bf16[3,160,128]{2,1,0:T(8,128)(2,1)}, bf16[3,160,128]{2,1,0:T(8,128)(2,1)}, u32[]{:S(2)}, u32[]{:S(2)}) collective-permute-start(bf16[3,160,128]{2,1,0:T(8,128)(2,1)} %get-tuple-element.66), channel_id=1, source_target_pairs={{0,2},{1,3},{2,0},{3,1},{4,6},{5,7},{6,4},{7,5},{8,10},{9,11},{10,... | collective-permute-start | bytes 368648 | tf_op jit(solution)/shard_map/ppermute | solution.py:56
  71.2 0.7 copy-start.9
  71.9 5.8 %collective-permute-start.19 = (bf16[3,160,128]{2,1,0:T(8,128)(2,1)}, bf16[3,160,128]{2,1,0:T(8,128)(2,1)}, u32[]{:S(2)}, u32[]{:S(2)}) collective-permute-start(bf16[3,160,128]{2,1,0:T(8,128)(2,1)} %get-tuple-element.67), channel_id=1, source_target_pairs={{0,1},{1,2},{2,3},{3,0},{4,5},{5,6},{6,7},{7,4},{8,9},{9,10},{10,1... | collective-permute-start | bytes 368648 | tf_op jit(solution)/shard_map/ppermute | solution.py:56
  74.7 12.8 %collective-permute-start.34 = (bf16[80,1024]{1,0:T(8,128)(2,1)}, bf16[80,1024]{1,0:T(8,128)(2,1)S(1)}, u32[]{:S(2)}, u32[]{:S(2)}) collective-permute-start(bf16[80,1024]{1,0:T(8,128)(2,1)} %get-tuple-element.96), channel_id=1, source_target_pairs={{0,28},{1,29},{2,30},{3,31},{4,0},{5,1},{6,2},{7,3},{8,4},{9,5},{1... | collective-permute-start | bytes 491528 | tf_op jit(solution)/shard_map/ppermute | solution.py:51
  77.8 0.9 copy-start.8
  78.7 0.9 copy-start.10
  79.6 0.9 copy-start.14
  82.6 9.8 %collective-permute-start.25 = (bf16[2,4,160,128]{3,2,1,0:T(8,128)(2,1)S(1)}, bf16[2,4,160,128]{3,2,1,0:T(8,128)(2,1)S(1)}, u32[]{:S(2)}, u32[]{:S(2)}) collective-permute-start(bf16[2,4,160,128]{3,2,1,0:T(8,128)(2,1)S(1)} %get-tuple-element.71.refs_12_), channel_id=1, source_target_pairs={{0,32},{32,0},{64,96},{96,64},{128,160},{160,128},{192,224},{224,1... | collective-permute-start | bytes 983048 | tf_op jit(solution)/shard_map/ppermute | solution.py:60
  86.1 4.2 %collective-permute-start.20 = (bf16[2,4,160,128]{3,2,1,0:T(8,128)(2,1)S(1)}, bf16[2,4,160,128]{3,2,1,0:T(8,128)(2,1)S(1)}, u32[]{:S(2)}, u32[]{:S(2)}) collective-permute-start(bf16[2,4,160,128]{3,2,1,0:T(8,128)(2,1)S(1)} %get-tuple-element.69.refs_5_), channel_id=1, source_target_pairs={{0,32},{32,0},{64,96},{96,64},{128,160},{160,128},{192,224},{224,1... | collective-permute-start | bytes 983048 | tf_op jit(solution)/shard_map/ppermute | solution.py:60
  87.2 10.4 %collective-permute-start.31 = (bf16[160,1024]{1,0:T(8,128)(2,1)S(1)}, bf16[160,1024]{1,0:T(8,128)(2,1)S(1)}, u32[]{:S(2)}, u32[]{:S(2)}) collective-permute-start(bf16[160,1024]{1,0:T(8,128)(2,1)S(1)} %pad_maximum_fusion.1), channel_id=1, source_target_pairs={{0,4},{1,5},{2,6},{3,7},{4,8},{5,9},{6,10},{7,11},{8,12},{9,13},{1... | collective-permute-start | bytes 983048 | tf_op jit(solution)/shard_map/ppermute | solution.py:51
  87.6 10.0 %copy-start.6 = (bf16[160,1024]{1,0:T(8,128)(2,1)S(1)}, bf16[160,1024]{1,0:T(8,128)(2,1)}, u32[]{:S(2)}) copy-start(bf16[160,1024]{1,0:T(8,128)(2,1)} %copy-done.5) | copy-start | bytes 983044
  87.6 10.2 %collective-permute-start.35 = (bf16[160,1024]{1,0:T(8,128)(2,1)S(1)}, bf16[160,1024]{1,0:T(8,128)(2,1)S(1)}, u32[]{:S(2)}, u32[]{:S(2)}) collective-permute-start(bf16[160,1024]{1,0:T(8,128)(2,1)S(1)} %pad_maximum_fusion.2), channel_id=1, source_target_pairs={{0,28},{1,29},{2,30},{3,31},{4,0},{5,1},{6,2},{7,3},{8,4},{9,5},{1... | collective-permute-start | bytes 983048 | tf_op jit(solution)/shard_map/ppermute | solution.py:51
  90.4 10.2 %collective-permute-start.21 = (bf16[2,4,160,128]{3,2,1,0:T(8,128)(2,1)S(1)}, bf16[2,4,160,128]{3,2,1,0:T(8,128)(2,1)S(1)}, u32[]{:S(2)}, u32[]{:S(2)}) collective-permute-start(bf16[2,4,160,128]{3,2,1,0:T(8,128)(2,1)S(1)} %fusion), channel_id=1, source_target_pairs={{192,128},{224,160},{128,64},{160,96},{193,129},{225,161},{129,65}... | collective-permute-start | bytes 983048 | tf_op jit(solution)/shard_map/ppermute | solution.py:65
  91.1 12.5 %collective-permute-start.22 = (bf16[2,4,160,128]{3,2,1,0:T(8,128)(2,1)S(1)}, bf16[2,4,160,128]{3,2,1,0:T(8,128)(2,1)S(1)}, u32[]{:S(2)}, u32[]{:S(2)}) collective-permute-start(bf16[2,4,160,128]{3,2,1,0:T(8,128)(2,1)S(1)} %fusion), channel_id=1, source_target_pairs={{192,0},{224,32},{193,1},{225,33},{194,2},{226,34},{195,3},{227,35... | collective-permute-start | bytes 983048 | tf_op jit(solution)/shard_map/ppermute | solution.py:65
  97.7 10.0 %collective-permute-start.32 = (bf16[160,1024]{1,0:T(8,128)(2,1)S(1)}, bf16[160,1024]{1,0:T(8,128)(2,1)S(1)}, u32[]{:S(2)}, u32[]{:S(2)}) collective-permute-start(bf16[160,1024]{1,0:T(8,128)(2,1)S(1)} %add_convert_fusion.3), channel_id=1, source_target_pairs={{0,4},{1,5},{2,6},{3,7},{4,8},{5,9},{6,10},{7,11},{8,12},{9,13},{1... | collective-permute-start | bytes 983048 | tf_op jit(solution)/shard_map/ppermute | solution.py:51
  97.9 18.9 %collective-permute-start.36 = (bf16[160,1024]{1,0:T(8,128)(2,1)S(1)}, bf16[160,1024]{1,0:T(8,128)(2,1)S(1)}, u32[]{:S(2)}, u32[]{:S(2)}) collective-permute-start(bf16[160,1024]{1,0:T(8,128)(2,1)S(1)} %add_convert_fusion.1), channel_id=1, source_target_pairs={{0,28},{1,29},{2,30},{3,31},{4,0},{5,1},{6,2},{7,3},{8,4},{9,5},{1... | collective-permute-start | bytes 983048 | tf_op jit(solution)/shard_map/ppermute | solution.py:51
  103.6 4.3 %collective-permute-start.26 = (bf16[2,4,160,128]{3,2,1,0:T(8,128)(2,1)S(1)}, bf16[2,4,160,128]{3,2,1,0:T(8,128)(2,1)S(1)}, u32[]{:S(2)}, u32[]{:S(2)}) collective-permute-start(bf16[2,4,160,128]{3,2,1,0:T(8,128)(2,1)S(1)} %fusion.5), channel_id=1, source_target_pairs={{192,128},{224,160},{128,64},{160,96},{193,129},{225,161},{129,65}... | collective-permute-start | bytes 983048 | tf_op jit(solution)/shard_map/ppermute | solution.py:65
  104.3 10.4 %collective-permute-start.27 = (bf16[2,4,160,128]{3,2,1,0:T(8,128)(2,1)S(1)}, bf16[2,4,160,128]{3,2,1,0:T(8,128)(2,1)S(1)}, u32[]{:S(2)}, u32[]{:S(2)}) collective-permute-start(bf16[2,4,160,128]{3,2,1,0:T(8,128)(2,1)S(1)} %fusion.5), channel_id=1, source_target_pairs={{192,0},{224,32},{193,1},{225,33},{194,2},{226,34},{195,3},{227,35... | collective-permute-start | bytes 983048 | tf_op jit(solution)/shard_map/ppermute | solution.py:65
  105.7 12.6 %collective-permute-start.23 = (bf16[2,4,160,128]{3,2,1,0:T(8,128)(2,1)S(1)}, bf16[2,4,160,128]{3,2,1,0:T(8,128)(2,1)S(1)}, u32[]{:S(2)}, u32[]{:S(2)}) collective-permute-start(bf16[2,4,160,128]{3,2,1,0:T(8,128)(2,1)S(1)} %fusion.3), channel_id=1, source_target_pairs={{0,64},{32,96},{64,0},{96,32},{1,65},{33,97},{65,1},{97,33},{2,66}... | collective-permute-start | bytes 983048 | tf_op jit(solution)/shard_map/ppermute | solution.py:65
  107.8 19.4 %collective-permute-start.33 = (bf16[160,1024]{1,0:T(8,128)(2,1)S(1)}, bf16[160,1024]{1,0:T(8,128)(2,1)S(1)}, u32[]{:S(2)}, u32[]{:S(2)}) collective-permute-start(bf16[160,1024]{1,0:T(8,128)(2,1)S(1)} %add_convert_fusion.2), channel_id=1, source_target_pairs={{0,4},{1,5},{2,6},{3,7},{4,8},{5,9},{6,10},{7,11},{8,12},{9,13},{1... | collective-permute-start | bytes 983048 | tf_op jit(solution)/shard_map/ppermute | solution.py:51
  114.8 8.3 %collective-permute-start.28 = (bf16[2,4,160,128]{3,2,1,0:T(8,128)(2,1)S(1)}, bf16[2,4,160,128]{3,2,1,0:T(8,128)(2,1)S(1)}, u32[]{:S(2)}, u32[]{:S(2)}) collective-permute-start(bf16[2,4,160,128]{3,2,1,0:T(8,128)(2,1)S(1)} %fusion.8), channel_id=1, source_target_pairs={{0,64},{32,96},{64,0},{96,32},{1,65},{33,97},{65,1},{97,33},{2,66}... | collective-permute-start | bytes 983048 | tf_op jit(solution)/shard_map/ppermute | solution.py:65
  116.9 10.3 %collective-permute-start.37 = (bf16[160,1024]{1,0:T(8,128)(2,1)S(1)}, bf16[160,1024]{1,0:T(8,128)(2,1)S(1)}, u32[]{:S(2)}, u32[]{:S(2)}) collective-permute-start(bf16[160,1024]{1,0:T(8,128)(2,1)S(1)} %add_convert_fusion), channel_id=1, source_target_pairs={{0,28},{1,29},{2,30},{3,31},{4,0},{5,1},{6,2},{7,3},{8,4},{9,5},{1... | collective-permute-start | bytes 983048 | tf_op jit(solution)/shard_map/ppermute | solution.py:51
  118.5 9.7 %collective-permute-start.24 = (bf16[2,4,160,128]{3,2,1,0:T(8,128)(2,1)S(1)}, bf16[2,4,160,128]{3,2,1,0:T(8,128)(2,1)S(1)}, u32[]{:S(2)}, u32[]{:S(2)}) collective-permute-start(bf16[2,4,160,128]{3,2,1,0:T(8,128)(2,1)S(1)} %fusion.2), channel_id=1, source_target_pairs={{0,32},{32,0},{64,96},{96,64},{128,160},{160,128},{192,224},{224,1... | collective-permute-start | bytes 983048 | tf_op jit(solution)/shard_map/ppermute | solution.py:60
  123.3 5.1 %copy-start.2 = (bf16[128,5120]{1,0:T(8,128)(2,1)S(1)}, bf16[128,5120]{1,0:T(8,128)(2,1)}, u32[]{:S(2)}) copy-start(bf16[128,5120]{1,0:T(8,128)(2,1)} %refs_14_.1) | copy-start | bytes 3932164
  123.3 5.1 %copy-start.16 = (f32[128]{0:T(128)S(1)}, f32[128]{0:T(128)}, u32[]{:S(2)}) copy-start(f32[128]{0:T(128)} %param.22) | copy-start | bytes 1540
  123.3 5.1 %copy-start.17 = (f32[128]{0:T(128)S(1)}, f32[128]{0:T(128)}, u32[]{:S(2)}) copy-start(f32[128]{0:T(128)} %param.23) | copy-start | bytes 1540
  123.4 5.1 %copy-start.18 = (f32[1,4]{1,0:T(1,128)S(1)}, f32[1,4]{1,0:T(1,128)}, u32[]{:S(2)}) copy-start(f32[1,4]{1,0:T(1,128)} %refs_17_.1) | copy-start | bytes 52
  123.4 5.1 %collective-permute-start.29 = (bf16[2,4,160,128]{3,2,1,0:T(8,128)(2,1)S(1)}, bf16[2,4,160,128]{3,2,1,0:T(8,128)(2,1)S(1)}, u32[]{:S(2)}, u32[]{:S(2)}) collective-permute-start(bf16[2,4,160,128]{3,2,1,0:T(8,128)(2,1)S(1)} %fusion.7), channel_id=1, source_target_pairs={{0,32},{32,0},{64,96},{96,64},{128,160},{160,128},{192,224},{224,1... | collective-permute-start | bytes 983048 | tf_op jit(solution)/shard_map/ppermute | solution.py:60

commit v2 on v1

v2 whole, which is shorter than its diff:
```python
import functools
import math

import jax
import jax.numpy as jnp
from jax import lax
from jax.experimental import pallas as pl
from jax.experimental.pallas import tpu as pltpu
from jax.sharding import PartitionSpec as P

D = 5120
HD = 128
KVH = 4
GROUP = 8
KVW = 512
ROWS = 128
NZ = 8
NX = 4
NY = 4
SLAB = D // (NZ * NX)
EPSILON = 1e-06
VMEM = pltpu.CompilerParams(vmem_limit_bytes=48 * 1024 * 1024)
MOST_VMEM = pltpu.CompilerParams(vmem_limit_bytes=57 * 1024 * 1024)
NT = (((1,), (1,)), ((), ()))

Z_ORDER = (0, 1, 7, 2, 6, 3, 5, 4)
COTS = 2 * KVW // 128
RELAY = NZ * SLAB
RELAYED = NZ // 2 * SLAB + COTS // 2 * ROWS
SENT = RELAY + RELAYED + COTS // 2 * ROWS


def shape_of(shape, dtype=jnp.bfloat16):
    return jax.ShapeDtypeStruct(shape, dtype)


def whole(count):
    return [pl.BlockSpec(memory_space=pltpu.VMEM)] * count


def after(values, *first):
    return lax.optimization_barrier((values, first))[0]


def cost(flops, moved, exps=0):
    return pl.CostEstimate(flops=flops, bytes_accessed=moved, transcendentals=exps)


def shift_z(value, step):
    pairs = [(z * NX + x, ((z + step) % NZ) * NX + x) for z in range(NZ) for x in range(NX)]
    return lax.ppermute(value, "dp", pairs)


def shift_x(value, step):
    pairs = [(z * NX + x, z * NX + (x + step) % NX) for z in range(NZ) for x in range(NX)]
    return lax.ppermute(value, "dp", pairs)


def swap_core(value):
    return lax.ppermute(value, "section", [(s, s ^ 1) for s in range(2 * NY)])


def send_y(value, routes):
    pairs = [(2 * a + c, 2 * b + c) for a, b in routes for c in range(2)]
    return lax.ppermute(value, "section", pairs)


def place():
    own = lax.axis_index("dp")
    layer = lax.axis_index("section")
    return own // NX, own % NX, layer // 2, layer % 2


def start_copies(sources, targets, sems):
    copies = [
        pltpu.make_async_copy(source, target, sems.at[index])
        for index, (source, target) in enumerate(zip(sources, targets))
    ]
    for copy in copies:
        copy.start()
    return copies


def attend_kernel(*refs):
    sources, (out_ref, near_ref, up_ref, down_ref) = refs[:6], refs[6:10]
    targets, held, sems = refs[10:16], refs[16], refs[17]
    copies = start_copies(sources, targets, sems)
    h_ref, row_ref, k_ref, v_ref, q_ref, o_ref = targets
    z, x, _, _ = place()
    copies[0].wait()
    squares = jnp.zeros((ROWS, 128), jnp.float32)
    for tile in range(D // 128):
        part = h_ref[:, tile * 128 : (tile + 1) * 128]
        turned = part.T
        part = part.astype(jnp.float32)
        squares = squares + part * part
        for piece in range(4):
            unit = tile * 4 + piece
            slab, fifth = unit // 5, unit % 5
            k = lax.rem(slab // NX - z + NZ, NZ)
            d = lax.rem(slab % NX - x + NX, NX)
            held[d, k, fifth * 32 : (fifth + 1) * 32, :] = turned[piece * 32 : (piece + 1) * 32, :]
    near_ref[...] = held[0]
    for ref, d, first in ((up_ref, 1, 0), (down_ref, 3, NZ // 2)):
        for k in range(NZ):
            ref[k * SLAB : (k + 1) * SLAB, :] = held[d, k]
        for k in range(NZ // 2):
            ref[RELAY + k * SLAB : RELAY + (k + 1) * SLAB, :] = held[2, first + k]
    inv_rms = lax.rsqrt(jnp.sum(squares, axis=1, keepdims=True) * (1.0 / D) + EPSILON)
    for copy in copies[1:]:
        copy.wait()
    j_place = lax.broadcasted_iota(jnp.int32, (ROWS, ROWS), 0)
    i_place = lax.broadcasted_iota(jnp.int32, (ROWS, ROWS), 1)
    segment = jnp.broadcast_to(row_ref[...].astype(jnp.float32), (ROWS, ROWS))
    allowed = (segment.T == segment) & (j_place <= i_place)
    scale = 1.0 / math.sqrt(HD)
    for g in range(KVH):
        key = k_ref[:, g * HD : (g + 1) * HD]
        value = v_ref[:, g * HD : (g + 1) * HD]
        heads = range(g * GROUP, (g + 1) * GROUP)
        query = jnp.concatenate([q_ref[:, n * HD : (n + 1) * HD] for n in heads], axis=0)
        cot = jnp.concatenate([o_ref[:, n * HD : (n + 1) * HD] for n in heads], axis=0)
        scores = lax.dot_general(key, query, NT, preferred_element_type=jnp.float32) * scale
        prob_cot = lax.dot_general(value, cot, NT, preferred_element_type=jnp.float32)
        halves, cots = [], []
        for n in range(GROUP):
            span = slice(n * ROWS, (n + 1) * ROWS)
            score = jnp.where(allowed, scores[:, span], -jnp.inf)
            high = jnp.max(score, axis=0, keepdims=True)
            grown = jnp.exp(score - high)
            probs = grown * (1.0 / jnp.sum(grown, axis=0, keepdims=True))
            half = probs.astype(jnp.bfloat16)
            pulled = prob_cot[:, span]
            delta = jnp.sum(half.astype(jnp.float32) * pulled, axis=0, keepdims=True)
            halves.append(half)
            cots.append((probs * (pulled - delta)).astype(jnp.bfloat16))
        key_cot = jnp.dot(jnp.concatenate(cots, axis=1), query, preferred_element_type=jnp.float32)
        value_cot = jnp.dot(jnp.concatenate(halves, axis=1), cot, preferred_element_type=jnp.float32)
        key_cot = (key_cot * scale).astype(jnp.bfloat16).astype(jnp.float32)
        value_cot = value_cot.astype(jnp.bfloat16).astype(jnp.float32)
        for index, value in ((g, key_cot), (KVH + g, value_cot)):
            scaled = (value * inv_rms).astype(jnp.bfloat16)
            out_ref[:, index * HD : (index + 1) * HD] = scaled
            for ref, turn in ((up_ref, 0), (down_ref, KVH)):
                first = SENT - COTS * ROWS + (index + turn) % COTS * ROWS
                ref[first : first + ROWS, :] = scaled


def attend(hidden, row, keys, values, queries, cotangent):
    operands = (hidden, row, keys, values, queries, cotangent)
    return pl.pallas_call(
        attend_kernel,
        out_shape=[
            shape_of((ROWS, 2 * KVW)),
            shape_of((NZ, SLAB, ROWS)),
            shape_of((SENT, ROWS)),
            shape_of((SENT, ROWS)),
        ],
        in_specs=[pl.BlockSpec(memory_space=pl.ANY)] * 6,
        out_specs=whole(4),
        scratch_shapes=[pltpu.VMEM(a.shape, a.dtype) for a in operands]
        + [pltpu.VMEM((NX, NZ, SLAB, ROWS), jnp.bfloat16), pltpu.SemaphoreType.DMA((6,))],
        compiler_params=MOST_VMEM,
        cost_estimate=cost(4 * 32 * 2 * 128**3, 4 * 2**20, 32 * 128 * 128),
        name="attend",
    )(*operands)


def join_cots(cots, up, down, far_up, far_down, right):
    right[:ROWS] = cots[...]
    lead, far = SENT - COTS * ROWS, RELAYED - COTS // 2 * ROWS
    for tile in range(COTS):
        span = slice(tile * 128, (tile + 1) * 128)
        first = lead + tile * ROWS
        right[ROWS : 2 * ROWS, span] = up[first : first + ROWS]
        source, first = (far_up, far + tile * ROWS) if tile < COTS // 2 else (far_down, far + (tile - COTS // 2) * ROWS)
        right[2 * ROWS : 3 * ROWS, span] = source[first : first + ROWS]
        first = lead + (tile + COTS // 2) % COTS * ROWS
        right[3 * ROWS :, span] = down[first : first + ROWS]


def grad_kernel(near, cots, up, down, far_up, far_down, *refs):
    outs, left, right = refs[:NZ], refs[NZ], refs[NZ + 1]
    join_cots(cots, up, down, far_up, far_down, right)
    middle = NZ // 2 * SLAB
    left[:, :ROWS] = near[...].reshape(NZ * SLAB, ROWS)
    left[:, ROWS : 2 * ROWS] = up[: NZ * SLAB]
    left[:middle, 2 * ROWS : 3 * ROWS] = far_up[:middle]
    left[middle:, 2 * ROWS : 3 * ROWS] = far_down[:middle]
    left[:, 3 * ROWS :] = down[: NZ * SLAB]
    for k in range(NZ):
        outs[k][...] = jnp.dot(
            left[k * SLAB : (k + 1) * SLAB], right[...], preferred_element_type=jnp.float32
        ).astype(jnp.bfloat16)


def weight_terms(near, met):
    return pl.pallas_call(
        grad_kernel,
        out_shape=[shape_of((SLAB, 2 * KVW))] * NZ,
        in_specs=whole(6),
        out_specs=whole(NZ),
        scratch_shapes=[
            pltpu.VMEM((NZ * SLAB, NX * ROWS), jnp.bfloat16),
            pltpu.VMEM((NX * ROWS, 2 * KVW), jnp.bfloat16),
        ],
        compiler_params=VMEM,
        cost_estimate=cost(2 * 512 * 1280 * 1024, 6 * 2**20),
        name="weight_terms",
    )(near, *met)


def back_kernel(count, past, *refs):
    weights, cots = refs[:count], refs[count : count + 5]
    earlier, outs, right = refs[count + 5 : -1 - NX], refs[-1 - NX : -1], refs[-1]
    join_cots(*cots, right)
    for d, ref in enumerate(earlier):
        outs[d][:past] = ref[...]
    for place_k, weight in enumerate(weights, past):
        full = lax.dot_general(weight[...], right[...], NT, preferred_element_type=jnp.float32)
        for d in range(NX):
            outs[d][place_k] = full[:, d * ROWS : (d + 1) * ROWS].astype(jnp.bfloat16)


def back(weights, cots, earlier=()):
    count = len(weights)
    past = earlier[0].shape[0] if earlier else 0
    return pl.pallas_call(
        functools.partial(back_kernel, count, past),
        out_shape=[shape_of((past + count, SLAB, ROWS))] * NX,
        in_specs=whole(count + 5 + len(earlier)),
        out_specs=whole(NX),
        scratch_shapes=[pltpu.VMEM((NX * ROWS, 2 * KVW), jnp.bfloat16)],
        compiler_params=VMEM,
        cost_estimate=cost(2 * 512 * 160 * count * 1024, 2**20 * 3),
        name="back",
    )(*weights, *cots, *earlier)


def local_kernel(*refs):
    products, (near, up, down) = refs[:NX], refs[NX : NX + 3]
    mine, other, held = refs[NX + 3 : NX + 5], refs[NX + 5 : NX + 7], refs[-1]

    def stream_of(d, k):
        if d == 0:
            part = near[k]
        else:
            source = (None, up, up if k < NZ // 2 else down, down)[d]
            first = RELAY + k % (NZ // 2) * SLAB if d == 2 else k * SLAB
            part = source[first : first + SLAB, :]
        return part.astype(jnp.float32)

    _, _, _, core = place()
    squares = jnp.zeros((SLAB, ROWS), jnp.float32)
    along = jnp.zeros((SLAB, ROWS), jnp.float32)
    for d in range(NX):
        for place_k, k in enumerate(Z_ORDER):
            stream = stream_of(d, k)
            squares = squares + stream * stream
            along = along + stream * products[d][place_k].astype(jnp.float32)
    inv_rms = lax.rsqrt(jnp.sum(squares, axis=0, keepdims=True) * (1.0 / D) + EPSILON)
    pull = inv_rms * inv_rms * (jnp.sum(along, axis=0, keepdims=True) * (1.0 / D))
    for d in range(NX):
        for place_k, k in enumerate(Z_ORDER):
            stream = stream_of(d, k)
            term = products[d][place_k].astype(jnp.float32) - stream * pull
            held[k // 4, k % 4, d] = term.astype(jnp.bfloat16)
    for chunk in range(2):
        mine[chunk][...] = held[core, 2 * chunk : 2 * chunk + 2]
        other[chunk][...] = held[1 - core, 2 * chunk : 2 * chunk + 2]


def local_terms(products, turned):
    return pl.pallas_call(
        local_kernel,
        out_shape=[shape_of((2, NX, SLAB, ROWS))] * 4,
        in_specs=whole(NX + 3),
        out_specs=whole(4),
        scratch_shapes=[pltpu.VMEM((2, 4, NX, SLAB, ROWS), jnp.bfloat16)],
        compiler_params=VMEM,
        cost_estimate=cost(0, 4 * 2**20),
        name="local_terms",
    )(*products, *turned)


FINISH_STEPS = 5
FINISH_WIDE = D // FINISH_STEPS


def spread(total, half, value_of):
    z, x, _, _ = place()
    for a in range(4):
        for d in range(NX):
            slab = lax.rem(z + half * 4 + a, NZ) * NX + lax.rem(x + d, NX)
            total[pl.ds(pl.multiple_of(slab * SLAB, 32), SLAB), :] = value_of(a, d)


def part_of(chunks, a, d):
    return chunks[a // 2][a % 2, d].astype(jnp.float32)


def base_kernel(*refs):
    mine, met, other = refs[:2], refs[2:4], refs[4:6]
    top_ref, row_ref, out_ref, total, coef = refs[6:]
    _, _, _, core = place()
    below = (1 - core).astype(jnp.float32)
    step = pl.program_id(0)

    def own_of(a, d):
        return part_of(mine, a, d) + below * part_of(met, a, d)

    @pl.when(step == 0)
    def _():
        spread(total, core, own_of)
        spread(total, 1 - core, functools.partial(part_of, other))
        coef[...] = jnp.broadcast_to(row_ref[...], (ROWS, ROWS)).T

    coefficient = coef[...]
    for tile in range(FINISH_WIDE // 128):
        span = slice(tile * 128, (tile + 1) * 128)
        first = pl.multiple_of(step * FINISH_WIDE + tile * 128, 128)
        top = coefficient * top_ref[:, span].astype(jnp.float32)
        out_ref[:, span] = top + total[pl.ds(first, 128), :].T


def base_terms(mine, met, other, top, coefficient):
    return pl.pallas_call(
        base_kernel,
        grid=(FINISH_STEPS,),
        out_shape=shape_of((ROWS, D), jnp.float32),
        in_specs=whole(6) + [pl.BlockSpec((ROWS, FINISH_WIDE), lambda step: (0, step))] + whole(1),
        out_specs=pl.BlockSpec((ROWS, FINISH_WIDE), lambda step: (0, step)),
        scratch_shapes=[pltpu.VMEM((D, ROWS), jnp.float32), pltpu.VMEM((ROWS, ROWS), jnp.float32)],
        compiler_params=VMEM,
        cost_estimate=cost(0, 8 * 2**20),
        name="base_terms",
    )(*mine, *met, *other, top, coefficient)


def finish_kernel(*refs):
    wrap, down, swap, back_in = refs[:2], refs[2:4], refs[4:6], refs[6:8]
    base_ref, out_ref, total = refs[8:]
    _, _, _, core = place()
    step = pl.program_id(0)

    def upper_of(a, d):
        return part_of(wrap, a, d) + (part_of(down, a, d) + part_of(swap, a, d))

    @pl.when(step == 0)
    def _():
        spread(total, core, upper_of)
        spread(total, 1 - core, functools.partial(part_of, back_in))

    for tile in range(FINISH_WIDE // 128):
        span = slice(tile * 128, (tile + 1) * 128)
        first = pl.multiple_of(step * FINISH_WIDE + tile * 128, 128)
        out_ref[:, span] = (base_ref[:, span] + total[pl.ds(first, 128), :].T).astype(jnp.bfloat16)


def finish(wrap, down, swap, back_in, base):
    return pl.pallas_call(
        finish_kernel,
        grid=(FINISH_STEPS,),
        out_shape=shape_of((ROWS, D)),
        in_specs=whole(8) + [pl.BlockSpec((ROWS, FINISH_WIDE), lambda step: (0, step))],
        out_specs=pl.BlockSpec((ROWS, FINISH_WIDE), lambda step: (0, step)),
        scratch_shapes=[pltpu.VMEM((D, ROWS), jnp.float32)],
        compiler_params=VMEM,
        cost_estimate=cost(0, 6 * 2**20),
        name="finish",
    )(*wrap, *down, *swap, *back_in, base)


def scatter_z(terms):
    half = SLAB // 2
    wide = jnp.float32

    def add(first, second):
        return (first.astype(wide) + second.astype(wide)).astype(jnp.bfloat16)

    far_up, far_down = shift_z(terms[4][:half], 1), shift_z(terms[4][half:], -1)
    up = jnp.concatenate([add(terms[3][:half], far_up), terms[3][half:]], axis=0)
    down = jnp.concatenate([terms[5][:half], add(terms[5][half:], far_down)], axis=0)
    up, down = shift_z(up, 1), shift_z(down, -1)
    up, down = add(terms[2], up), add(terms[6], down)
    up, down = shift_z(up, 1), shift_z(down, -1)
    up, down = add(terms[1], up), add(terms[7], down)
    return terms[0], shift_z(up, 1), shift_z(down, -1)


def local(
    hidden_in,
    norm_gain,
    key_weight,
    value_weight,
    queries,
    stashed_keys,
    stashed_values,
    out_cotangent,
    logprob_grad,
    new_logprob,
    old_logprob,
    advantages,
    segment_ids,
):
    wide = jnp.float32
    _, _, y, core = place()
    half = SLAB // 2
    gain = norm_gain[0].astype(wide)[:, None]
    weight_pair = jnp.concatenate([key_weight[0], value_weight[0]], axis=1).astype(wide)
    own = (weight_pair * gain).astype(jnp.bfloat16)
    up_1, down_1 = shift_z(own, 1), shift_z(own, -1)

    cots, near, part_up, part_down = attend(
        hidden_in[0],
        after(segment_ids, own),
        stashed_keys[0],
        stashed_values[0],
        queries[0],
        out_cotangent[0],
    )
    up_1, down_1 = after((up_1, down_1), cots)
    met_up, met_down = shift_x(part_up, 1), shift_x(part_down, -1)
    up_2, down_2 = shift_z(up_1, 1), shift_z(down_1, -1)

    segments = after(segment_ids, up_1)[0]
    row_adv = jnp.zeros((ROWS,), wide)
    for index in range(advantages.shape[1]):
        row_adv = row_adv + jnp.where(segments == index, advantages[0, index], 0.0)
    ratio = jnp.exp(after(new_logprob, up_1) - old_logprob)
    coefficient = -jnp.clip(ratio, 0.8, 1.28) * row_adv
    up_2, down_2 = after((up_2, down_2), coefficient)

    up_3, down_3 = shift_z(up_2, 1), shift_z(down_2, -1)
    relay = slice(RELAY, RELAY + RELAYED)
    far_up, far_down = shift_x(met_up[relay], 1), shift_x(met_down[relay], -1)
    met = [cots, met_up, met_down, far_up, far_down]
    up_4, down_4 = shift_z(up_3[:half], 1), shift_z(down_3[half:], -1)

    firsts = back([own, down_1, up_1, down_2, up_2, down_3, up_3], met)
    opposite = jnp.concatenate([up_4, down_4], axis=0)
    products = back([opposite], met, firsts)
    met_late = after(met, products[0])
    products = [products[0]] + [shift_x(products[d], -d) for d in (1, 2, 3)]
    terms = weight_terms(near, met_late)
    sums = scatter_z(after(terms, products[1]))
    key_grad, value_grad = (
        gain * (sums[0][:, span].astype(wide) + (sums[1][:, span].astype(wide) + sums[2][:, span].astype(wide)))
        for span in (slice(0, KVW), slice(KVW, 2 * KVW))
    )

    *mine, other_a, other_b = local_terms(products, (near, part_up, part_down))
    other = [other_a, other_b]
    met_other = [swap_core(part) for part in other]
    pairs = [(own.astype(wide) + part.astype(wide)).astype(jnp.bfloat16) for own, part in zip(mine, met_other)]
    base = base_terms(mine, met_other, other, logprob_grad, after(coefficient[None], *pairs))
    wrap, down, swap, back_in = [], [], [], []
    for own, pair in zip(mine, pairs):
        wrap.append(send_y(pair, [(3, 0)]))
        down.append(send_y(pair, [(3, 2), (2, 1)]))
        if len(wrap) == 2:
            wrap[-1] = after(wrap[-1], base)
        onward = jnp.where(y == 0, wrap[-1].astype(wide), pair.astype(wide) + down[-1].astype(wide))
        swap.append(send_y(onward.astype(jnp.bfloat16), [(0, 1), (1, 0)]))
        upper = wrap[-1].astype(wide) + (down[-1].astype(wide) + swap[-1].astype(wide))
        upper = upper + jnp.where(core == 1, own.astype(wide), 0.0)
        back_in.append(swap_core(upper.astype(jnp.bfloat16)))
    hidden_cotangent = finish(wrap, down, swap, back_in, base)
    return hidden_cotangent[None], key_grad[None], value_grad[None]


def solution(mesh):
    return jax.shard_map(
        local,
        mesh=mesh,
        in_specs=(
            P("section", "dp", None),
            P("section", "dp"),
            P("section", "dp", None),
            P("section", "dp", None),
            P("section", "dp", None),
            P("section", "dp", None),
            P("section", "dp", None),
            P("section", "dp", None),
            P("dp", None),
            P("dp"),
            P("dp"),
            P("dp", None),
            P("dp", None),
        ),
        out_specs=(P("section", "dp", None), P("section", "dp", None), P("section", "dp", None)),
        check_vma=False,
    )
```

time: 133 us -> 112 us (0.84)
  waiting for transfers between devices: 40.9 us -> 26 us
  starting transfers between devices: 60.1 us -> 54.3 us
  local copies, waits for them, and re-layouts: 11.1 us -> 5.46 us
  other arithmetic: 4.27 us -> 7.58 us
  Pallas kernels: 15.1 us -> 16.9 us
    ppermute x12 -> x7, waiting for transfers between devices: 22.5 us -> 5.71 us  [shift_x(): return lax.ppermute(value, 'dp', pairs)]
    ppermute x12 -> x7, starting transfers between devices: 19.2 us -> 8.59 us  [shift_x(): return lax.ppermute(value, 'dp', pairs)]
    unnamed x38 -> x42, local copies, waits for them, and re-layouts: 9.38 us -> 3.04 us
    ppermute x16, waiting for transfers between devices: 7 us -> 12.6 us  [shift_z(): return lax.ppermute(value, 'dp', pairs)]
    pallas_call x4, Pallas kernels: 7.35 us -> 11.2 us  [the longest x1 5.51 us: attend(): pl.pallas_call(attend_kernel, out_shape=[shape_of((ROWS, 2 * KVW)), shape...]
    ppermute x6, waiting for transfers between devices: 11.2 us -> 7.41 us  [send_y(): return lax.ppermute(value, 'section', pairs)]
    ppermute x6, starting transfers between devices: 7.78 us -> 11.4 us  [send_y(): return lax.ppermute(value, 'section', pairs)]
    mul x1, other arithmetic: 0.14 us -> 2.51 us  [local(): coefficient = -jnp.clip(ratio, 0.8, 1.28) * row_adv]
  transfers between devices with their start and end apart: 38 -> 33, of which waited for: 12 -> 11; matrix products, arithmetic and copies ran while one was open for 3% -> 7% of each run, Pallas kernels for 8% -> 6%
where the time goes in v2:
time: 112 us; the launch traced here: 111 us
  starting transfers between devices  54.3 us (48%)
  waiting for transfers between devices  26 us (23%)
  Pallas kernels  16.9 us (15%)
  other arithmetic  7.58 us (7%)
  local copies, waits for them, and re-layouts  5.46 us (5%)
  between operations  1.14 us (1%)
    ppermute x16, starting transfers between devices, shift_z(): return lax.ppermute(value, 'dp', pairs)  22.7 us
    ppermute x16, waiting for transfers between devices, shift_z(): return lax.ppermute(value, 'dp', pairs)  12.6 us
    ppermute x4, starting transfers between devices, swap_core(): return lax.ppermute(value, 'section', [(s, s ^ 1) for s in range(2 * NY)])  11.6 us
    ppermute x6, starting transfers between devices, send_y(): return lax.ppermute(value, 'section', pairs)  11.4 us
    ppermute x7, starting transfers between devices, shift_x(): return lax.ppermute(value, 'dp', pairs)  8.59 us
    ppermute x6, waiting for transfers between devices, send_y(): return lax.ppermute(value, 'section', pairs)  7.41 us
    ppermute x7, waiting for transfers between devices, shift_x(): return lax.ppermute(value, 'dp', pairs)  5.71 us
    pallas_call x1, Pallas kernels, attend(): pl.pallas_call(attend_kernel, out_shape=[shape_of((ROWS, 2 * KVW)), shape...  5.51 us
  transfers between devices with their start and end apart: 33, of which 11 were waited for; matrix products, arithmetic and copies ran while one was open for 7% of the time, Pallas kernels for 6%

profile of v2, /device:TPU:1, one launch (start us, length us, event | category | flops | bytes accessed | tf_op | source)
XLA Modules:
  0.0 111.4 jit_solution(7598975456719814887)
XLA Ops:
  0.6 0.7 convert_element_type.194
  1.3 1.1 %multiply_convert_fusion.refs_0_ = bf16[160,1024]{1,0:T(8,128)(2,1)S(1)} fusion(bf16[160,512]{1,0:T(8,128)(2,1)} %bitcast.27, bf16[160,512]{1,0:T(8,128)(2,1)} %bitcast.28, f32[160]{0:T(256)S(1)} %bitcast.31), kind=kLoop, calls=%fused_computation.24 | loop fusion | flops 983040 | bytes 656000 | tf_op jit(solution)/shard_map/convert_element_type | solution.py:411
  2.5 5.5 %attend.1 = (bf16[128,1024]{1,0:T(8,128)(2,1)}, bf16[8,160,128]{2,1,0:T(8,128)(2,1)}, bf16[2944,128]{1,0:T(8,128)(2,1)}, bf16[2944,128]{1,0:T(8,128)(2,1)}) custom-call(bf16[128,5120]{1,0:T(8,128)(2,1)} %bitcast.23, s32[1,128]{1,0:T(1,128)} %refs_1_, bf16[128,512]{1,0:T(8,128)(2,1)} %bitcast.29, bf16[128,512]{1,0:T(8,128)(2,1)} %bitcast.30, ...), custom_call_target="tpu_custom_call" | custom-call | flops 536870912 | bytes 4194304 | tf_op jit(solution)/shard_map/attend/pallas_call | solution.py:151
  8.0 2.1 %collective-permute-start.8 = (bf16[2944,128]{1,0:T(8,128)(2,1)}, bf16[2944,128]{1,0:T(8,128)(2,1)S(1)}, u32[]{:S(2)}, u32[]{:S(2)}) collective-permute-start(bf16[2944,128]{1,0:T(8,128)(2,1)} %get-tuple-element.57.refs_5_), channel_id=1, source_target_pairs={{0,1},{1,2},{2,3},{3,0},{4,5},{5,6},{6,7},{7,4},{8,9},{9,10},{10,1... | collective-permute-start | bytes 2261000 | tf_op jit(solution)/shard_map/ppermute | solution.py:56
  10.1 1.4 %collective-permute-start.9 = (bf16[2944,128]{1,0:T(8,128)(2,1)}, bf16[2944,128]{1,0:T(8,128)(2,1)S(1)}, u32[]{:S(2)}, u32[]{:S(2)}) collective-permute-start(bf16[2944,128]{1,0:T(8,128)(2,1)} %get-tuple-element.58.refs_6_), channel_id=1, source_target_pairs={{0,3},{1,0},{2,1},{3,2},{4,7},{5,4},{6,5},{7,6},{8,11},{9,8},{10,9... | collective-permute-start | bytes 2261000 | tf_op jit(solution)/shard_map/ppermute | solution.py:56
  11.5 1.7 %collective-permute-start = (bf16[160,1024]{1,0:T(8,128)(2,1)S(1)}, bf16[160,1024]{1,0:T(8,128)(2,1)S(1)}, u32[]{:S(2)}, u32[]{:S(2)}) collective-permute-start(bf16[160,1024]{1,0:T(8,128)(2,1)S(1)} %multiply_convert_fusion.refs_0_), channel_id=1, source_target_pairs={{0,4},{1,5},{2,6},{3,7},{4,8},{5,9},{6,10},{7,11},{8,12},{9,13},{1... | collective-permute-start | bytes 983048 | tf_op jit(solution)/shard_map/ppermute | solution.py:51
  13.2 3.9 %collective-permute-start.1 = (bf16[160,1024]{1,0:T(8,128)(2,1)S(1)}, bf16[160,1024]{1,0:T(8,128)(2,1)S(1)}, u32[]{:S(2)}, u32[]{:S(2)}) collective-permute-start(bf16[160,1024]{1,0:T(8,128)(2,1)S(1)} %multiply_convert_fusion.refs_0_), channel_id=1, source_target_pairs={{0,28},{1,29},{2,30},{3,31},{4,0},{5,1},{6,2},{7,3},{8,4},{9,5},{1... | collective-permute-start | bytes 983048 | tf_op jit(solution)/shard_map/ppermute | solution.py:51
  17.2 6.8 %collective-permute-done.refs_2_ = bf16[160,1024]{1,0:T(8,128)(2,1)S(1)} collective-permute-done((bf16[160,1024]{1,0:T(8,128)(2,1)S(1)}, bf16[160,1024]{1,0:T(8,128)(2,1)S(1)}, u32[]{:S(2)}, u32[]{:S(2)}) %collective-permute-start) | collective-permute-done | bytes 327712 | tf_op jit(solution)/shard_map/ppermute | solution.py:51
  24.0 2.7 %collective-permute-start.3 = (bf16[160,1024]{1,0:T(8,128)(2,1)S(1)}, bf16[160,1024]{1,0:T(8,128)(2,1)S(1)}, u32[]{:S(2)}, u32[]{:S(2)}) collective-permute-start(bf16[160,1024]{1,0:T(8,128)(2,1)S(1)} %collective-permute-done.1.refs_1_), channel_id=1, source_target_pairs={{0,28},{1,29},{2,30},{3,31},{4,0},{5,1},{6,2},{7,3},{8,4},{9,5},{1... | collective-permute-start | bytes 983048 | tf_op jit(solution)/shard_map/ppermute | solution.py:51
  26.7 0.7 fusion.14
  27.3 2.5 %fusion.12 = f32[128]{0:T(128)S(1)} fusion(s32[1,128]{1,0:T(1,128)S(1)} %copy-done.18, f32[128]{0:T(128)S(1)} %copy-done.19, f32[128]{0:T(128)S(1)} %copy-done.20, f32[]{:T(128)} %bitcast.11, f32[]{:T(128)} %bitcast.10, f32[]{:T(128)} %bitcast.9, f32[]{:T(128)} %bitcast.8), kind=kLoop, calls=%fused_computation.40 | loop fusion | flops 1920 | bytes 2064 | tf_op jit(solution)/shard_map/mul | solution.py:431
  29.9 2.7 %collective-permute-done.2.refs_4_ = bf16[160,1024]{1,0:T(8,128)(2,1)S(1)} collective-permute-done((bf16[160,1024]{1,0:T(8,128)(2,1)S(1)}, bf16[160,1024]{1,0:T(8,128)(2,1)S(1)}, u32[]{:S(2)}, u32[]{:S(2)}) %collective-permute-start.2) | collective-permute-done | bytes 327712 | tf_op jit(solution)/shard_map/ppermute | solution.py:51
  32.5 1.0 collective-permute-start.4
  33.6 1.7 %collective-permute-start.6 = (bf16[160,1024]{1,0:T(8,128)(2,1)S(1)}, bf16[160,1024]{1,0:T(8,128)(2,1)S(1)}, u32[]{:S(2)}, u32[]{:S(2)}) collective-permute-start(bf16[160,1024]{1,0:T(8,128)(2,1)S(1)} %collective-permute-done.3.refs_3_), channel_id=1, source_target_pairs={{0,28},{1,29},{2,30},{3,31},{4,0},{5,1},{6,2},{7,3},{8,4},{9,5},{1... | collective-permute-start | bytes 983048 | tf_op jit(solution)/shard_map/ppermute | solution.py:51
  35.4 2.7 %collective-permute-start.11 = (bf16[1152,128]{1,0:T(8,128)(2,1)S(1)}, bf16[1152,128]{1,0:T(8,128)(2,1)S(1)}, u32[]{:S(2)}, u32[]{:S(2)}) collective-permute-start(bf16[1152,128]{1,0:T(8,128)(2,1)S(1)} %slice.83), channel_id=1, source_target_pairs={{0,3},{1,0},{2,1},{3,2},{4,7},{5,4},{6,5},{7,6},{8,11},{9,8},{10,9... | collective-permute-start | bytes 884744 | tf_op jit(solution)/shard_map/ppermute | solution.py:56
  38.1 2.1 %collective-permute-done.4.refs_6_ = bf16[160,1024]{1,0:T(8,128)(2,1)S(1)} collective-permute-done((bf16[160,1024]{1,0:T(8,128)(2,1)S(1)}, bf16[160,1024]{1,0:T(8,128)(2,1)S(1)}, u32[]{:S(2)}, u32[]{:S(2)}) %collective-permute-start.4) | collective-permute-done | bytes 327712 | tf_op jit(solution)/shard_map/ppermute | solution.py:51
  40.3 2.9 %collective-permute-start.7 = (bf16[80,1024]{1,0:T(8,128)(2,1)S(1)}, bf16[80,1024]{1,0:T(8,128)(2,1)S(1)}, u32[]{:S(2)}, u32[]{:S(2)}) collective-permute-start(bf16[80,1024]{1,0:T(8,128)(2,1)S(1)} %slice.81), channel_id=1, source_target_pairs={{0,28},{1,29},{2,30},{3,31},{4,0},{5,1},{6,2},{7,3},{8,4},{9,5},{1... | collective-permute-start | bytes 491528 | tf_op jit(solution)/shard_map/ppermute | solution.py:51
  43.2 2.6 %back.2 = (bf16[7,160,128]{2,1,0:T(8,128)(2,1)S(1)}, bf16[7,160,128]{2,1,0:T(8,128)(2,1)S(1)}, bf16[7,160,128]{2,1,0:T(8,128)(2,1)S(1)}, bf16[7,160,128]{2,1,0:T(8,128)(2,1)S(1)}) custom-call(bf16[160,1024]{1,0:T(8,128)(2,1)S(1)} %multiply_convert_fusion.refs_0_, bf16[160,1024]{1,0:T(8,128)(2,1)S(1)} %collective-permute-done.1.refs_1_, ...), custom_call_target="tpu_custom_call" | custom-call | flops 1174405120 | bytes 3145728 | tf_op jit(solution)/shard_map/back/pallas_call | solution.py:228
  45.8 0.1 collective-permute-done.5
  46.0 1.4 %back.3 = (bf16[8,160,128]{2,1,0:T(8,128)(2,1)S(1)}, bf16[8,160,128]{2,1,0:T(8,128)(2,1)S(1)}, bf16[8,160,128]{2,1,0:T(8,128)(2,1)}, bf16[8,160,128]{2,1,0:T(8,128)(2,1)}) custom-call(bf16[160,1024]{1,0:T(8,128)(2,1)S(1)} %pad_maximum_fusion.refs_0_, bf16[128,1024]{1,0:T(8,128)(2,1)S(1)} %copy-done.1, ...), custom_call_target="tpu_custom_call" | custom-call | flops 167772160 | bytes 3145728 | tf_op jit(solution)/shard_map/back/pallas_call | solution.py:228
  47.4 1.6 %collective-permute-start.12 = (bf16[8,160,128]{2,1,0:T(8,128)(2,1)S(1)}, bf16[8,160,128]{2,1,0:T(8,128)(2,1)S(1)}, u32[]{:S(2)}, u32[]{:S(2)}) collective-permute-start(bf16[8,160,128]{2,1,0:T(8,128)(2,1)S(1)} %get-tuple-element.64), channel_id=1, source_target_pairs={{0,3},{1,0},{2,1},{3,2},{4,7},{5,4},{6,5},{7,6},{8,11},{9,8},{10,9... | collective-permute-start | bytes 983048 | tf_op jit(solution)/shard_map/ppermute | solution.py:56
  49.1 0.6 collective-permute-start.14
  49.7 1.6 %weight_terms.1 = (bf16[160,1024]{1,0:T(8,128)(2,1)S(1)}, bf16[160,1024]{1,0:T(8,128)(2,1)S(1)}, bf16[160,1024]{1,0:T(8,128)(2,1)S(1)}, bf16[160,1024]{1,0:T(8,1...) custom-call(bf16[8,160,128]{2,1,0:T(8,128)(2,1)S(1)} %copy-done.4, ...), custom_call_target="tpu_custom_call" | custom-call | flops 1342177280 | bytes 6291456 | tf_op jit(solution)/shard_map/weight_terms/pallas_call | solution.py:198
  51.3 0.7 copy-done.9
  52.1 0.8 copy-done.11
  52.8 0.7 copy-done.13
  53.5 0.7 copy-done.15
  54.3 1.2 %collective-permute-done.12.refs_1_ = bf16[8,160,128]{2,1,0:T(8,128)(2,1)S(1)} collective-permute-done((bf16[8,160,128]{2,1,0:T(8,128)(2,1)S(1)}, bf16[8,160,128]{2,1,0:T(8,128)(2,1)S(1)}, u32[]{:S(2)}, u32[]{:S(2)}) %collective-permute-start.12) | collective-permute-done | bytes 327712 | tf_op jit(solution)/shard_map/ppermute | solution.py:56
  55.5 0.7 fusion.13
  56.2 1.8 %collective-permute-start.25 = (bf16[80,1024]{1,0:T(8,128)(2,1)}, bf16[80,1024]{1,0:T(8,128)(2,1)}, u32[]{:S(2)}, u32[]{:S(2)}) collective-permute-start(bf16[80,1024]{1,0:T(8,128)(2,1)} %get-tuple-element.97), channel_id=1, source_target_pairs={{0,4},{1,5},{2,6},{3,7},{4,8},{5,9},{6,10},{7,11},{8,12},{9,13},{1... | collective-permute-start | bytes 491528 | tf_op jit(solution)/shard_map/ppermute | solution.py:51
  58.0 0.9 slice.71
  58.9 1.0 collective-permute-start.29
  59.9 4.5 %collective-permute-done.14.refs_3_ = bf16[8,160,128]{2,1,0:T(8,128)(2,1)S(1)} collective-permute-done((bf16[8,160,128]{2,1,0:T(8,128)(2,1)}, bf16[8,160,128]{2,1,0:T(8,128)(2,1)S(1)}, u32[]{:S(2)}, u32[]{:S(2)}) %collective-permute-start.14) | collective-permute-done | bytes 327712 | tf_op jit(solution)/shard_map/ppermute | solution.py:56
  64.5 0.9 local_terms.1
  65.4 4.6 %collective-permute-start.17 = (bf16[2,4,160,128]{3,2,1,0:T(8,128)(2,1)S(1)}, bf16[2,4,160,128]{3,2,1,0:T(8,128)(2,1)S(1)}, u32[]{:S(2)}, u32[]{:S(2)}) collective-permute-start(bf16[2,4,160,128]{3,2,1,0:T(8,128)(2,1)S(1)} %get-tuple-element.71.refs_5_), channel_id=1, source_target_pairs={{0,32},{32,0},{64,96},{96,64},{128,160},{160,128},{192,224},{224,1... | collective-permute-start | bytes 983048 | tf_op jit(solution)/shard_map/ppermute | solution.py:60
  70.0 0.1 collective-permute-start.15
  70.1 1.0 add_convert_fusion.5
  71.3 2.7 %collective-permute-start.30 = (bf16[160,1024]{1,0:T(8,128)(2,1)S(1)}, bf16[160,1024]{1,0:T(8,128)(2,1)S(1)}, u32[]{:S(2)}, u32[]{:S(2)}) collective-permute-start(bf16[160,1024]{1,0:T(8,128)(2,1)S(1)} %pad_maximum_fusion.2), channel_id=1, source_target_pairs={{0,28},{1,29},{2,30},{3,31},{4,0},{5,1},{6,2},{7,3},{8,4},{9,5},{1... | collective-permute-start | bytes 983048 | tf_op jit(solution)/shard_map/ppermute | solution.py:51
  74.1 1.3 %collective-permute-start.18 = (bf16[2,4,160,128]{3,2,1,0:T(8,128)(2,1)S(1)}, bf16[2,4,160,128]{3,2,1,0:T(8,128)(2,1)S(1)}, u32[]{:S(2)}, u32[]{:S(2)}) collective-permute-start(bf16[2,4,160,128]{3,2,1,0:T(8,128)(2,1)S(1)} %fusion.3), channel_id=1, source_target_pairs={{192,0},{224,32},{193,1},{225,33},{194,2},{226,34},{195,3},{227,35... | collective-permute-start | bytes 983048 | tf_op jit(solution)/shard_map/ppermute | solution.py:65
  75.4 0.7 collective-permute-start.20
  76.2 1.3 %collective-permute-start.16 = (bf16[2,4,160,128]{3,2,1,0:T(8,128)(2,1)S(1)}, bf16[2,4,160,128]{3,2,1,0:T(8,128)(2,1)S(1)}, u32[]{:S(2)}, u32[]{:S(2)}) collective-permute-start(bf16[2,4,160,128]{3,2,1,0:T(8,128)(2,1)S(1)} %fusion), channel_id=1, source_target_pairs={{192,0},{224,32},{193,1},{225,33},{194,2},{226,34},{195,3},{227,35... | collective-permute-start | bytes 983048 | tf_op jit(solution)/shard_map/ppermute | solution.py:65
  77.6 1.7 %base_terms.1.refs_8_ = f32[128,5120]{1,0:T(8,128)S(1)} custom-call(bf16[2,4,160,128]{3,2,1,0:T(8,128)(2,1)S(1)} %get-tuple-element.68.refs_0_, bf16[2,4,160,128]{3,2,1,0:T(8,128)(2,1)S(1)} %get-tuple-element.70.refs_1_, bf16[2,4,160,128]{3,2,1,0:T(8,128)(2,1)S(1)} %collective-permute-done.15.refs_2_, ...), custom_call_target="tpu_custom_call" | custom-call | bytes 8388608 | tf_op jit(solution)/shard_map/base_terms/pallas_call | solution.py:327
  79.2 0.9 collective-permute-done.26
  80.2 0.9 collective-permute-start.19
  81.1 0.1 add_convert_fusion.3
  81.3 0.1 add_convert_fusion.1
  81.4 3.0 %collective-permute-done.18.refs_1_ = bf16[2,4,160,128]{3,2,1,0:T(8,128)(2,1)S(1)} collective-permute-done((bf16[2,4,160,128]{3,2,1,0:T(8,128)(2,1)S(1)}, bf16[2,4,160,128]{3,2,1,0:T(8,128)(2,1)S(1)}, u32[]{:S(2)}, u32[]{:S(2)}) %collective-permute-start.18) | collective-permute-done | bytes 327712 | tf_op jit(solution)/shard_map/ppermute | solution.py:65
  84.4 0.2 collective-permute-start.31
  84.7 0.1 fusion.7
  84.8 3.4 %collective-permute-start.22 = (bf16[2,4,160,128]{3,2,1,0:T(8,128)(2,1)S(1)}, bf16[2,4,160,128]{3,2,1,0:T(8,128)(2,1)S(1)}, u32[]{:S(2)}, u32[]{:S(2)}) collective-permute-start(bf16[2,4,160,128]{3,2,1,0:T(8,128)(2,1)S(1)} %fusion.7), channel_id=1, source_target_pairs={{0,64},{32,96},{64,0},{96,32},{1,65},{33,97},{65,1},{97,33},{2,66}... | collective-permute-start | bytes 983048 | tf_op jit(solution)/shard_map/ppermute | solution.py:65
  88.3 3.2 %collective-permute-done.16.refs_0_ = bf16[2,4,160,128]{3,2,1,0:T(8,128)(2,1)S(1)} collective-permute-done((bf16[2,4,160,128]{3,2,1,0:T(8,128)(2,1)S(1)}, bf16[2,4,160,128]{3,2,1,0:T(8,128)(2,1)S(1)}, u32[]{:S(2)}, u32[]{:S(2)}) %collective-permute-start.16) | collective-permute-done | bytes 327712 | tf_op jit(solution)/shard_map/ppermute | solution.py:65
  91.5 0.1 fusion.6
  91.6 3.8 %collective-permute-start.21 = (bf16[2,4,160,128]{3,2,1,0:T(8,128)(2,1)S(1)}, bf16[2,4,160,128]{3,2,1,0:T(8,128)(2,1)S(1)}, u32[]{:S(2)}, u32[]{:S(2)}) collective-permute-start(bf16[2,4,160,128]{3,2,1,0:T(8,128)(2,1)S(1)} %fusion.6), channel_id=1, source_target_pairs={{0,64},{32,96},{64,0},{96,32},{1,65},{33,97},{65,1},{97,33},{2,66}... | collective-permute-start | bytes 983048 | tf_op jit(solution)/shard_map/ppermute | solution.py:65
  95.5 0.1 add_convert_fusion.2
  95.7 0.1 add_convert_fusion
  95.8 2.7 %collective-permute-start.32 = (bf16[160,1024]{1,0:T(8,128)(2,1)S(1)}, bf16[160,1024]{1,0:T(8,128)(2,1)S(1)}, u32[]{:S(2)}, u32[]{:S(2)}) collective-permute-start(bf16[160,1024]{1,0:T(8,128)(2,1)S(1)} %add_convert_fusion), channel_id=1, source_target_pairs={{0,28},{1,29},{2,30},{3,31},{4,0},{5,1},{6,2},{7,3},{8,4},{9,5},{1... | collective-permute-start | bytes 983048 | tf_op jit(solution)/shard_map/ppermute | solution.py:51
  98.5 0.2 fusion.5
  98.7 3.8 %collective-permute-start.24 = (bf16[2,4,160,128]{3,2,1,0:T(8,128)(2,1)S(1)}, bf16[2,4,160,128]{3,2,1,0:T(8,128)(2,1)S(1)}, u32[]{:S(2)}, u32[]{:S(2)}) collective-permute-start(bf16[2,4,160,128]{3,2,1,0:T(8,128)(2,1)S(1)} %fusion.5), channel_id=1, source_target_pairs={{0,32},{32,0},{64,96},{96,64},{128,160},{160,128},{192,224},{224,1... | collective-permute-start | bytes 983048 | tf_op jit(solution)/shard_map/ppermute | solution.py:60
  102.5 1.2 %collective-permute-done.21.refs_4_ = bf16[2,4,160,128]{3,2,1,0:T(8,128)(2,1)S(1)} collective-permute-done((bf16[2,4,160,128]{3,2,1,0:T(8,128)(2,1)S(1)}, bf16[2,4,160,128]{3,2,1,0:T(8,128)(2,1)S(1)}, u32[]{:S(2)}, u32[]{:S(2)}) %collective-permute-start.21) | collective-permute-done | bytes 327712 | tf_op jit(solution)/shard_map/ppermute | solution.py:65
  103.7 0.2 fusion.2
  103.9 3.1 %collective-permute-start.23 = (bf16[2,4,160,128]{3,2,1,0:T(8,128)(2,1)S(1)}, bf16[2,4,160,128]{3,2,1,0:T(8,128)(2,1)S(1)}, u32[]{:S(2)}, u32[]{:S(2)}) collective-permute-start(bf16[2,4,160,128]{3,2,1,0:T(8,128)(2,1)S(1)} %fusion.2), channel_id=1, source_target_pairs={{0,32},{32,0},{64,96},{96,64},{128,160},{160,128},{192,224},{224,1... | collective-permute-start | bytes 983048 | tf_op jit(solution)/shard_map/ppermute | solution.py:60
  107.0 1.0 multiply_bitcast_fusion
  107.9 0.3 collective-permute-done.23.refs_6_
  108.2 3.2 %finish.1 = bf16[128,5120]{1,0:T(8,128)(2,1)} custom-call(bf16[2,4,160,128]{3,2,1,0:T(8,128)(2,1)S(1)} %collective-permute-done.16.refs_0_, bf16[2,4,160,128]{3,2,1,0:T(8,128)(2,1)S(1)} %collective-permute-done.18.refs_1_, bf16[2,4,160,128]{3,2,1,0:T(8,128)(2,1)S(1)} %collective-permute-done.19.refs_2_, ...), custom_call_target="tpu_custom_call" | custom-call | bytes 6291456 | tf_op jit(solution)/shard_map/finish/pallas_call | solution.py:361
  (78 shorter events, 1.0 us)
Async XLA Ops:
  2.4 24.2 %copy-start.17 = (f32[1,4]{1,0:T(1,128)S(1)}, f32[1,4]{1,0:T(1,128)}, u32[]{:S(2)}) copy-start(f32[1,4]{1,0:T(1,128)} %param.24) | copy-start | bytes 52
  2.4 24.9 %copy-start.18 = (s32[1,128]{1,0:T(1,128)S(1)}, s32[1,128]{1,0:T(1,128)}, u32[]{:S(2)}) copy-start(s32[1,128]{1,0:T(1,128)} %refs_1_) | copy-start | bytes 1540
  2.5 24.9 %copy-start.19 = (f32[128]{0:T(128)S(1)}, f32[128]{0:T(128)}, u32[]{:S(2)}) copy-start(f32[128]{0:T(128)} %param.22) | copy-start | bytes 1540
  2.5 24.9 %copy-start.20 = (f32[128]{0:T(128)S(1)}, f32[128]{0:T(128)}, u32[]{:S(2)}) copy-start(f32[128]{0:T(128)} %param.23) | copy-start | bytes 1540
  8.0 35.2 %copy-start.1 = (bf16[128,1024]{1,0:T(8,128)(2,1)S(1)}, bf16[128,1024]{1,0:T(8,128)(2,1)}, u32[]{:S(2)}) copy-start(bf16[128,1024]{1,0:T(8,128)(2,1)} %get-tuple-element.74.refs_7_.refs_1_.cots) | copy-start | bytes 786436
  8.0 27.2 %collective-permute-start.8 = (bf16[2944,128]{1,0:T(8,128)(2,1)}, bf16[2944,128]{1,0:T(8,128)(2,1)S(1)}, u32[]{:S(2)}, u32[]{:S(2)}) collective-permute-start(bf16[2944,128]{1,0:T(8,128)(2,1)} %get-tuple-element.57.refs_5_), channel_id=1, source_target_pairs={{0,1},{1,2},{2,3},{3,0},{4,5},{5,6},{6,7},{7,4},{8,9},{9,10},{10,1... | collective-permute-start | bytes 2261000 | tf_op jit(solution)/shard_map/ppermute | solution.py:56
  10.1 25.2 %collective-permute-start.9 = (bf16[2944,128]{1,0:T(8,128)(2,1)}, bf16[2944,128]{1,0:T(8,128)(2,1)S(1)}, u32[]{:S(2)}, u32[]{:S(2)}) collective-permute-start(bf16[2944,128]{1,0:T(8,128)(2,1)} %get-tuple-element.58.refs_6_), channel_id=1, source_target_pairs={{0,3},{1,0},{2,1},{3,2},{4,7},{5,4},{6,5},{7,6},{8,11},{9,8},{10,9... | collective-permute-start | bytes 2261000 | tf_op jit(solution)/shard_map/ppermute | solution.py:56
  11.5 12.5 %collective-permute-start = (bf16[160,1024]{1,0:T(8,128)(2,1)S(1)}, bf16[160,1024]{1,0:T(8,128)(2,1)S(1)}, u32[]{:S(2)}, u32[]{:S(2)}) collective-permute-start(bf16[160,1024]{1,0:T(8,128)(2,1)S(1)} %multiply_convert_fusion.refs_0_), channel_id=1, source_target_pairs={{0,4},{1,5},{2,6},{3,7},{4,8},{5,9},{6,10},{7,11},{8,12},{9,13},{1... | collective-permute-start | bytes 983048 | tf_op jit(solution)/shard_map/ppermute | solution.py:51
  13.2 10.7 %collective-permute-start.1 = (bf16[160,1024]{1,0:T(8,128)(2,1)S(1)}, bf16[160,1024]{1,0:T(8,128)(2,1)S(1)}, u32[]{:S(2)}, u32[]{:S(2)}) collective-permute-start(bf16[160,1024]{1,0:T(8,128)(2,1)S(1)} %multiply_convert_fusion.refs_0_), channel_id=1, source_target_pairs={{0,28},{1,29},{2,30},{3,31},{4,0},{5,1},{6,2},{7,3},{8,4},{9,5},{1... | collective-permute-start | bytes 983048 | tf_op jit(solution)/shard_map/ppermute | solution.py:51
  24.0 8.6 %collective-permute-start.2 = (bf16[160,1024]{1,0:T(8,128)(2,1)S(1)}, bf16[160,1024]{1,0:T(8,128)(2,1)S(1)}, u32[]{:S(2)}, u32[]{:S(2)}) collective-permute-start(bf16[160,1024]{1,0:T(8,128)(2,1)S(1)} %collective-permute-done.refs_2_), channel_id=1, source_target_pairs={{0,4},{1,5},{2,6},{3,7},{4,8},{5,9},{6,10},{7,11},{8,12},{9,13},{1... | collective-permute-start | bytes 983048 | tf_op jit(solution)/shard_map/ppermute | solution.py:51
  24.0 8.6 %collective-permute-start.3 = (bf16[160,1024]{1,0:T(8,128)(2,1)S(1)}, bf16[160,1024]{1,0:T(8,128)(2,1)S(1)}, u32[]{:S(2)}, u32[]{:S(2)}) collective-permute-start(bf16[160,1024]{1,0:T(8,128)(2,1)S(1)} %collective-permute-done.1.refs_1_), channel_id=1, source_target_pairs={{0,28},{1,29},{2,30},{3,31},{4,0},{5,1},{6,2},{7,3},{8,4},{9,5},{1... | collective-permute-start | bytes 983048 | tf_op jit(solution)/shard_map/ppermute | solution.py:51
  32.5 7.6 %collective-permute-start.4 = (bf16[160,1024]{1,0:T(8,128)(2,1)S(1)}, bf16[160,1024]{1,0:T(8,128)(2,1)S(1)}, u32[]{:S(2)}, u32[]{:S(2)}) collective-permute-start(bf16[160,1024]{1,0:T(8,128)(2,1)S(1)} %collective-permute-done.2.refs_4_), channel_id=1, source_target_pairs={{0,4},{1,5},{2,6},{3,7},{4,8},{5,9},{6,10},{7,11},{8,12},{9,13},{1... | collective-permute-start | bytes 983048 | tf_op jit(solution)/shard_map/ppermute | solution.py:51
  33.6 6.7 %collective-permute-start.6 = (bf16[160,1024]{1,0:T(8,128)(2,1)S(1)}, bf16[160,1024]{1,0:T(8,128)(2,1)S(1)}, u32[]{:S(2)}, u32[]{:S(2)}) collective-permute-start(bf16[160,1024]{1,0:T(8,128)(2,1)S(1)} %collective-permute-done.3.refs_3_), channel_id=1, source_target_pairs={{0,28},{1,29},{2,30},{3,31},{4,0},{5,1},{6,2},{7,3},{8,4},{9,5},{1... | collective-permute-start | bytes 983048 | tf_op jit(solution)/shard_map/ppermute | solution.py:51
  35.2 8.0 %collective-permute-start.10 = (bf16[1152,128]{1,0:T(8,128)(2,1)S(1)}, bf16[1152,128]{1,0:T(8,128)(2,1)S(1)}, u32[]{:S(2)}, u32[]{:S(2)}) collective-permute-start(bf16[1152,128]{1,0:T(8,128)(2,1)S(1)} %slice.82), channel_id=1, source_target_pairs={{0,1},{1,2},{2,3},{3,0},{4,5},{5,6},{6,7},{7,4},{8,9},{9,10},{10,1... | collective-permute-start | bytes 884744 | tf_op jit(solution)/shard_map/ppermute | solution.py:56
  35.4 7.8 %collective-permute-start.11 = (bf16[1152,128]{1,0:T(8,128)(2,1)S(1)}, bf16[1152,128]{1,0:T(8,128)(2,1)S(1)}, u32[]{:S(2)}, u32[]{:S(2)}) collective-permute-start(bf16[1152,128]{1,0:T(8,128)(2,1)S(1)} %slice.83), channel_id=1, source_target_pairs={{0,3},{1,0},{2,1},{3,2},{4,7},{5,4},{6,5},{7,6},{8,11},{9,8},{10,9... | collective-permute-start | bytes 884744 | tf_op jit(solution)/shard_map/ppermute | solution.py:56
  40.2 5.8 %collective-permute-start.5 = (bf16[80,1024]{1,0:T(8,128)(2,1)S(1)}, bf16[80,1024]{1,0:T(8,128)(2,1)S(1)}, u32[]{:S(2)}, u32[]{:S(2)}) collective-permute-start(bf16[80,1024]{1,0:T(8,128)(2,1)S(1)} %slice.80), channel_id=1, source_target_pairs={{0,4},{1,5},{2,6},{3,7},{4,8},{5,9},{6,10},{7,11},{8,12},{9,13},{1... | collective-permute-start | bytes 491528 | tf_op jit(solution)/shard_map/ppermute | solution.py:51
  40.3 5.6 %collective-permute-start.7 = (bf16[80,1024]{1,0:T(8,128)(2,1)S(1)}, bf16[80,1024]{1,0:T(8,128)(2,1)S(1)}, u32[]{:S(2)}, u32[]{:S(2)}) collective-permute-start(bf16[80,1024]{1,0:T(8,128)(2,1)S(1)} %slice.81), channel_id=1, source_target_pairs={{0,28},{1,29},{2,30},{3,31},{4,0},{5,1},{6,2},{7,3},{8,4},{9,5},{1... | collective-permute-start | bytes 491528 | tf_op jit(solution)/shard_map/ppermute | solution.py:51
  46.0 3.7 %copy-start.4 = (bf16[8,160,128]{2,1,0:T(8,128)(2,1)S(1)}, bf16[8,160,128]{2,1,0:T(8,128)(2,1)}, u32[]{:S(2)}) copy-start(bf16[8,160,128]{2,1,0:T(8,128)(2,1)} %get-tuple-element.67.refs_4_.near) | copy-start | bytes 983044
  47.4 8.1 %collective-permute-start.12 = (bf16[8,160,128]{2,1,0:T(8,128)(2,1)S(1)}, bf16[8,160,128]{2,1,0:T(8,128)(2,1)S(1)}, u32[]{:S(2)}, u32[]{:S(2)}) collective-permute-start(bf16[8,160,128]{2,1,0:T(8,128)(2,1)S(1)} %get-tuple-element.64), channel_id=1, source_target_pairs={{0,3},{1,0},{2,1},{3,2},{4,7},{5,4},{6,5},{7,6},{8,11},{9,8},{10,9... | collective-permute-start | bytes 983048 | tf_op jit(solution)/shard_map/ppermute | solution.py:56
  49.0 11.0 %collective-permute-start.13 = (bf16[8,160,128]{2,1,0:T(8,128)(2,1)}, bf16[8,160,128]{2,1,0:T(8,128)(2,1)S(1)}, u32[]{:S(2)}, u32[]{:S(2)}) collective-permute-start(bf16[8,160,128]{2,1,0:T(8,128)(2,1)} %get-tuple-element.65), channel_id=1, source_target_pairs={{0,2},{1,3},{2,0},{3,1},{4,6},{5,7},{6,4},{7,5},{8,10},{9,11},{10,... | collective-permute-start | bytes 983048 | tf_op jit(solution)/shard_map/ppermute | solution.py:56
  49.1 15.4 %collective-permute-start.14 = (bf16[8,160,128]{2,1,0:T(8,128)(2,1)}, bf16[8,160,128]{2,1,0:T(8,128)(2,1)S(1)}, u32[]{:S(2)}, u32[]{:S(2)}) collective-permute-start(bf16[8,160,128]{2,1,0:T(8,128)(2,1)} %get-tuple-element.66), channel_id=1, source_target_pairs={{0,1},{1,2},{2,3},{3,0},{4,5},{5,6},{6,7},{7,4},{8,9},{9,10},{10,1... | collective-permute-start | bytes 983048 | tf_op jit(solution)/shard_map/ppermute | solution.py:56
  49.7 14.8 %copy-start.3 = (bf16[2944,128]{1,0:T(8,128)(2,1)S(1)}, bf16[2944,128]{1,0:T(8,128)(2,1)}, u32[]{:S(2)}) copy-start(bf16[2944,128]{1,0:T(8,128)(2,1)} %get-tuple-element.58.refs_6_) | copy-start | bytes 2260996
  51.3 0.7 copy-start.9
  52.1 0.8 copy-start.11
  52.8 0.7 copy-start.13
  53.5 0.7 copy-start.15
  54.3 1.9 %copy-start.5 = (bf16[160,1024]{1,0:T(8,128)(2,1)}, bf16[160,1024]{1,0:T(8,128)(2,1)S(1)}, u32[]{:S(2)}) copy-start(bf16[160,1024]{1,0:T(8,128)(2,1)S(1)} %get-tuple-element.90) | copy-start | bytes 983044
  54.3 1.9 %copy-start.7 = (bf16[160,1024]{1,0:T(8,128)(2,1)}, bf16[160,1024]{1,0:T(8,128)(2,1)S(1)}, u32[]{:S(2)}) copy-start(bf16[160,1024]{1,0:T(8,128)(2,1)S(1)} %get-tuple-element.87) | copy-start | bytes 983044
  54.3 10.2 %copy-start.2 = (bf16[2944,128]{1,0:T(8,128)(2,1)S(1)}, bf16[2944,128]{1,0:T(8,128)(2,1)}, u32[]{:S(2)}) copy-start(bf16[2944,128]{1,0:T(8,128)(2,1)} %get-tuple-element.57.refs_5_) | copy-start | bytes 2260996
  56.2 13.9 %collective-permute-start.25 = (bf16[80,1024]{1,0:T(8,128)(2,1)}, bf16[80,1024]{1,0:T(8,128)(2,1)}, u32[]{:S(2)}, u32[]{:S(2)}) collective-permute-start(bf16[80,1024]{1,0:T(8,128)(2,1)} %get-tuple-element.97), channel_id=1, source_target_pairs={{0,4},{1,5},{2,6},{3,7},{4,8},{5,9},{6,10},{7,11},{8,12},{9,13},{1... | collective-permute-start | bytes 491528 | tf_op jit(solution)/shard_map/ppermute | solution.py:51
  58.9 12.3 %collective-permute-start.29 = (bf16[80,1024]{1,0:T(8,128)(2,1)}, bf16[80,1024]{1,0:T(8,128)(2,1)S(1)}, u32[]{:S(2)}, u32[]{:S(2)}) collective-permute-start(bf16[80,1024]{1,0:T(8,128)(2,1)} %get-tuple-element.98), channel_id=1, source_target_pairs={{0,28},{1,29},{2,30},{3,31},{4,0},{5,1},{6,2},{7,3},{8,4},{9,5},{1... | collective-permute-start | bytes 491528 | tf_op jit(solution)/shard_map/ppermute | solution.py:51
  59.9 10.2 %copy-start.6 = (bf16[160,1024]{1,0:T(8,128)(2,1)S(1)}, bf16[160,1024]{1,0:T(8,128)(2,1)}, u32[]{:S(2)}) copy-start(bf16[160,1024]{1,0:T(8,128)(2,1)} %copy-done.5) | copy-start | bytes 983044
  65.4 8.6 %collective-permute-start.17 = (bf16[2,4,160,128]{3,2,1,0:T(8,128)(2,1)S(1)}, bf16[2,4,160,128]{3,2,1,0:T(8,128)(2,1)S(1)}, u32[]{:S(2)}, u32[]{:S(2)}) collective-permute-start(bf16[2,4,160,128]{3,2,1,0:T(8,128)(2,1)S(1)} %get-tuple-element.71.refs_5_), channel_id=1, source_target_pairs={{0,32},{32,0},{64,96},{96,64},{128,160},{160,128},{192,224},{224,1... | collective-permute-start | bytes 983048 | tf_op jit(solution)/shard_map/ppermute | solution.py:60
  70.0 6.1 %collective-permute-start.15 = (bf16[2,4,160,128]{3,2,1,0:T(8,128)(2,1)S(1)}, bf16[2,4,160,128]{3,2,1,0:T(8,128)(2,1)S(1)}, u32[]{:S(2)}, u32[]{:S(2)}) collective-permute-start(bf16[2,4,160,128]{3,2,1,0:T(8,128)(2,1)S(1)} %get-tuple-element.69.refs_4_), channel_id=1, source_target_pairs={{0,32},{32,0},{64,96},{96,64},{128,160},{160,128},{192,224},{224,1... | collective-permute-start | bytes 983048 | tf_op jit(solution)/shard_map/ppermute | solution.py:60
  71.1 9.1 %collective-permute-start.26 = (bf16[160,1024]{1,0:T(8,128)(2,1)S(1)}, bf16[160,1024]{1,0:T(8,128)(2,1)S(1)}, u32[]{:S(2)}, u32[]{:S(2)}) collective-permute-start(bf16[160,1024]{1,0:T(8,128)(2,1)S(1)} %pad_maximum_fusion.1), channel_id=1, source_target_pairs={{0,4},{1,5},{2,6},{3,7},{4,8},{5,9},{6,10},{7,11},{8,12},{9,13},{1... | collective-permute-start | bytes 983048 | tf_op jit(solution)/shard_map/ppermute | solution.py:51
  71.3 6.3 %copy-start = (bf16[128,5120]{1,0:T(8,128)(2,1)S(1)}, bf16[128,5120]{1,0:T(8,128)(2,1)}, u32[]{:S(2)}) copy-start(bf16[128,5120]{1,0:T(8,128)(2,1)} %refs_6_.1) | copy-start | bytes 3932164
  71.3 9.9 %collective-permute-start.30 = (bf16[160,1024]{1,0:T(8,128)(2,1)S(1)}, bf16[160,1024]{1,0:T(8,128)(2,1)S(1)}, u32[]{:S(2)}, u32[]{:S(2)}) collective-permute-start(bf16[160,1024]{1,0:T(8,128)(2,1)S(1)} %pad_maximum_fusion.2), channel_id=1, source_target_pairs={{0,28},{1,29},{2,30},{3,31},{4,0},{5,1},{6,2},{7,3},{8,4},{9,5},{1... | collective-permute-start | bytes 983048 | tf_op jit(solution)/shard_map/ppermute | solution.py:51
  74.1 10.3 %collective-permute-start.18 = (bf16[2,4,160,128]{3,2,1,0:T(8,128)(2,1)S(1)}, bf16[2,4,160,128]{3,2,1,0:T(8,128)(2,1)S(1)}, u32[]{:S(2)}, u32[]{:S(2)}) collective-permute-start(bf16[2,4,160,128]{3,2,1,0:T(8,128)(2,1)S(1)} %fusion.3), channel_id=1, source_target_pairs={{192,0},{224,32},{193,1},{225,33},{194,2},{226,34},{195,3},{227,35... | collective-permute-start | bytes 983048 | tf_op jit(solution)/shard_map/ppermute | solution.py:65
  75.4 9.3 %collective-permute-start.20 = (bf16[2,4,160,128]{3,2,1,0:T(8,128)(2,1)S(1)}, bf16[2,4,160,128]{3,2,1,0:T(8,128)(2,1)S(1)}, u32[]{:S(2)}, u32[]{:S(2)}) collective-permute-start(bf16[2,4,160,128]{3,2,1,0:T(8,128)(2,1)S(1)} %fusion.3), channel_id=1, source_target_pairs={{192,128},{224,160},{128,64},{160,96},{193,129},{225,161},{129,65}... | collective-permute-start | bytes 983048 | tf_op jit(solution)/shard_map/ppermute | solution.py:65
  76.2 15.2 %collective-permute-start.16 = (bf16[2,4,160,128]{3,2,1,0:T(8,128)(2,1)S(1)}, bf16[2,4,160,128]{3,2,1,0:T(8,128)(2,1)S(1)}, u32[]{:S(2)}, u32[]{:S(2)}) collective-permute-start(bf16[2,4,160,128]{3,2,1,0:T(8,128)(2,1)S(1)} %fusion), channel_id=1, source_target_pairs={{192,0},{224,32},{193,1},{225,33},{194,2},{226,34},{195,3},{227,35... | collective-permute-start | bytes 983048 | tf_op jit(solution)/shard_map/ppermute | solution.py:65
  77.5 3.5 %copy-start.16 = (bf16[160,1024]{1,0:T(8,128)(2,1)S(1)}, bf16[160,1024]{1,0:T(8,128)(2,1)}, u32[]{:S(2)}) copy-start(bf16[160,1024]{1,0:T(8,128)(2,1)} %copy-done.15) | copy-start | bytes 983044
  77.5 3.7 %copy-start.14 = (bf16[160,1024]{1,0:T(8,128)(2,1)S(1)}, bf16[160,1024]{1,0:T(8,128)(2,1)}, u32[]{:S(2)}) copy-start(bf16[160,1024]{1,0:T(8,128)(2,1)} %copy-done.13) | copy-start | bytes 983044
  80.2 11.3 %collective-permute-start.19 = (bf16[2,4,160,128]{3,2,1,0:T(8,128)(2,1)S(1)}, bf16[2,4,160,128]{3,2,1,0:T(8,128)(2,1)S(1)}, u32[]{:S(2)}, u32[]{:S(2)}) collective-permute-start(bf16[2,4,160,128]{3,2,1,0:T(8,128)(2,1)S(1)} %fusion), channel_id=1, source_target_pairs={{192,128},{224,160},{128,64},{160,96},{193,129},{225,161},{129,65}... | collective-permute-start | bytes 983048 | tf_op jit(solution)/shard_map/ppermute | solution.py:65
  81.2 14.2 %collective-permute-start.27 = (bf16[160,1024]{1,0:T(8,128)(2,1)S(1)}, bf16[160,1024]{1,0:T(8,128)(2,1)S(1)}, u32[]{:S(2)}, u32[]{:S(2)}) collective-permute-start(bf16[160,1024]{1,0:T(8,128)(2,1)S(1)} %add_convert_fusion.3), channel_id=1, source_target_pairs={{0,4},{1,5},{2,6},{3,7},{4,8},{5,9},{6,10},{7,11},{8,12},{9,13},{1... | collective-permute-start | bytes 983048 | tf_op jit(solution)/shard_map/ppermute | solution.py:51
  81.4 14.0 %copy-start.12 = (bf16[160,1024]{1,0:T(8,128)(2,1)S(1)}, bf16[160,1024]{1,0:T(8,128)(2,1)}, u32[]{:S(2)}) copy-start(bf16[160,1024]{1,0:T(8,128)(2,1)} %copy-done.11) | copy-start | bytes 983044
  84.4 11.2 %collective-permute-start.31 = (bf16[160,1024]{1,0:T(8,128)(2,1)S(1)}, bf16[160,1024]{1,0:T(8,128)(2,1)S(1)}, u32[]{:S(2)}, u32[]{:S(2)}) collective-permute-start(bf16[160,1024]{1,0:T(8,128)(2,1)S(1)} %add_convert_fusion.1), channel_id=1, source_target_pairs={{0,28},{1,29},{2,30},{3,31},{4,0},{5,1},{6,2},{7,3},{8,4},{9,5},{1... | collective-permute-start | bytes 983048 | tf_op jit(solution)/shard_map/ppermute | solution.py:51
  84.8 10.8 %copy-start.10 = (bf16[160,1024]{1,0:T(8,128)(2,1)S(1)}, bf16[160,1024]{1,0:T(8,128)(2,1)}, u32[]{:S(2)}) copy-start(bf16[160,1024]{1,0:T(8,128)(2,1)} %copy-done.9) | copy-start | bytes 983044
  84.8 13.7 %collective-permute-start.22 = (bf16[2,4,160,128]{3,2,1,0:T(8,128)(2,1)S(1)}, bf16[2,4,160,128]{3,2,1,0:T(8,128)(2,1)S(1)}, u32[]{:S(2)}, u32[]{:S(2)}) collective-permute-start(bf16[2,4,160,128]{3,2,1,0:T(8,128)(2,1)S(1)} %fusion.7), channel_id=1, source_target_pairs={{0,64},{32,96},{64,0},{96,32},{1,65},{33,97},{65,1},{97,33},{2,66}... | collective-permute-start | bytes 983048 | tf_op jit(solution)/shard_map/ppermute | solution.py:65
  91.6 12.1 %collective-permute-start.21 = (bf16[2,4,160,128]{3,2,1,0:T(8,128)(2,1)S(1)}, bf16[2,4,160,128]{3,2,1,0:T(8,128)(2,1)S(1)}, u32[]{:S(2)}, u32[]{:S(2)}) collective-permute-start(bf16[2,4,160,128]{3,2,1,0:T(8,128)(2,1)S(1)} %fusion.6), channel_id=1, source_target_pairs={{0,64},{32,96},{64,0},{96,32},{1,65},{33,97},{65,1},{97,33},{2,66}... | collective-permute-start | bytes 983048 | tf_op jit(solution)/shard_map/ppermute | solution.py:65
  95.6 11.4 %collective-permute-start.28 = (bf16[160,1024]{1,0:T(8,128)(2,1)S(1)}, bf16[160,1024]{1,0:T(8,128)(2,1)S(1)}, u32[]{:S(2)}, u32[]{:S(2)}) collective-permute-start(bf16[160,1024]{1,0:T(8,128)(2,1)S(1)} %add_convert_fusion.2), channel_id=1, source_target_pairs={{0,4},{1,5},{2,6},{3,7},{4,8},{5,9},{6,10},{7,11},{8,12},{9,13},{1... | collective-permute-start | bytes 983048 | tf_op jit(solution)/shard_map/ppermute | solution.py:51
  95.8 11.2 %copy-start.8 = (bf16[160,1024]{1,0:T(8,128)(2,1)S(1)}, bf16[160,1024]{1,0:T(8,128)(2,1)}, u32[]{:S(2)}) copy-start(bf16[160,1024]{1,0:T(8,128)(2,1)} %copy-done.7) | copy-start | bytes 983044
  95.8 11.2 %collective-permute-start.32 = (bf16[160,1024]{1,0:T(8,128)(2,1)S(1)}, bf16[160,1024]{1,0:T(8,128)(2,1)S(1)}, u32[]{:S(2)}, u32[]{:S(2)}) collective-permute-start(bf16[160,1024]{1,0:T(8,128)(2,1)S(1)} %add_convert_fusion), channel_id=1, source_target_pairs={{0,28},{1,29},{2,30},{3,31},{4,0},{5,1},{6,2},{7,3},{8,4},{9,5},{1... | collective-permute-start | bytes 983048 | tf_op jit(solution)/shard_map/ppermute | solution.py:51
  98.7 9.2 %collective-permute-start.24 = (bf16[2,4,160,128]{3,2,1,0:T(8,128)(2,1)S(1)}, bf16[2,4,160,128]{3,2,1,0:T(8,128)(2,1)S(1)}, u32[]{:S(2)}, u32[]{:S(2)}) collective-permute-start(bf16[2,4,160,128]{3,2,1,0:T(8,128)(2,1)S(1)} %fusion.5), channel_id=1, source_target_pairs={{0,32},{32,0},{64,96},{96,64},{128,160},{160,128},{192,224},{224,1... | collective-permute-start | bytes 983048 | tf_op jit(solution)/shard_map/ppermute | solution.py:60
  103.9 4.3 %collective-permute-start.23 = (bf16[2,4,160,128]{3,2,1,0:T(8,128)(2,1)S(1)}, bf16[2,4,160,128]{3,2,1,0:T(8,128)(2,1)S(1)}, u32[]{:S(2)}, u32[]{:S(2)}) collective-permute-start(bf16[2,4,160,128]{3,2,1,0:T(8,128)(2,1)S(1)} %fusion.2), channel_id=1, source_target_pairs={{0,32},{32,0},{64,96},{96,64},{128,160},{160,128},{192,224},{224,1... | collective-permute-start | bytes 983048 | tf_op jit(solution)/shard_map/ppermute | solution.py:60

commit v3 on v2

--- a/solution.py
+++ b/solution.py
@@ -19,13 +19,16 @@
 NY = 4
 SLAB = D // (NZ * NX)
 EPSILON = 1e-06
-VMEM = pltpu.CompilerParams(vmem_limit_bytes=48 * 1024 * 1024)
+VMEM = pltpu.CompilerParams(vmem_limit_bytes=16 * 1024 * 1024)
 MOST_VMEM = pltpu.CompilerParams(vmem_limit_bytes=57 * 1024 * 1024)
 NT = (((1,), (1,)), ((), ()))
 
 Z_ORDER = (0, 1, 7, 2, 6, 3, 5, 4)
+HALVED = (3, 4, 5)
+TERM_ROWS = [SLAB] * 3 + [SLAB // 2] * 6 + [SLAB] * 2
 COTS = 2 * KVW // 128
-RELAY = NZ * SLAB
+STREAM = NZ * SLAB
+RELAY = STREAM
 RELAYED = NZ // 2 * SLAB + COTS // 2 * ROWS
 SENT = RELAY + RELAYED + COTS // 2 * ROWS
 
@@ -82,14 +85,23 @@
 
 
 def attend_kernel(*refs):
-    sources, (out_ref, near_ref, up_ref, down_ref) = refs[:6], refs[6:10]
-    targets, held, sems = refs[10:16], refs[16], refs[17]
-    copies = start_copies(sources, targets, sems)
-    h_ref, row_ref, k_ref, v_ref, q_ref, o_ref = targets
+    (h_hbm, row_hbm, k_hbm, v_hbm, q_hbm, o_hbm), (cots_out, near_out, up_out, down_out) = refs[:6], refs[6:10]
+    h_ref, row_ref, k_ref, v_ref, q_ref, o_ref, held, tiles, in_sems, out_sems = refs[10:]
+    pieces = [
+        (hbm.at[:, first : first + wide], ref.at[:, first : first + wide])
+        for hbm, ref, wide in ((h_hbm, h_ref, D // 4),)
+        for first in range(0, D, wide)
+    ]
+    pieces += [(row_hbm, row_ref), (k_hbm, k_ref), (v_hbm, v_ref)]
+    for g in range(KVH):
+        span = slice(g * GROUP * HD, (g + 1) * GROUP * HD)
+        pieces += [(q_hbm.at[:, span], q_ref.at[:, span]), (o_hbm.at[:, span], o_ref.at[:, span])]
+    copies = start_copies([pair[0] for pair in pieces], [pair[1] for pair in pieces], in_sems)
     z, x, _, _ = place()
-    copies[0].wait()
     squares = jnp.zeros((ROWS, 128), jnp.float32)
     for tile in range(D // 128):
+        if tile % 10 == 0:
+            copies[tile // 10].wait()
         part = h_ref[:, tile * 128 : (tile + 1) * 128]
         turned = part.T
         part = part.astype(jnp.float32)
@@ -99,15 +111,22 @@
             slab, fifth = unit // 5, unit % 5
             k = lax.rem(slab // NX - z + NZ, NZ)
             d = lax.rem(slab % NX - x + NX, NX)
-            held[d, k, fifth * 32 : (fifth + 1) * 32, :] = turned[piece * 32 : (piece + 1) * 32, :]
-    near_ref[...] = held[0]
-    for ref, d, first in ((up_ref, 1, 0), (down_ref, 3, NZ // 2)):
-        for k in range(NZ):
-            ref[k * SLAB : (k + 1) * SLAB, :] = held[d, k]
-        for k in range(NZ // 2):
-            ref[RELAY + k * SLAB : RELAY + (k + 1) * SLAB, :] = held[2, first + k]
+            first = pl.multiple_of(k * SLAB + fifth * 32, 32)
+            held[d, pl.ds(first, 32), :] = turned[piece * 32 : (piece + 1) * 32, :]
+    middle = STREAM // 2
+    sent = start_copies(
+        [held.at[0], held.at[1], held.at[2, :middle], held.at[3], held.at[2, middle:]],
+        [
+            near_out,
+            up_out.at[:STREAM],
+            up_out.at[STREAM : STREAM + middle],
+            down_out.at[:STREAM],
+            down_out.at[STREAM : STREAM + middle],
+        ],
+        out_sems,
+    )
     inv_rms = lax.rsqrt(jnp.sum(squares, axis=1, keepdims=True) * (1.0 / D) + EPSILON)
-    for copy in copies[1:]:
+    for copy in copies[4:7]:
         copy.wait()
     j_place = lax.broadcasted_iota(jnp.int32, (ROWS, ROWS), 0)
     i_place = lax.broadcasted_iota(jnp.int32, (ROWS, ROWS), 1)
@@ -115,6 +134,8 @@
     allowed = (segment.T == segment) & (j_place <= i_place)
     scale = 1.0 / math.sqrt(HD)
     for g in range(KVH):
+        for copy in copies[7 + 2 * g : 9 + 2 * g]:
+            copy.wait()
         key = k_ref[:, g * HD : (g + 1) * HD]
         value = v_ref[:, g * HD : (g + 1) * HD]
         heads = range(g * GROUP, (g + 1) * GROUP)
@@ -139,27 +160,31 @@
         key_cot = (key_cot * scale).astype(jnp.bfloat16).astype(jnp.float32)
         value_cot = value_cot.astype(jnp.bfloat16).astype(jnp.float32)
         for index, value in ((g, key_cot), (KVH + g, value_cot)):
-            scaled = (value * inv_rms).astype(jnp.bfloat16)
-            out_ref[:, index * HD : (index + 1) * HD] = scaled
-            for ref, turn in ((up_ref, 0), (down_ref, KVH)):
-                first = SENT - COTS * ROWS + (index + turn) % COTS * ROWS
-                ref[first : first + ROWS, :] = scaled
+            tiles[index * ROWS : (index + 1) * ROWS, :] = (value * inv_rms).astype(jnp.bfloat16)
+    part, lead = COTS // 2 * ROWS, STREAM + STREAM // 2
+    sent += start_copies(
+        [tiles, tiles, tiles.at[part:], tiles.at[:part]],
+        [cots_out, up_out.at[lead:], down_out.at[lead : lead + part], down_out.at[lead + part :]],
+        out_sems.at[5:],
+    )
+    for copy in sent:
+        copy.wait()
 
 
 def attend(hidden, row, keys, values, queries, cotangent):
     operands = (hidden, row, keys, values, queries, cotangent)
     return pl.pallas_call(
         attend_kernel,
-        out_shape=[
-            shape_of((ROWS, 2 * KVW)),
-            shape_of((NZ, SLAB, ROWS)),
-            shape_of((SENT, ROWS)),
-            shape_of((SENT, ROWS)),
+        out_shape=[shape_of((COTS * ROWS, ROWS)), shape_of((STREAM, ROWS)), shape_of((SENT, ROWS)), shape_of((SENT, ROWS))],
+        in_specs=[pl.BlockSpec(memory_space=pl.ANY)] * 6,
+        out_specs=[pl.BlockSpec(memory_space=pl.ANY)] * 4,
+        scratch_shapes=[pltpu.VMEM(a.shape, a.dtype) for a in operands]
+        + [
+            pltpu.VMEM((NX, STREAM, ROWS), jnp.bfloat16),
+            pltpu.VMEM((COTS * ROWS, ROWS), jnp.bfloat16),
+            pltpu.SemaphoreType.DMA((15,)),
+            pltpu.SemaphoreType.DMA((9,)),
         ],
-        in_specs=[pl.BlockSpec(memory_space=pl.ANY)] * 6,
-        out_specs=whole(4),
-        scratch_shapes=[pltpu.VMEM(a.shape, a.dtype) for a in operands]
-        + [pltpu.VMEM((NX, NZ, SLAB, ROWS), jnp.bfloat16), pltpu.SemaphoreType.DMA((6,))],
         compiler_params=MOST_VMEM,
         cost_estimate=cost(4 * 32 * 2 * 128**3, 4 * 2**20, 32 * 128 * 128),
         name="attend",
@@ -167,10 +192,10 @@
 
 
 def join_cots(cots, up, down, far_up, far_down, right):
-    right[:ROWS] = cots[...]
     lead, far = SENT - COTS * ROWS, RELAYED - COTS // 2 * ROWS
     for tile in range(COTS):
         span = slice(tile * 128, (tile + 1) * 128)
+        right[:ROWS, span] = cots[tile * ROWS : (tile + 1) * ROWS]
         first = lead + tile * ROWS
         right[ROWS : 2 * ROWS, span] = up[first : first + ROWS]
         source, first = (far_up, far + tile * ROWS) if tile < COTS // 2 else (far_down, far + (tile - COTS // 2) * ROWS)
@@ -180,26 +205,33 @@
 
 
 def grad_kernel(near, cots, up, down, far_up, far_down, *refs):
-    outs, left, right = refs[:NZ], refs[NZ], refs[NZ + 1]
+    outs, (left, right) = refs[:-2], refs[-2:]
     join_cots(cots, up, down, far_up, far_down, right)
     middle = NZ // 2 * SLAB
-    left[:, :ROWS] = near[...].reshape(NZ * SLAB, ROWS)
+    left[:, :ROWS] = near[...]
     left[:, ROWS : 2 * ROWS] = up[: NZ * SLAB]
     left[:middle, 2 * ROWS : 3 * ROWS] = far_up[:middle]
     left[middle:, 2 * ROWS : 3 * ROWS] = far_down[:middle]
     left[:, 3 * ROWS :] = down[: NZ * SLAB]
+    place_k, half = 0, SLAB // 2
     for k in range(NZ):
-        outs[k][...] = jnp.dot(
+        term = jnp.dot(
             left[k * SLAB : (k + 1) * SLAB], right[...], preferred_element_type=jnp.float32
         ).astype(jnp.bfloat16)
+        if k in HALVED:
+            outs[place_k][...] = term[:half]
+            outs[place_k + 1][...] = term[half:]
+        else:
+            outs[place_k][...] = term
+        place_k += 2 if k in HALVED else 1
 
 
 def weight_terms(near, met):
     return pl.pallas_call(
         grad_kernel,
-        out_shape=[shape_of((SLAB, 2 * KVW))] * NZ,
+        out_shape=[shape_of((rows, 2 * KVW)) for rows in TERM_ROWS],
         in_specs=whole(6),
-        out_specs=whole(NZ),
+        out_specs=whole(len(TERM_ROWS)),
         scratch_shapes=[
             pltpu.VMEM((NZ * SLAB, NX * ROWS), jnp.bfloat16),
             pltpu.VMEM((NX * ROWS, 2 * KVW), jnp.bfloat16),
@@ -210,31 +242,26 @@
     )(near, *met)
 
 
-def back_kernel(count, past, *refs):
-    weights, cots = refs[:count], refs[count : count + 5]
-    earlier, outs, right = refs[count + 5 : -1 - NX], refs[-1 - NX : -1], refs[-1]
+def back_kernel(*refs):
+    weights, cots, outs, right = refs[:NZ], refs[NZ : NZ + 5], refs[NZ + 5 : -1], refs[-1]
     join_cots(*cots, right)
-    for d, ref in enumerate(earlier):
-        outs[d][:past] = ref[...]
-    for place_k, weight in enumerate(weights, past):
+    for place_k, weight in enumerate(weights):
         full = lax.dot_general(weight[...], right[...], NT, preferred_element_type=jnp.float32)
         for d in range(NX):
             outs[d][place_k] = full[:, d * ROWS : (d + 1) * ROWS].astype(jnp.bfloat16)
 
 
-def back(weights, cots, earlier=()):
-    count = len(weights)
-    past = earlier[0].shape[0] if earlier else 0
+def back(weights, cots):
     return pl.pallas_call(
-        functools.partial(back_kernel, count, past),
-        out_shape=[shape_of((past + count, SLAB, ROWS))] * NX,
-        in_specs=whole(count + 5 + len(earlier)),
+        back_kernel,
+        out_shape=[shape_of((NZ, SLAB, ROWS))] * NX,
+        in_specs=whole(NZ + 5),
         out_specs=whole(NX),
         scratch_shapes=[pltpu.VMEM((NX * ROWS, 2 * KVW), jnp.bfloat16)],
         compiler_params=VMEM,
-        cost_estimate=cost(2 * 512 * 160 * count * 1024, 2**20 * 3),
+        cost_estimate=cost(2 * 512 * 1280 * 1024, 2**20 * 5),
         name="back",
-    )(*weights, *cots, *earlier)
+    )(*weights, *cots)
 
 
 def local_kernel(*refs):
@@ -243,7 +270,7 @@
 
     def stream_of(d, k):
         if d == 0:
-            part = near[k]
+            part = near[k * SLAB : (k + 1) * SLAB]
         else:
             source = (None, up, up if k < NZ // 2 else down, down)[d]
             first = RELAY + k % (NZ // 2) * SLAB if d == 2 else k * SLAB
@@ -320,7 +347,7 @@
         span = slice(tile * 128, (tile + 1) * 128)
         first = pl.multiple_of(step * FINISH_WIDE + tile * 128, 128)
         top = coefficient * top_ref[:, span].astype(jnp.float32)
-        out_ref[:, span] = top + total[pl.ds(first, 128), :].T
+        out_ref[:, pl.ds(first, 128)] = top + total[pl.ds(first, 128), :].T
 
 
 def base_terms(mine, met, other, top, coefficient):
@@ -329,7 +356,7 @@
         grid=(FINISH_STEPS,),
         out_shape=shape_of((ROWS, D), jnp.float32),
         in_specs=whole(6) + [pl.BlockSpec((ROWS, FINISH_WIDE), lambda step: (0, step))] + whole(1),
-        out_specs=pl.BlockSpec((ROWS, FINISH_WIDE), lambda step: (0, step)),
+        out_specs=pl.BlockSpec(memory_space=pltpu.VMEM),
         scratch_shapes=[pltpu.VMEM((D, ROWS), jnp.float32), pltpu.VMEM((ROWS, ROWS), jnp.float32)],
         compiler_params=VMEM,
         cost_estimate=cost(0, 8 * 2**20),
@@ -339,32 +366,38 @@
 
 def finish_kernel(*refs):
     wrap, down, swap, back_in = refs[:2], refs[2:4], refs[4:6], refs[6:8]
-    base_ref, out_ref, total = refs[8:]
+    base_ref, out_hbm, total, out_ref, sems = refs[8:]
     _, _, _, core = place()
-    step = pl.program_id(0)
 
     def upper_of(a, d):
-        return part_of(wrap, a, d) + (part_of(down, a, d) + part_of(swap, a, d))
-
-    @pl.when(step == 0)
-    def _():
-        spread(total, core, upper_of)
-        spread(total, 1 - core, functools.partial(part_of, back_in))
-
-    for tile in range(FINISH_WIDE // 128):
-        span = slice(tile * 128, (tile + 1) * 128)
-        first = pl.multiple_of(step * FINISH_WIDE + tile * 128, 128)
-        out_ref[:, span] = (base_ref[:, span] + total[pl.ds(first, 128), :].T).astype(jnp.bfloat16)
+        upper = part_of(wrap, a, d) + (part_of(down, a, d) + part_of(swap, a, d))
+        return upper.astype(jnp.bfloat16)
+
+    spread(total, core, upper_of)
+    spread(total, 1 - core, lambda a, d: back_in[a // 2][a % 2, d])
+    copies = []
+    for step in range(FINISH_STEPS):
+        for tile in range(step * FINISH_WIDE // 128, (step + 1) * FINISH_WIDE // 128):
+            span = slice(tile * 128, (tile + 1) * 128)
+            turned = total[span, :].T.astype(jnp.float32)
+            out_ref[:, span] = (base_ref[:, span] + turned).astype(jnp.bfloat16)
+        wide = slice(step * FINISH_WIDE, (step + 1) * FINISH_WIDE)
+        copies += start_copies([out_ref.at[:, wide]], [out_hbm.at[:, wide]], sems.at[step:])
+    for copy in copies:
+        copy.wait()
 
 
 def finish(wrap, down, swap, back_in, base):
     return pl.pallas_call(
         finish_kernel,
-        grid=(FINISH_STEPS,),
         out_shape=shape_of((ROWS, D)),
-        in_specs=whole(8) + [pl.BlockSpec((ROWS, FINISH_WIDE), lambda step: (0, step))],
-        out_specs=pl.BlockSpec((ROWS, FINISH_WIDE), lambda step: (0, step)),
-        scratch_shapes=[pltpu.VMEM((D, ROWS), jnp.float32)],
+        in_specs=whole(9),
+        out_specs=pl.BlockSpec(memory_space=pl.ANY),
+        scratch_shapes=[
+            pltpu.VMEM((D, ROWS), jnp.bfloat16),
+            pltpu.VMEM((ROWS, D), jnp.bfloat16),
+            pltpu.SemaphoreType.DMA((FINISH_STEPS,)),
+        ],
         compiler_params=VMEM,
         cost_estimate=cost(0, 6 * 2**20),
         name="finish",
@@ -372,20 +405,20 @@
 
 
 def scatter_z(terms):
-    half = SLAB // 2
     wide = jnp.float32
 
     def add(first, second):
         return (first.astype(wide) + second.astype(wide)).astype(jnp.bfloat16)
 
-    far_up, far_down = shift_z(terms[4][:half], 1), shift_z(terms[4][half:], -1)
-    up = jnp.concatenate([add(terms[3][:half], far_up), terms[3][half:]], axis=0)
-    down = jnp.concatenate([terms[5][:half], add(terms[5][half:], far_down)], axis=0)
+    own, next_up, after_up, low_3, high_3, low_4, high_4, low_5, high_5, after_down, next_down = terms
+    far_up, far_down = shift_z(low_4, 1), shift_z(high_4, -1)
+    up = jnp.concatenate([add(low_3, far_up), high_3], axis=0)
+    down = jnp.concatenate([low_5, add(high_5, far_down)], axis=0)
     up, down = shift_z(up, 1), shift_z(down, -1)
-    up, down = add(terms[2], up), add(terms[6], down)
+    up, down = add(after_up, up), add(after_down, down)
     up, down = shift_z(up, 1), shift_z(down, -1)
-    up, down = add(terms[1], up), add(terms[7], down)
-    return terms[0], shift_z(up, 1), shift_z(down, -1)
+    up, down = add(next_up, up), add(next_down, down)
+    return own, shift_z(up, 1), shift_z(down, -1)
 
 
 def local(
@@ -413,13 +446,12 @@
 
     cots, near, part_up, part_down = attend(
         hidden_in[0],
-        after(segment_ids, own),
+        segment_ids,
         stashed_keys[0],
         stashed_values[0],
         queries[0],
         out_cotangent[0],
     )
-    up_1, down_1 = after((up_1, down_1), cots)
     met_up, met_down = shift_x(part_up, 1), shift_x(part_down, -1)
     up_2, down_2 = shift_z(up_1, 1), shift_z(down_1, -1)
 
@@ -437,9 +469,8 @@
     met = [cots, met_up, met_down, far_up, far_down]
     up_4, down_4 = shift_z(up_3[:half], 1), shift_z(down_3[half:], -1)
 
-    firsts = back([own, down_1, up_1, down_2, up_2, down_3, up_3], met)
     opposite = jnp.concatenate([up_4, down_4], axis=0)
-    products = back([opposite], met, firsts)
+    products = back([own, down_1, up_1, down_2, up_2, down_3, up_3, opposite], met)
     met_late = after(met, products[0])
     products = [products[0]] + [shift_x(products[d], -d) for d in (1, 2, 3)]
     terms = weight_terms(near, met_late)

time: 112 us -> 107 us (0.955)
  waiting for transfers between devices: 26 us -> 21.8 us
  local copies, waits for them, and re-layouts: 5.46 us -> 7.03 us
  Pallas kernels: 16.9 us -> 15.4 us
    ppermute x16, waiting for transfers between devices: 12.6 us -> 5.85 us  [shift_z(): return lax.ppermute(value, 'dp', pairs)]
    ppermute x7, waiting for transfers between devices: 5.71 us -> 10.7 us  [shift_x(): return lax.ppermute(value, 'dp', pairs)]
    unnamed x42 -> x52, local copies, waits for them, and re-layouts: 3.04 us -> 6.3 us
    ppermute x16, starting transfers between devices: 22.7 us -> 25.9 us  [shift_z(): return lax.ppermute(value, 'dp', pairs)]
    ppermute x6, waiting for transfers between devices: 7.41 us -> 4.96 us  [send_y(): return lax.ppermute(value, 'section', pairs)]
    slice x3 -> x0, local copies, waits for them, and re-layouts: 1.68 us -> none  [the longest x1 0.93 us: scatter_z(): terms[3][half:]]
    ppermute x4, starting transfers between devices: 11.6 us -> 10 us  [swap_core(): return lax.ppermute(value, 'section', [(s, s ^ 1) for s in range(2 * NY)])]
    pallas_call x5 -> x4, Pallas kernels: 14.3 us -> 12.9 us  [the longest x1 5.55 us: attend(): pl.pallas_call(attend_kernel, out_shape=[shape_of((COTS * ROWS, ROWS)), s...]
  transfers between devices with their start and end apart: 33 -> 33, of which waited for: 11 -> 8; matrix products, arithmetic and copies ran while one was open for 7% -> 6% of each run, Pallas kernels for 6% -> 9%
where the time goes in v3:
time: 107 us
  starting transfers between devices  54.1 us (51%)
  waiting for transfers between devices  21.8 us (20%)
  Pallas kernels  15.4 us (14%)
  other arithmetic  7.59 us (7%)
  local copies, waits for them, and re-layouts  7.03 us (7%)
  between operations  1.29 us (1%)
    ppermute x16, starting transfers between devices, shift_z(): return lax.ppermute(value, 'dp', pairs)  25.9 us
    ppermute x7, waiting for transfers between devices, shift_x(): return lax.ppermute(value, 'dp', pairs)  10.7 us
    ppermute x6, starting transfers between devices, send_y(): return lax.ppermute(value, 'section', pairs)  10.3 us
    ppermute x4, starting transfers between devices, swap_core(): return lax.ppermute(value, 'section', [(s, s ^ 1) for s in range(2 * NY)])  10 us
    ppermute x7, starting transfers between devices, shift_x(): return lax.ppermute(value, 'dp', pairs)  7.87 us
    unnamed x52, local copies, waits for them, and re-layouts  6.3 us
    ppermute x16, waiting for transfers between devices, shift_z(): return lax.ppermute(value, 'dp', pairs)  5.85 us
    pallas_call x1, Pallas kernels, attend(): pl.pallas_call(attend_kernel, out_shape=[shape_of((COTS * ROWS, ROWS)), s...  5.55 us
  transfers between devices with their start and end apart: 33, of which 8 were waited for; matrix products, arithmetic and copies ran while one was open for 6% of the time, Pallas kernels for 9%

profile of v3, /device:TPU:1, one launch (start us, length us, event | category | flops | bytes accessed | tf_op | source)
XLA Modules:
  0.0 107.2 jit_solution(4656720493988388073)
XLA Ops:
  0.6 0.7 convert_element_type.194
  1.3 1.1 %multiply_convert_fusion.refs_0_ = bf16[160,1024]{1,0:T(8,128)(2,1)S(1)} fusion(bf16[160,512]{1,0:T(8,128)(2,1)} %bitcast.27, bf16[160,512]{1,0:T(8,128)(2,1)} %bitcast.28, f32[160]{0:T(256)S(1)} %bitcast.31), kind=kLoop, calls=%fused_computation.24 | loop fusion | flops 983040 | bytes 656000 | tf_op jit(solution)/shard_map/convert_element_type | solution.py:444
  2.4 2.5 %collective-permute-start.1 = (bf16[160,1024]{1,0:T(8,128)(2,1)S(1)}, bf16[160,1024]{1,0:T(8,128)(2,1)S(1)}, u32[]{:S(2)}, u32[]{:S(2)}) collective-permute-start(bf16[160,1024]{1,0:T(8,128)(2,1)S(1)} %multiply_convert_fusion.refs_0_), channel_id=1, source_target_pairs={{0,4},{1,5},{2,6},{3,7},{4,8},{5,9},{6,10},{7,11},{8,12},{9,13},{1... | collective-permute-start | bytes 983048 | tf_op jit(solution)/shard_map/ppermute | solution.py:54
  5.0 4.0 %collective-permute-start = (bf16[160,1024]{1,0:T(8,128)(2,1)S(1)}, bf16[160,1024]{1,0:T(8,128)(2,1)S(1)}, u32[]{:S(2)}, u32[]{:S(2)}) collective-permute-start(bf16[160,1024]{1,0:T(8,128)(2,1)S(1)} %multiply_convert_fusion.refs_0_), channel_id=1, source_target_pairs={{0,28},{1,29},{2,30},{3,31},{4,0},{5,1},{6,2},{7,3},{8,4},{9,5},{1... | collective-permute-start | bytes 983048 | tf_op jit(solution)/shard_map/ppermute | solution.py:54
  9.0 5.6 %attend.1 = (bf16[1024,128]{1,0:T(8,128)(2,1)}, bf16[1280,128]{1,0:T(8,128)(2,1)}, bf16[2944,128]{1,0:T(8,128)(2,1)}, bf16[2944,128]{1,0:T(8,128)(2,1)}) custom-call(bf16[128,5120]{1,0:T(8,128)(2,1)} %bitcast.23, s32[1,128]{1,0:T(1,128)} %refs_1_.1, bf16[128,512]{1,0:T(8,128)(2,1)} %bitcast.29, bf16[128,512]{1,0:T(8,128)(2,1)} %bitcast.30, ...), custom_call_target="tpu_custom_call" | custom-call | flops 536870912 | bytes 4194304 | tf_op jit(solution)/shard_map/attend/pallas_call | solution.py:176
  14.6 1.3 %collective-permute-start.8 = (bf16[2944,128]{1,0:T(8,128)(2,1)}, bf16[2944,128]{1,0:T(8,128)(2,1)S(1)}, u32[]{:S(2)}, u32[]{:S(2)}) collective-permute-start(bf16[2944,128]{1,0:T(8,128)(2,1)} %get-tuple-element.53.refs_5_), channel_id=1, source_target_pairs={{0,1},{1,2},{2,3},{3,0},{4,5},{5,6},{6,7},{7,4},{8,9},{9,10},{10,1... | collective-permute-start | bytes 2261000 | tf_op jit(solution)/shard_map/ppermute | solution.py:59
  15.9 1.5 %collective-permute-start.9 = (bf16[2944,128]{1,0:T(8,128)(2,1)}, bf16[2944,128]{1,0:T(8,128)(2,1)S(1)}, u32[]{:S(2)}, u32[]{:S(2)}) collective-permute-start(bf16[2944,128]{1,0:T(8,128)(2,1)} %get-tuple-element.54.refs_6_), channel_id=1, source_target_pairs={{0,3},{1,0},{2,1},{3,2},{4,7},{5,4},{6,5},{7,6},{8,11},{9,8},{10,9... | collective-permute-start | bytes 2261000 | tf_op jit(solution)/shard_map/ppermute | solution.py:59
  17.4 2.7 %collective-permute-start.3 = (bf16[160,1024]{1,0:T(8,128)(2,1)S(1)}, bf16[160,1024]{1,0:T(8,128)(2,1)S(1)}, u32[]{:S(2)}, u32[]{:S(2)}) collective-permute-start(bf16[160,1024]{1,0:T(8,128)(2,1)S(1)} %collective-permute-done.refs_1_), channel_id=1, source_target_pairs={{0,28},{1,29},{2,30},{3,31},{4,0},{5,1},{6,2},{7,3},{8,4},{9,5},{1... | collective-permute-start | bytes 983048 | tf_op jit(solution)/shard_map/ppermute | solution.py:54
  20.0 0.7 fusion.13
  20.7 2.5 %fusion.12 = f32[128]{0:T(128)S(1)} fusion(s32[1,128]{1,0:T(1,128)S(1)} %copy-done.23, f32[128]{0:T(128)S(1)} %copy-done.24, f32[128]{0:T(128)S(1)} %copy-done.25, f32[]{:T(128)} %bitcast.6, f32[]{:T(128)} %bitcast.5, f32[]{:T(128)} %bitcast.4, f32[]{:T(128)} %bitcast.3), kind=kLoop, calls=%fused_computation.40 | loop fusion | flops 1920 | bytes 2064 | tf_op jit(solution)/shard_map/mul | solution.py:463
  23.2 3.0 %collective-permute-done.2.refs_4_ = bf16[160,1024]{1,0:T(8,128)(2,1)S(1)} collective-permute-done((bf16[160,1024]{1,0:T(8,128)(2,1)S(1)}, bf16[160,1024]{1,0:T(8,128)(2,1)S(1)}, u32[]{:S(2)}, u32[]{:S(2)}) %collective-permute-start.2) | collective-permute-done | bytes 327712 | tf_op jit(solution)/shard_map/ppermute | solution.py:54
  26.3 2.7 %collective-permute-start.4 = (bf16[160,1024]{1,0:T(8,128)(2,1)S(1)}, bf16[160,1024]{1,0:T(8,128)(2,1)S(1)}, u32[]{:S(2)}, u32[]{:S(2)}) collective-permute-start(bf16[160,1024]{1,0:T(8,128)(2,1)S(1)} %collective-permute-done.3.refs_3_), channel_id=1, source_target_pairs={{0,28},{1,29},{2,30},{3,31},{4,0},{5,1},{6,2},{7,3},{8,4},{9,5},{1... | collective-permute-start | bytes 983048 | tf_op jit(solution)/shard_map/ppermute | solution.py:54
  28.9 4.5 %collective-permute-done.8.refs_9_.up = bf16[2944,128]{1,0:T(8,128)(2,1)S(1)} collective-permute-done((bf16[2944,128]{1,0:T(8,128)(2,1)}, bf16[2944,128]{1,0:T(8,128)(2,1)S(1)}, u32[]{:S(2)}, u32[]{:S(2)}) %collective-permute-start.8) | collective-permute-done | bytes 753696 | tf_op jit(solution)/shard_map/ppermute | solution.py:59
  33.6 2.7 %collective-permute-start.11 = (bf16[1152,128]{1,0:T(8,128)(2,1)S(1)}, bf16[1152,128]{1,0:T(8,128)(2,1)S(1)}, u32[]{:S(2)}, u32[]{:S(2)}) collective-permute-start(bf16[1152,128]{1,0:T(8,128)(2,1)S(1)} %slice.59), channel_id=1, source_target_pairs={{0,3},{1,0},{2,1},{3,2},{4,7},{5,4},{6,5},{7,6},{8,11},{9,8},{10,9... | collective-permute-start | bytes 884744 | tf_op jit(solution)/shard_map/ppermute | solution.py:59
  36.5 2.9 %collective-permute-start.7 = (bf16[80,1024]{1,0:T(8,128)(2,1)S(1)}, bf16[80,1024]{1,0:T(8,128)(2,1)S(1)}, u32[]{:S(2)}, u32[]{:S(2)}) collective-permute-start(bf16[80,1024]{1,0:T(8,128)(2,1)S(1)} %slice.57), channel_id=1, source_target_pairs={{0,28},{1,29},{2,30},{3,31},{4,0},{5,1},{6,2},{7,3},{8,4},{9,5},{1... | collective-permute-start | bytes 491528 | tf_op jit(solution)/shard_map/ppermute | solution.py:54
  39.4 2.7 %collective-permute-done.6 = bf16[80,1024]{1,0:T(8,128)(2,1)S(1)} collective-permute-done((bf16[80,1024]{1,0:T(8,128)(2,1)S(1)}, bf16[80,1024]{1,0:T(8,128)(2,1)S(1)}, u32[]{:S(2)}, u32[]{:S(2)}) %collective-permute-start.6) | collective-permute-done | bytes 163872 | tf_op jit(solution)/shard_map/ppermute | solution.py:54
  42.2 3.8 %back.1 = (bf16[8,160,128]{2,1,0:T(8,128)(2,1)S(1)}, bf16[8,160,128]{2,1,0:T(8,128)(2,1)S(1)}, bf16[8,160,128]{2,1,0:T(8,128)(2,1)}, bf16[8,160,128]{2,1,0:T(8,128)(2,1)}) custom-call(bf16[160,1024]{1,0:T(8,128)(2,1)S(1)} %multiply_convert_fusion.refs_0_, bf16[160,1024]{1,0:T(8,128)(2,1)S(1)} %collective-permute-done.refs_1_, ...), custom_call_target="tpu_custom_call" | custom-call | flops 1342177280 | bytes 5242880 | tf_op jit(solution)/shard_map/back/pallas_call | solution.py:255
  46.0 1.7 %collective-permute-start.12 = (bf16[8,160,128]{2,1,0:T(8,128)(2,1)S(1)}, bf16[8,160,128]{2,1,0:T(8,128)(2,1)S(1)}, u32[]{:S(2)}, u32[]{:S(2)}) collective-permute-start(bf16[8,160,128]{2,1,0:T(8,128)(2,1)S(1)} %get-tuple-element.56), channel_id=1, source_target_pairs={{0,3},{1,0},{2,1},{3,2},{4,7},{5,4},{6,5},{7,6},{8,11},{9,8},{10,9... | collective-permute-start | bytes 983048 | tf_op jit(solution)/shard_map/ppermute | solution.py:59
  47.7 0.6 collective-permute-start.14
  48.3 2.1 %weight_terms.1 = (bf16[160,1024]{1,0:T(8,128)(2,1)S(1)}, bf16[160,1024]{1,0:T(8,128)(2,1)S(1)}, bf16[160,1024]{1,0:T(8,128)(2,1)S(1)}, bf16[80,1024]{1,0:T(8,12...) custom-call(bf16[1280,128]{1,0:T(8,128)(2,1)S(1)} %copy-done.3, ...), custom_call_target="tpu_custom_call" | custom-call | flops 1342177280 | bytes 6291456 | tf_op jit(solution)/shard_map/weight_terms/pallas_call | solution.py:230
  50.4 0.7 copy-done.4
  51.1 0.7 copy-done.6
  51.8 0.7 copy-done.8
  52.6 0.7 copy-done.10
  53.3 0.7 copy-done.13
  54.0 0.6 copy-done.15
  54.6 0.7 copy-done.17
  55.3 0.7 copy-done.19
  56.0 0.7 copy-done.21
  56.6 2.7 %collective-permute-start.29 = (bf16[80,1024]{1,0:T(8,128)(2,1)}, bf16[80,1024]{1,0:T(8,128)(2,1)S(1)}, u32[]{:S(2)}, u32[]{:S(2)}) collective-permute-start(bf16[80,1024]{1,0:T(8,128)(2,1)} %copy-done.21), channel_id=1, source_target_pairs={{0,28},{1,29},{2,30},{3,31},{4,0},{5,1},{6,2},{7,3},{8,4},{9,5},{1... | collective-permute-start | bytes 491528 | tf_op jit(solution)/shard_map/ppermute | solution.py:54
  59.3 6.1 %collective-permute-done.14.refs_3_ = bf16[8,160,128]{2,1,0:T(8,128)(2,1)S(1)} collective-permute-done((bf16[8,160,128]{2,1,0:T(8,128)(2,1)}, bf16[8,160,128]{2,1,0:T(8,128)(2,1)S(1)}, u32[]{:S(2)}, u32[]{:S(2)}) %collective-permute-start.14) | collective-permute-done | bytes 327712 | tf_op jit(solution)/shard_map/ppermute | solution.py:59
  65.5 0.9 local_terms.1
  66.4 0.9 collective-permute-start.17
  67.3 0.1 collective-permute-start.15
  67.4 1.0 add_convert_fusion.5
  68.7 2.7 %collective-permute-start.30 = (bf16[160,1024]{1,0:T(8,128)(2,1)S(1)}, bf16[160,1024]{1,0:T(8,128)(2,1)S(1)}, u32[]{:S(2)}, u32[]{:S(2)}) collective-permute-start(bf16[160,1024]{1,0:T(8,128)(2,1)S(1)} %pad_maximum_fusion.2), channel_id=1, source_target_pairs={{0,28},{1,29},{2,30},{3,31},{4,0},{5,1},{6,2},{7,3},{8,4},{9,5},{1... | collective-permute-start | bytes 983048 | tf_op jit(solution)/shard_map/ppermute | solution.py:54
  71.4 0.1 fusion.3
  71.5 1.3 %collective-permute-start.18 = (bf16[2,4,160,128]{3,2,1,0:T(8,128)(2,1)S(1)}, bf16[2,4,160,128]{3,2,1,0:T(8,128)(2,1)S(1)}, u32[]{:S(2)}, u32[]{:S(2)}) collective-permute-start(bf16[2,4,160,128]{3,2,1,0:T(8,128)(2,1)S(1)} %fusion.3), channel_id=1, source_target_pairs={{192,0},{224,32},{193,1},{225,33},{194,2},{226,34},{195,3},{227,35... | collective-permute-start | bytes 983048 | tf_op jit(solution)/shard_map/ppermute | solution.py:68
  72.8 0.7 collective-permute-start.20
  73.5 0.1 fusion
  73.6 1.5 %collective-permute-start.16 = (bf16[2,4,160,128]{3,2,1,0:T(8,128)(2,1)S(1)}, bf16[2,4,160,128]{3,2,1,0:T(8,128)(2,1)S(1)}, u32[]{:S(2)}, u32[]{:S(2)}) collective-permute-start(bf16[2,4,160,128]{3,2,1,0:T(8,128)(2,1)S(1)} %fusion), channel_id=1, source_target_pairs={{192,0},{224,32},{193,1},{225,33},{194,2},{226,34},{195,3},{227,35... | collective-permute-start | bytes 983048 | tf_op jit(solution)/shard_map/ppermute | solution.py:68
  75.1 1.6 %base_terms.1.refs_8_ = f32[128,5120]{1,0:T(8,128)S(1)} custom-call(bf16[2,4,160,128]{3,2,1,0:T(8,128)(2,1)S(1)} %get-tuple-element.60.refs_0_, bf16[2,4,160,128]{3,2,1,0:T(8,128)(2,1)S(1)} %get-tuple-element.62.refs_1_, bf16[2,4,160,128]{3,2,1,0:T(8,128)(2,1)S(1)} %collective-permute-done.15.refs_2_, ...), custom_call_target="tpu_custom_call" | custom-call | bytes 8388608 | tf_op jit(solution)/shard_map/base_terms/pallas_call | solution.py:354
  76.7 0.1 collective-permute-done.26
  76.8 0.7 collective-permute-start.19
  77.5 0.1 add_convert_fusion.3
  77.6 1.9 %collective-permute-start.27 = (bf16[160,1024]{1,0:T(8,128)(2,1)S(1)}, bf16[160,1024]{1,0:T(8,128)(2,1)S(1)}, u32[]{:S(2)}, u32[]{:S(2)}) collective-permute-start(bf16[160,1024]{1,0:T(8,128)(2,1)S(1)} %add_convert_fusion.3), channel_id=1, source_target_pairs={{0,4},{1,5},{2,6},{3,7},{4,8},{5,9},{6,10},{7,11},{8,12},{9,13},{1... | collective-permute-start | bytes 983048 | tf_op jit(solution)/shard_map/ppermute | solution.py:54
  79.5 0.1 add_convert_fusion.1
  79.6 1.5 %collective-permute-done.18.refs_1_ = bf16[2,4,160,128]{3,2,1,0:T(8,128)(2,1)S(1)} collective-permute-done((bf16[2,4,160,128]{3,2,1,0:T(8,128)(2,1)S(1)}, bf16[2,4,160,128]{3,2,1,0:T(8,128)(2,1)S(1)}, u32[]{:S(2)}, u32[]{:S(2)}) %collective-permute-start.18) | collective-permute-done | bytes 327712 | tf_op jit(solution)/shard_map/ppermute | solution.py:68
  81.1 0.8 collective-permute-start.31
  81.9 0.1 fusion.7
  82.0 2.6 %collective-permute-start.22 = (bf16[2,4,160,128]{3,2,1,0:T(8,128)(2,1)S(1)}, bf16[2,4,160,128]{3,2,1,0:T(8,128)(2,1)S(1)}, u32[]{:S(2)}, u32[]{:S(2)}) collective-permute-start(bf16[2,4,160,128]{3,2,1,0:T(8,128)(2,1)S(1)} %fusion.7), channel_id=1, source_target_pairs={{0,64},{32,96},{64,0},{96,32},{1,65},{33,97},{65,1},{97,33},{2,66}... | collective-permute-start | bytes 983048 | tf_op jit(solution)/shard_map/ppermute | solution.py:68
  84.6 3.5 %collective-permute-done.16.refs_0_ = bf16[2,4,160,128]{3,2,1,0:T(8,128)(2,1)S(1)} collective-permute-done((bf16[2,4,160,128]{3,2,1,0:T(8,128)(2,1)S(1)}, bf16[2,4,160,128]{3,2,1,0:T(8,128)(2,1)S(1)}, u32[]{:S(2)}, u32[]{:S(2)}) %collective-permute-start.16) | collective-permute-done | bytes 327712 | tf_op jit(solution)/shard_map/ppermute | solution.py:68
  88.1 0.1 fusion.6
  88.2 3.6 %collective-permute-start.21 = (bf16[2,4,160,128]{3,2,1,0:T(8,128)(2,1)S(1)}, bf16[2,4,160,128]{3,2,1,0:T(8,128)(2,1)S(1)}, u32[]{:S(2)}, u32[]{:S(2)}) collective-permute-start(bf16[2,4,160,128]{3,2,1,0:T(8,128)(2,1)S(1)} %fusion.6), channel_id=1, source_target_pairs={{0,64},{32,96},{64,0},{96,32},{1,65},{33,97},{65,1},{97,33},{2,66}... | collective-permute-start | bytes 983048 | tf_op jit(solution)/shard_map/ppermute | solution.py:68
  91.8 0.1 add_convert_fusion.2
  92.0 0.1 add_convert_fusion
  92.2 2.7 %collective-permute-start.32 = (bf16[160,1024]{1,0:T(8,128)(2,1)S(1)}, bf16[160,1024]{1,0:T(8,128)(2,1)S(1)}, u32[]{:S(2)}, u32[]{:S(2)}) collective-permute-start(bf16[160,1024]{1,0:T(8,128)(2,1)S(1)} %add_convert_fusion), channel_id=1, source_target_pairs={{0,28},{1,29},{2,30},{3,31},{4,0},{5,1},{6,2},{7,3},{8,4},{9,5},{1... | collective-permute-start | bytes 983048 | tf_op jit(solution)/shard_map/ppermute | solution.py:54
  94.9 0.2 fusion.5
  95.1 5.7 %collective-permute-start.24 = (bf16[2,4,160,128]{3,2,1,0:T(8,128)(2,1)S(1)}, bf16[2,4,160,128]{3,2,1,0:T(8,128)(2,1)S(1)}, u32[]{:S(2)}, u32[]{:S(2)}) collective-permute-start(bf16[2,4,160,128]{3,2,1,0:T(8,128)(2,1)S(1)} %fusion.5), channel_id=1, source_target_pairs={{0,32},{32,0},{64,96},{96,64},{128,160},{160,128},{192,224},{224,1... | collective-permute-start | bytes 983048 | tf_op jit(solution)/shard_map/ppermute | solution.py:63
  100.7 0.2 fusion.2
  100.9 3.3 %collective-permute-start.23 = (bf16[2,4,160,128]{3,2,1,0:T(8,128)(2,1)S(1)}, bf16[2,4,160,128]{3,2,1,0:T(8,128)(2,1)S(1)}, u32[]{:S(2)}, u32[]{:S(2)}) collective-permute-start(bf16[2,4,160,128]{3,2,1,0:T(8,128)(2,1)S(1)} %fusion.2), channel_id=1, source_target_pairs={{0,32},{32,0},{64,96},{96,64},{128,160},{160,128},{192,224},{224,1... | collective-permute-start | bytes 983048 | tf_op jit(solution)/shard_map/ppermute | solution.py:63
  104.3 1.0 multiply_bitcast_fusion
  105.2 0.3 collective-permute-done.23.refs_6_
  105.5 1.5 %finish.1 = bf16[128,5120]{1,0:T(8,128)(2,1)} custom-call(bf16[2,4,160,128]{3,2,1,0:T(8,128)(2,1)S(1)} %collective-permute-done.16.refs_0_, bf16[2,4,160,128]{3,2,1,0:T(8,128)(2,1)S(1)} %collective-permute-done.18.refs_1_, bf16[2,4,160,128]{3,2,1,0:T(8,128)(2,1)S(1)} %collective-permute-done.19.refs_2_, ...), custom_call_target="tpu_custom_call" | custom-call | bytes 6291456 | tf_op jit(solution)/shard_map/finish/pallas_call | solution.py:391
  (84 shorter events, 0.7 us)
Async XLA Ops:
  2.4 14.9 %collective-permute-start.1 = (bf16[160,1024]{1,0:T(8,128)(2,1)S(1)}, bf16[160,1024]{1,0:T(8,128)(2,1)S(1)}, u32[]{:S(2)}, u32[]{:S(2)}) collective-permute-start(bf16[160,1024]{1,0:T(8,128)(2,1)S(1)} %multiply_convert_fusion.refs_0_), channel_id=1, source_target_pairs={{0,4},{1,5},{2,6},{3,7},{4,8},{5,9},{6,10},{7,11},{8,12},{9,13},{1... | collective-permute-start | bytes 983048 | tf_op jit(solution)/shard_map/ppermute | solution.py:54
  5.0 12.4 %collective-permute-start = (bf16[160,1024]{1,0:T(8,128)(2,1)S(1)}, bf16[160,1024]{1,0:T(8,128)(2,1)S(1)}, u32[]{:S(2)}, u32[]{:S(2)}) collective-permute-start(bf16[160,1024]{1,0:T(8,128)(2,1)S(1)} %multiply_convert_fusion.refs_0_), channel_id=1, source_target_pairs={{0,28},{1,29},{2,30},{3,31},{4,0},{5,1},{6,2},{7,3},{8,4},{9,5},{1... | collective-permute-start | bytes 983048 | tf_op jit(solution)/shard_map/ppermute | solution.py:54
  9.0 11.0 %copy-start.22 = (f32[1,4]{1,0:T(1,128)S(1)}, f32[1,4]{1,0:T(1,128)}, u32[]{:S(2)}) copy-start(f32[1,4]{1,0:T(1,128)} %param.24) | copy-start | bytes 52
  9.0 11.7 %copy-start.23 = (s32[1,128]{1,0:T(1,128)S(1)}, s32[1,128]{1,0:T(1,128)}, u32[]{:S(2)}) copy-start(s32[1,128]{1,0:T(1,128)} %refs_1_.1) | copy-start | bytes 1540
  9.0 11.7 %copy-start.24 = (f32[128]{0:T(128)S(1)}, f32[128]{0:T(128)}, u32[]{:S(2)}) copy-start(f32[128]{0:T(128)} %param.22) | copy-start | bytes 1540
  9.0 11.7 %copy-start.25 = (f32[128]{0:T(128)S(1)}, f32[128]{0:T(128)}, u32[]{:S(2)}) copy-start(f32[128]{0:T(128)} %param.23) | copy-start | bytes 1540
  14.6 27.6 %copy-start.12 = (bf16[1024,128]{1,0:T(8,128)(2,1)S(1)}, bf16[1024,128]{1,0:T(8,128)(2,1)}, u32[]{:S(2)}) copy-start(bf16[1024,128]{1,0:T(8,128)(2,1)} %get-tuple-element.66.refs_8_.cots) | copy-start | bytes 786436
  14.6 18.9 %collective-permute-start.8 = (bf16[2944,128]{1,0:T(8,128)(2,1)}, bf16[2944,128]{1,0:T(8,128)(2,1)S(1)}, u32[]{:S(2)}, u32[]{:S(2)}) collective-permute-start(bf16[2944,128]{1,0:T(8,128)(2,1)} %get-tuple-element.53.refs_5_), channel_id=1, source_target_pairs={{0,1},{1,2},{2,3},{3,0},{4,5},{5,6},{6,7},{7,4},{8,9},{9,10},{10,1... | collective-permute-start | bytes 2261000 | tf_op jit(solution)/shard_map/ppermute | solution.py:59
  15.9 17.7 %collective-permute-start.9 = (bf16[2944,128]{1,0:T(8,128)(2,1)}, bf16[2944,128]{1,0:T(8,128)(2,1)S(1)}, u32[]{:S(2)}, u32[]{:S(2)}) collective-permute-start(bf16[2944,128]{1,0:T(8,128)(2,1)} %get-tuple-element.54.refs_6_), channel_id=1, source_target_pairs={{0,3},{1,0},{2,1},{3,2},{4,7},{5,4},{6,5},{7,6},{8,11},{9,8},{10,9... | collective-permute-start | bytes 2261000 | tf_op jit(solution)/shard_map/ppermute | solution.py:59
  17.3 8.9 %collective-permute-start.2 = (bf16[160,1024]{1,0:T(8,128)(2,1)S(1)}, bf16[160,1024]{1,0:T(8,128)(2,1)S(1)}, u32[]{:S(2)}, u32[]{:S(2)}) collective-permute-start(bf16[160,1024]{1,0:T(8,128)(2,1)S(1)} %collective-permute-done.1.refs_2_), channel_id=1, source_target_pairs={{0,4},{1,5},{2,6},{3,7},{4,8},{5,9},{6,10},{7,11},{8,12},{9,13},{1... | collective-permute-start | bytes 983048 | tf_op jit(solution)/shard_map/ppermute | solution.py:54
  17.4 8.9 %collective-permute-start.3 = (bf16[160,1024]{1,0:T(8,128)(2,1)S(1)}, bf16[160,1024]{1,0:T(8,128)(2,1)S(1)}, u32[]{:S(2)}, u32[]{:S(2)}) collective-permute-start(bf16[160,1024]{1,0:T(8,128)(2,1)S(1)} %collective-permute-done.refs_1_), channel_id=1, source_target_pairs={{0,28},{1,29},{2,30},{3,31},{4,0},{5,1},{6,2},{7,3},{8,4},{9,5},{1... | collective-permute-start | bytes 983048 | tf_op jit(solution)/shard_map/ppermute | solution.py:54
  26.3 10.1 %collective-permute-start.5 = (bf16[160,1024]{1,0:T(8,128)(2,1)S(1)}, bf16[160,1024]{1,0:T(8,128)(2,1)S(1)}, u32[]{:S(2)}, u32[]{:S(2)}) collective-permute-start(bf16[160,1024]{1,0:T(8,128)(2,1)S(1)} %collective-permute-done.2.refs_4_), channel_id=1, source_target_pairs={{0,4},{1,5},{2,6},{3,7},{4,8},{5,9},{6,10},{7,11},{8,12},{9,13},{1... | collective-permute-start | bytes 983048 | tf_op jit(solution)/shard_map/ppermute | solution.py:54
  26.3 10.2 %collective-permute-start.4 = (bf16[160,1024]{1,0:T(8,128)(2,1)S(1)}, bf16[160,1024]{1,0:T(8,128)(2,1)S(1)}, u32[]{:S(2)}, u32[]{:S(2)}) collective-permute-start(bf16[160,1024]{1,0:T(8,128)(2,1)S(1)} %collective-permute-done.3.refs_3_), channel_id=1, source_target_pairs={{0,28},{1,29},{2,30},{3,31},{4,0},{5,1},{6,2},{7,3},{8,4},{9,5},{1... | collective-permute-start | bytes 983048 | tf_op jit(solution)/shard_map/ppermute | solution.py:54
  33.5 8.7 %collective-permute-start.10 = (bf16[1152,128]{1,0:T(8,128)(2,1)S(1)}, bf16[1152,128]{1,0:T(8,128)(2,1)S(1)}, u32[]{:S(2)}, u32[]{:S(2)}) collective-permute-start(bf16[1152,128]{1,0:T(8,128)(2,1)S(1)} %slice.58), channel_id=1, source_target_pairs={{0,1},{1,2},{2,3},{3,0},{4,5},{5,6},{6,7},{7,4},{8,9},{9,10},{10,1... | collective-permute-start | bytes 884744 | tf_op jit(solution)/shard_map/ppermute | solution.py:59
  33.6 8.5 %collective-permute-start.11 = (bf16[1152,128]{1,0:T(8,128)(2,1)S(1)}, bf16[1152,128]{1,0:T(8,128)(2,1)S(1)}, u32[]{:S(2)}, u32[]{:S(2)}) collective-permute-start(bf16[1152,128]{1,0:T(8,128)(2,1)S(1)} %slice.59), channel_id=1, source_target_pairs={{0,3},{1,0},{2,1},{3,2},{4,7},{5,4},{6,5},{7,6},{8,11},{9,8},{10,9... | collective-permute-start | bytes 884744 | tf_op jit(solution)/shard_map/ppermute | solution.py:59
  36.4 5.8 %collective-permute-start.6 = (bf16[80,1024]{1,0:T(8,128)(2,1)S(1)}, bf16[80,1024]{1,0:T(8,128)(2,1)S(1)}, u32[]{:S(2)}, u32[]{:S(2)}) collective-permute-start(bf16[80,1024]{1,0:T(8,128)(2,1)S(1)} %slice.56), channel_id=1, source_target_pairs={{0,4},{1,5},{2,6},{3,7},{4,8},{5,9},{6,10},{7,11},{8,12},{9,13},{1... | collective-permute-start | bytes 491528 | tf_op jit(solution)/shard_map/ppermute | solution.py:54
  36.5 5.6 %collective-permute-start.7 = (bf16[80,1024]{1,0:T(8,128)(2,1)S(1)}, bf16[80,1024]{1,0:T(8,128)(2,1)S(1)}, u32[]{:S(2)}, u32[]{:S(2)}) collective-permute-start(bf16[80,1024]{1,0:T(8,128)(2,1)S(1)} %slice.57), channel_id=1, source_target_pairs={{0,28},{1,29},{2,30},{3,31},{4,0},{5,1},{6,2},{7,3},{8,4},{9,5},{1... | collective-permute-start | bytes 491528 | tf_op jit(solution)/shard_map/ppermute | solution.py:54
  42.2 6.1 %copy-start.3 = (bf16[1280,128]{1,0:T(8,128)(2,1)S(1)}, bf16[1280,128]{1,0:T(8,128)(2,1)}, u32[]{:S(2)}) copy-start(bf16[1280,128]{1,0:T(8,128)(2,1)} %get-tuple-element.59.refs_4_.near) | copy-start | bytes 983044
  46.0 9.9 %collective-permute-start.12 = (bf16[8,160,128]{2,1,0:T(8,128)(2,1)S(1)}, bf16[8,160,128]{2,1,0:T(8,128)(2,1)S(1)}, u32[]{:S(2)}, u32[]{:S(2)}) collective-permute-start(bf16[8,160,128]{2,1,0:T(8,128)(2,1)S(1)} %get-tuple-element.56), channel_id=1, source_target_pairs={{0,3},{1,0},{2,1},{3,2},{4,7},{5,4},{6,5},{7,6},{8,11},{9,8},{10,9... | collective-permute-start | bytes 983048 | tf_op jit(solution)/shard_map/ppermute | solution.py:59
  47.7 11.6 %collective-permute-start.13 = (bf16[8,160,128]{2,1,0:T(8,128)(2,1)}, bf16[8,160,128]{2,1,0:T(8,128)(2,1)S(1)}, u32[]{:S(2)}, u32[]{:S(2)}) collective-permute-start(bf16[8,160,128]{2,1,0:T(8,128)(2,1)} %get-tuple-element.57), channel_id=1, source_target_pairs={{0,2},{1,3},{2,0},{3,1},{4,6},{5,7},{6,4},{7,5},{8,10},{9,11},{10,... | collective-permute-start | bytes 983048 | tf_op jit(solution)/shard_map/ppermute | solution.py:59
  47.7 17.7 %collective-permute-start.14 = (bf16[8,160,128]{2,1,0:T(8,128)(2,1)}, bf16[8,160,128]{2,1,0:T(8,128)(2,1)S(1)}, u32[]{:S(2)}, u32[]{:S(2)}) collective-permute-start(bf16[8,160,128]{2,1,0:T(8,128)(2,1)} %get-tuple-element.58), channel_id=1, source_target_pairs={{0,1},{1,2},{2,3},{3,0},{4,5},{5,6},{6,7},{7,4},{8,9},{9,10},{10,1... | collective-permute-start | bytes 983048 | tf_op jit(solution)/shard_map/ppermute | solution.py:59
  48.3 17.1 %copy-start.1 = (bf16[2944,128]{1,0:T(8,128)(2,1)S(1)}, bf16[2944,128]{1,0:T(8,128)(2,1)}, u32[]{:S(2)}) copy-start(bf16[2944,128]{1,0:T(8,128)(2,1)} %get-tuple-element.53.refs_5_) | copy-start | bytes 2260996
  48.3 17.1 %copy-start.2 = (bf16[2944,128]{1,0:T(8,128)(2,1)S(1)}, bf16[2944,128]{1,0:T(8,128)(2,1)}, u32[]{:S(2)}) copy-start(bf16[2944,128]{1,0:T(8,128)(2,1)} %get-tuple-element.54.refs_6_) | copy-start | bytes 2260996
  50.4 0.7 copy-start.4
  51.1 0.7 copy-start.6
  51.8 0.7 copy-start.8
  52.6 0.7 copy-start.10
  53.3 0.7 copy-start.13
  54.0 0.6 copy-start.15
  54.6 0.7 copy-start.17
  55.3 0.7 copy-start.19
  56.0 0.7 copy-start.21
  56.6 10.8 %collective-permute-start.25 = (bf16[80,1024]{1,0:T(8,128)(2,1)}, bf16[80,1024]{1,0:T(8,128)(2,1)}, u32[]{:S(2)}, u32[]{:S(2)}) collective-permute-start(bf16[80,1024]{1,0:T(8,128)(2,1)} %get-tuple-element.86), channel_id=1, source_target_pairs={{0,4},{1,5},{2,6},{3,7},{4,8},{5,9},{6,10},{7,11},{8,12},{9,13},{1... | collective-permute-start | bytes 491528 | tf_op jit(solution)/shard_map/ppermute | solution.py:54
  56.6 10.8 %copy-start.20 = (bf16[80,1024]{1,0:T(8,128)(2,1)S(1)}, bf16[80,1024]{1,0:T(8,128)(2,1)}, u32[]{:S(2)}) copy-start(bf16[80,1024]{1,0:T(8,128)(2,1)} %copy-done.19) | copy-start | bytes 491524
  56.6 11.8 %copy-start.16 = (bf16[80,1024]{1,0:T(8,128)(2,1)S(1)}, bf16[80,1024]{1,0:T(8,128)(2,1)}, u32[]{:S(2)}) copy-start(bf16[80,1024]{1,0:T(8,128)(2,1)} %copy-done.15) | copy-start | bytes 491524
  56.6 11.9 %copy-start.18 = (bf16[80,1024]{1,0:T(8,128)(2,1)S(1)}, bf16[80,1024]{1,0:T(8,128)(2,1)}, u32[]{:S(2)}) copy-start(bf16[80,1024]{1,0:T(8,128)(2,1)} %copy-done.17) | copy-start | bytes 491524
  56.6 11.9 %collective-permute-start.29 = (bf16[80,1024]{1,0:T(8,128)(2,1)}, bf16[80,1024]{1,0:T(8,128)(2,1)S(1)}, u32[]{:S(2)}, u32[]{:S(2)}) collective-permute-start(bf16[80,1024]{1,0:T(8,128)(2,1)} %copy-done.21), channel_id=1, source_target_pairs={{0,28},{1,29},{2,30},{3,31},{4,0},{5,1},{6,2},{7,3},{8,4},{9,5},{1... | collective-permute-start | bytes 491528 | tf_op jit(solution)/shard_map/ppermute | solution.py:54
  66.4 2.2 %copy-start.14 = (bf16[80,1024]{1,0:T(8,128)(2,1)S(1)}, bf16[80,1024]{1,0:T(8,128)(2,1)}, u32[]{:S(2)}) copy-start(bf16[80,1024]{1,0:T(8,128)(2,1)} %copy-done.13) | copy-start | bytes 491524
  66.4 5.0 %collective-permute-start.17 = (bf16[2,4,160,128]{3,2,1,0:T(8,128)(2,1)S(1)}, bf16[2,4,160,128]{3,2,1,0:T(8,128)(2,1)S(1)}, u32[]{:S(2)}, u32[]{:S(2)}) collective-permute-start(bf16[2,4,160,128]{3,2,1,0:T(8,128)(2,1)S(1)} %get-tuple-element.63.refs_5_), channel_id=1, source_target_pairs={{0,32},{32,0},{64,96},{96,64},{128,160},{160,128},{192,224},{224,1... | collective-permute-start | bytes 983048 | tf_op jit(solution)/shard_map/ppermute | solution.py:63
  67.3 6.1 %collective-permute-start.15 = (bf16[2,4,160,128]{3,2,1,0:T(8,128)(2,1)S(1)}, bf16[2,4,160,128]{3,2,1,0:T(8,128)(2,1)S(1)}, u32[]{:S(2)}, u32[]{:S(2)}) collective-permute-start(bf16[2,4,160,128]{3,2,1,0:T(8,128)(2,1)S(1)} %get-tuple-element.61.refs_4_), channel_id=1, source_target_pairs={{0,32},{32,0},{64,96},{96,64},{128,160},{160,128},{192,224},{224,1... | collective-permute-start | bytes 983048 | tf_op jit(solution)/shard_map/ppermute | solution.py:63
  68.4 8.4 %collective-permute-start.26 = (bf16[160,1024]{1,0:T(8,128)(2,1)S(1)}, bf16[160,1024]{1,0:T(8,128)(2,1)S(1)}, u32[]{:S(2)}, u32[]{:S(2)}) collective-permute-start(bf16[160,1024]{1,0:T(8,128)(2,1)S(1)} %pad_maximum_fusion.1), channel_id=1, source_target_pairs={{0,4},{1,5},{2,6},{3,7},{4,8},{5,9},{6,10},{7,11},{8,12},{9,13},{1... | collective-permute-start | bytes 983048 | tf_op jit(solution)/shard_map/ppermute | solution.py:54
  68.6 6.5 %copy-start = (bf16[128,5120]{1,0:T(8,128)(2,1)S(1)}, bf16[128,5120]{1,0:T(8,128)(2,1)}, u32[]{:S(2)}) copy-start(bf16[128,5120]{1,0:T(8,128)(2,1)} %refs_6_.1) | copy-start | bytes 3932164
  68.7 8.9 %collective-permute-start.30 = (bf16[160,1024]{1,0:T(8,128)(2,1)S(1)}, bf16[160,1024]{1,0:T(8,128)(2,1)S(1)}, u32[]{:S(2)}, u32[]{:S(2)}) collective-permute-start(bf16[160,1024]{1,0:T(8,128)(2,1)S(1)} %pad_maximum_fusion.2), channel_id=1, source_target_pairs={{0,28},{1,29},{2,30},{3,31},{4,0},{5,1},{6,2},{7,3},{8,4},{9,5},{1... | collective-permute-start | bytes 983048 | tf_op jit(solution)/shard_map/ppermute | solution.py:54
  71.5 9.6 %collective-permute-start.18 = (bf16[2,4,160,128]{3,2,1,0:T(8,128)(2,1)S(1)}, bf16[2,4,160,128]{3,2,1,0:T(8,128)(2,1)S(1)}, u32[]{:S(2)}, u32[]{:S(2)}) collective-permute-start(bf16[2,4,160,128]{3,2,1,0:T(8,128)(2,1)S(1)} %fusion.3), channel_id=1, source_target_pairs={{192,0},{224,32},{193,1},{225,33},{194,2},{226,34},{195,3},{227,35... | collective-permute-start | bytes 983048 | tf_op jit(solution)/shard_map/ppermute | solution.py:68
  72.8 9.1 %collective-permute-start.20 = (bf16[2,4,160,128]{3,2,1,0:T(8,128)(2,1)S(1)}, bf16[2,4,160,128]{3,2,1,0:T(8,128)(2,1)S(1)}, u32[]{:S(2)}, u32[]{:S(2)}) collective-permute-start(bf16[2,4,160,128]{3,2,1,0:T(8,128)(2,1)S(1)} %fusion.3), channel_id=1, source_target_pairs={{192,128},{224,160},{128,64},{160,96},{193,129},{225,161},{129,65}... | collective-permute-start | bytes 983048 | tf_op jit(solution)/shard_map/ppermute | solution.py:68
  73.6 14.5 %collective-permute-start.16 = (bf16[2,4,160,128]{3,2,1,0:T(8,128)(2,1)S(1)}, bf16[2,4,160,128]{3,2,1,0:T(8,128)(2,1)S(1)}, u32[]{:S(2)}, u32[]{:S(2)}) collective-permute-start(bf16[2,4,160,128]{3,2,1,0:T(8,128)(2,1)S(1)} %fusion), channel_id=1, source_target_pairs={{192,0},{224,32},{193,1},{225,33},{194,2},{226,34},{195,3},{227,35... | collective-permute-start | bytes 983048 | tf_op jit(solution)/shard_map/ppermute | solution.py:68
  75.1 2.4 %copy-start.11 = (bf16[160,1024]{1,0:T(8,128)(2,1)S(1)}, bf16[160,1024]{1,0:T(8,128)(2,1)}, u32[]{:S(2)}) copy-start(bf16[160,1024]{1,0:T(8,128)(2,1)} %copy-done.10) | copy-start | bytes 983044
  75.1 4.4 %copy-start.9 = (bf16[160,1024]{1,0:T(8,128)(2,1)S(1)}, bf16[160,1024]{1,0:T(8,128)(2,1)}, u32[]{:S(2)}) copy-start(bf16[160,1024]{1,0:T(8,128)(2,1)} %copy-done.8) | copy-start | bytes 983044
  76.8 11.3 %collective-permute-start.19 = (bf16[2,4,160,128]{3,2,1,0:T(8,128)(2,1)S(1)}, bf16[2,4,160,128]{3,2,1,0:T(8,128)(2,1)S(1)}, u32[]{:S(2)}, u32[]{:S(2)}) collective-permute-start(bf16[2,4,160,128]{3,2,1,0:T(8,128)(2,1)S(1)} %fusion), channel_id=1, source_target_pairs={{192,128},{224,160},{128,64},{160,96},{193,129},{225,161},{129,65}... | collective-permute-start | bytes 983048 | tf_op jit(solution)/shard_map/ppermute | solution.py:68
  77.6 14.2 %collective-permute-start.27 = (bf16[160,1024]{1,0:T(8,128)(2,1)S(1)}, bf16[160,1024]{1,0:T(8,128)(2,1)S(1)}, u32[]{:S(2)}, u32[]{:S(2)}) collective-permute-start(bf16[160,1024]{1,0:T(8,128)(2,1)S(1)} %add_convert_fusion.3), channel_id=1, source_target_pairs={{0,4},{1,5},{2,6},{3,7},{4,8},{5,9},{6,10},{7,11},{8,12},{9,13},{1... | collective-permute-start | bytes 983048 | tf_op jit(solution)/shard_map/ppermute | solution.py:54
  79.6 12.2 %copy-start.7 = (bf16[160,1024]{1,0:T(8,128)(2,1)S(1)}, bf16[160,1024]{1,0:T(8,128)(2,1)}, u32[]{:S(2)}) copy-start(bf16[160,1024]{1,0:T(8,128)(2,1)} %copy-done.6) | copy-start | bytes 983044
  81.1 10.9 %collective-permute-start.31 = (bf16[160,1024]{1,0:T(8,128)(2,1)S(1)}, bf16[160,1024]{1,0:T(8,128)(2,1)S(1)}, u32[]{:S(2)}, u32[]{:S(2)}) collective-permute-start(bf16[160,1024]{1,0:T(8,128)(2,1)S(1)} %add_convert_fusion.1), channel_id=1, source_target_pairs={{0,28},{1,29},{2,30},{3,31},{4,0},{5,1},{6,2},{7,3},{8,4},{9,5},{1... | collective-permute-start | bytes 983048 | tf_op jit(solution)/shard_map/ppermute | solution.py:54
  82.0 10.0 %copy-start.5 = (bf16[160,1024]{1,0:T(8,128)(2,1)S(1)}, bf16[160,1024]{1,0:T(8,128)(2,1)}, u32[]{:S(2)}) copy-start(bf16[160,1024]{1,0:T(8,128)(2,1)} %copy-done.4) | copy-start | bytes 983044
  82.0 12.9 %collective-permute-start.22 = (bf16[2,4,160,128]{3,2,1,0:T(8,128)(2,1)S(1)}, bf16[2,4,160,128]{3,2,1,0:T(8,128)(2,1)S(1)}, u32[]{:S(2)}, u32[]{:S(2)}) collective-permute-start(bf16[2,4,160,128]{3,2,1,0:T(8,128)(2,1)S(1)} %fusion.7), channel_id=1, source_target_pairs={{0,64},{32,96},{64,0},{96,32},{1,65},{33,97},{65,1},{97,33},{2,66}... | collective-permute-start | bytes 983048 | tf_op jit(solution)/shard_map/ppermute | solution.py:68
  88.2 12.5 %collective-permute-start.21 = (bf16[2,4,160,128]{3,2,1,0:T(8,128)(2,1)S(1)}, bf16[2,4,160,128]{3,2,1,0:T(8,128)(2,1)S(1)}, u32[]{:S(2)}, u32[]{:S(2)}) collective-permute-start(bf16[2,4,160,128]{3,2,1,0:T(8,128)(2,1)S(1)} %fusion.6), channel_id=1, source_target_pairs={{0,64},{32,96},{64,0},{96,32},{1,65},{33,97},{65,1},{97,33},{2,66}... | collective-permute-start | bytes 983048 | tf_op jit(solution)/shard_map/ppermute | solution.py:68
  91.9 12.3 %collective-permute-start.28 = (bf16[160,1024]{1,0:T(8,128)(2,1)S(1)}, bf16[160,1024]{1,0:T(8,128)(2,1)S(1)}, u32[]{:S(2)}, u32[]{:S(2)}) collective-permute-start(bf16[160,1024]{1,0:T(8,128)(2,1)S(1)} %add_convert_fusion.2), channel_id=1, source_target_pairs={{0,4},{1,5},{2,6},{3,7},{4,8},{5,9},{6,10},{7,11},{8,12},{9,13},{1... | collective-permute-start | bytes 983048 | tf_op jit(solution)/shard_map/ppermute | solution.py:54
  92.2 12.1 %collective-permute-start.32 = (bf16[160,1024]{1,0:T(8,128)(2,1)S(1)}, bf16[160,1024]{1,0:T(8,128)(2,1)S(1)}, u32[]{:S(2)}, u32[]{:S(2)}) collective-permute-start(bf16[160,1024]{1,0:T(8,128)(2,1)S(1)} %add_convert_fusion), channel_id=1, source_target_pairs={{0,28},{1,29},{2,30},{3,31},{4,0},{5,1},{6,2},{7,3},{8,4},{9,5},{1... | collective-permute-start | bytes 983048 | tf_op jit(solution)/shard_map/ppermute | solution.py:54
  95.1 10.2 %collective-permute-start.24 = (bf16[2,4,160,128]{3,2,1,0:T(8,128)(2,1)S(1)}, bf16[2,4,160,128]{3,2,1,0:T(8,128)(2,1)S(1)}, u32[]{:S(2)}, u32[]{:S(2)}) collective-permute-start(bf16[2,4,160,128]{3,2,1,0:T(8,128)(2,1)S(1)} %fusion.5), channel_id=1, source_target_pairs={{0,32},{32,0},{64,96},{96,64},{128,160},{160,128},{192,224},{224,1... | collective-permute-start | bytes 983048 | tf_op jit(solution)/shard_map/ppermute | solution.py:63
  100.9 4.6 %collective-permute-start.23 = (bf16[2,4,160,128]{3,2,1,0:T(8,128)(2,1)S(1)}, bf16[2,4,160,128]{3,2,1,0:T(8,128)(2,1)S(1)}, u32[]{:S(2)}, u32[]{:S(2)}) collective-permute-start(bf16[2,4,160,128]{3,2,1,0:T(8,128)(2,1)S(1)} %fusion.2), channel_id=1, source_target_pairs={{0,32},{32,0},{64,96},{96,64},{128,160},{160,128},{192,224},{224,1... | collective-permute-start | bytes 983048 | tf_op jit(solution)/shard_map/ppermute | solution.py:63

commit v4 on v3

--- a/solution.py
+++ b/solution.py
@@ -19,7 +19,7 @@
 NY = 4
 SLAB = D // (NZ * NX)
 EPSILON = 1e-06
-VMEM = pltpu.CompilerParams(vmem_limit_bytes=16 * 1024 * 1024)
+VMEM = pltpu.CompilerParams(vmem_limit_bytes=12 * 1024 * 1024)
 MOST_VMEM = pltpu.CompilerParams(vmem_limit_bytes=57 * 1024 * 1024)
 NT = (((1,), (1,)), ((), ()))
 

time: 107 us -> 107 us (level)
  no operation moved by 1% of the time
where the time goes in v4:
time: 107 us
  starting transfers between devices  54.1 us (51%)
  waiting for transfers between devices  21.8 us (20%)
  Pallas kernels  15.4 us (14%)
  other arithmetic  7.59 us (7%)
  local copies, waits for them, and re-layouts  7.03 us (7%)
  between operations  1.29 us (1%)
    ppermute x16, starting transfers between devices, shift_z(): return lax.ppermute(value, 'dp', pairs)  25.9 us
    ppermute x7, waiting for transfers between devices, shift_x(): return lax.ppermute(value, 'dp', pairs)  10.7 us
    ppermute x6, starting transfers between devices, send_y(): return lax.ppermute(value, 'section', pairs)  10.3 us
    ppermute x4, starting transfers between devices, swap_core(): return lax.ppermute(value, 'section', [(s, s ^ 1) for s in range(2 * NY)])  10 us
    ppermute x7, starting transfers between devices, shift_x(): return lax.ppermute(value, 'dp', pairs)  7.87 us
    unnamed x52, local copies, waits for them, and re-layouts  6.3 us
    ppermute x16, waiting for transfers between devices, shift_z(): return lax.ppermute(value, 'dp', pairs)  5.85 us
    pallas_call x1, Pallas kernels, attend(): pl.pallas_call(attend_kernel, out_shape=[shape_of((COTS * ROWS, ROWS)), s...  5.55 us
  transfers between devices with their start and end apart: 33, of which 8 were waited for; matrix products, arithmetic and copies ran while one was open for 6% of the time, Pallas kernels for 9%

profile of v4, /device:TPU:1, one launch (start us, length us, event | category | flops | bytes accessed | tf_op | source)
XLA Modules:
  0.0 107.2 jit_solution(13821093336761477228)
XLA Ops:
  0.6 0.7 convert_element_type.194
  1.3 1.1 %multiply_convert_fusion.refs_0_ = bf16[160,1024]{1,0:T(8,128)(2,1)S(1)} fusion(bf16[160,512]{1,0:T(8,128)(2,1)} %bitcast.27, bf16[160,512]{1,0:T(8,128)(2,1)} %bitcast.28, f32[160]{0:T(256)S(1)} %bitcast.31), kind=kLoop, calls=%fused_computation.24 | loop fusion | flops 983040 | bytes 656000 | tf_op jit(solution)/shard_map/convert_element_type | solution.py:444
  2.4 2.5 %collective-permute-start.1 = (bf16[160,1024]{1,0:T(8,128)(2,1)S(1)}, bf16[160,1024]{1,0:T(8,128)(2,1)S(1)}, u32[]{:S(2)}, u32[]{:S(2)}) collective-permute-start(bf16[160,1024]{1,0:T(8,128)(2,1)S(1)} %multiply_convert_fusion.refs_0_), channel_id=1, source_target_pairs={{0,4},{1,5},{2,6},{3,7},{4,8},{5,9},{6,10},{7,11},{8,12},{9,13},{1... | collective-permute-start | bytes 983048 | tf_op jit(solution)/shard_map/ppermute | solution.py:54
  5.0 4.0 %collective-permute-start = (bf16[160,1024]{1,0:T(8,128)(2,1)S(1)}, bf16[160,1024]{1,0:T(8,128)(2,1)S(1)}, u32[]{:S(2)}, u32[]{:S(2)}) collective-permute-start(bf16[160,1024]{1,0:T(8,128)(2,1)S(1)} %multiply_convert_fusion.refs_0_), channel_id=1, source_target_pairs={{0,28},{1,29},{2,30},{3,31},{4,0},{5,1},{6,2},{7,3},{8,4},{9,5},{1... | collective-permute-start | bytes 983048 | tf_op jit(solution)/shard_map/ppermute | solution.py:54
  9.0 5.6 %attend.1 = (bf16[1024,128]{1,0:T(8,128)(2,1)}, bf16[1280,128]{1,0:T(8,128)(2,1)}, bf16[2944,128]{1,0:T(8,128)(2,1)}, bf16[2944,128]{1,0:T(8,128)(2,1)}) custom-call(bf16[128,5120]{1,0:T(8,128)(2,1)} %bitcast.23, s32[1,128]{1,0:T(1,128)} %refs_1_.1, bf16[128,512]{1,0:T(8,128)(2,1)} %bitcast.29, bf16[128,512]{1,0:T(8,128)(2,1)} %bitcast.30, ...), custom_call_target="tpu_custom_call" | custom-call | flops 536870912 | bytes 4194304 | tf_op jit(solution)/shard_map/attend/pallas_call | solution.py:176
  14.6 1.3 %collective-permute-start.8 = (bf16[2944,128]{1,0:T(8,128)(2,1)}, bf16[2944,128]{1,0:T(8,128)(2,1)S(1)}, u32[]{:S(2)}, u32[]{:S(2)}) collective-permute-start(bf16[2944,128]{1,0:T(8,128)(2,1)} %get-tuple-element.53.refs_5_), channel_id=1, source_target_pairs={{0,1},{1,2},{2,3},{3,0},{4,5},{5,6},{6,7},{7,4},{8,9},{9,10},{10,1... | collective-permute-start | bytes 2261000 | tf_op jit(solution)/shard_map/ppermute | solution.py:59
  15.9 1.5 %collective-permute-start.9 = (bf16[2944,128]{1,0:T(8,128)(2,1)}, bf16[2944,128]{1,0:T(8,128)(2,1)S(1)}, u32[]{:S(2)}, u32[]{:S(2)}) collective-permute-start(bf16[2944,128]{1,0:T(8,128)(2,1)} %get-tuple-element.54.refs_6_), channel_id=1, source_target_pairs={{0,3},{1,0},{2,1},{3,2},{4,7},{5,4},{6,5},{7,6},{8,11},{9,8},{10,9... | collective-permute-start | bytes 2261000 | tf_op jit(solution)/shard_map/ppermute | solution.py:59
  17.4 2.7 %collective-permute-start.3 = (bf16[160,1024]{1,0:T(8,128)(2,1)S(1)}, bf16[160,1024]{1,0:T(8,128)(2,1)S(1)}, u32[]{:S(2)}, u32[]{:S(2)}) collective-permute-start(bf16[160,1024]{1,0:T(8,128)(2,1)S(1)} %collective-permute-done.refs_1_), channel_id=1, source_target_pairs={{0,28},{1,29},{2,30},{3,31},{4,0},{5,1},{6,2},{7,3},{8,4},{9,5},{1... | collective-permute-start | bytes 983048 | tf_op jit(solution)/shard_map/ppermute | solution.py:54
  20.0 0.7 fusion.13
  20.7 2.5 %fusion.12 = f32[128]{0:T(128)S(1)} fusion(s32[1,128]{1,0:T(1,128)S(1)} %copy-done.23, f32[128]{0:T(128)S(1)} %copy-done.24, f32[128]{0:T(128)S(1)} %copy-done.25, f32[]{:T(128)} %bitcast.6, f32[]{:T(128)} %bitcast.5, f32[]{:T(128)} %bitcast.4, f32[]{:T(128)} %bitcast.3), kind=kLoop, calls=%fused_computation.40 | loop fusion | flops 1920 | bytes 2064 | tf_op jit(solution)/shard_map/mul | solution.py:463
  23.2 3.0 %collective-permute-done.2.refs_4_ = bf16[160,1024]{1,0:T(8,128)(2,1)S(1)} collective-permute-done((bf16[160,1024]{1,0:T(8,128)(2,1)S(1)}, bf16[160,1024]{1,0:T(8,128)(2,1)S(1)}, u32[]{:S(2)}, u32[]{:S(2)}) %collective-permute-start.2) | collective-permute-done | bytes 327712 | tf_op jit(solution)/shard_map/ppermute | solution.py:54
  26.3 2.7 %collective-permute-start.4 = (bf16[160,1024]{1,0:T(8,128)(2,1)S(1)}, bf16[160,1024]{1,0:T(8,128)(2,1)S(1)}, u32[]{:S(2)}, u32[]{:S(2)}) collective-permute-start(bf16[160,1024]{1,0:T(8,128)(2,1)S(1)} %collective-permute-done.3.refs_3_), channel_id=1, source_target_pairs={{0,28},{1,29},{2,30},{3,31},{4,0},{5,1},{6,2},{7,3},{8,4},{9,5},{1... | collective-permute-start | bytes 983048 | tf_op jit(solution)/shard_map/ppermute | solution.py:54
  28.9 4.5 %collective-permute-done.8.refs_9_.up = bf16[2944,128]{1,0:T(8,128)(2,1)S(1)} collective-permute-done((bf16[2944,128]{1,0:T(8,128)(2,1)}, bf16[2944,128]{1,0:T(8,128)(2,1)S(1)}, u32[]{:S(2)}, u32[]{:S(2)}) %collective-permute-start.8) | collective-permute-done | bytes 753696 | tf_op jit(solution)/shard_map/ppermute | solution.py:59
  33.6 2.7 %collective-permute-start.11 = (bf16[1152,128]{1,0:T(8,128)(2,1)S(1)}, bf16[1152,128]{1,0:T(8,128)(2,1)S(1)}, u32[]{:S(2)}, u32[]{:S(2)}) collective-permute-start(bf16[1152,128]{1,0:T(8,128)(2,1)S(1)} %slice.59), channel_id=1, source_target_pairs={{0,3},{1,0},{2,1},{3,2},{4,7},{5,4},{6,5},{7,6},{8,11},{9,8},{10,9... | collective-permute-start | bytes 884744 | tf_op jit(solution)/shard_map/ppermute | solution.py:59
  36.5 2.9 %collective-permute-start.7 = (bf16[80,1024]{1,0:T(8,128)(2,1)S(1)}, bf16[80,1024]{1,0:T(8,128)(2,1)S(1)}, u32[]{:S(2)}, u32[]{:S(2)}) collective-permute-start(bf16[80,1024]{1,0:T(8,128)(2,1)S(1)} %slice.57), channel_id=1, source_target_pairs={{0,28},{1,29},{2,30},{3,31},{4,0},{5,1},{6,2},{7,3},{8,4},{9,5},{1... | collective-permute-start | bytes 491528 | tf_op jit(solution)/shard_map/ppermute | solution.py:54
  39.4 2.7 %collective-permute-done.6 = bf16[80,1024]{1,0:T(8,128)(2,1)S(1)} collective-permute-done((bf16[80,1024]{1,0:T(8,128)(2,1)S(1)}, bf16[80,1024]{1,0:T(8,128)(2,1)S(1)}, u32[]{:S(2)}, u32[]{:S(2)}) %collective-permute-start.6) | collective-permute-done | bytes 163872 | tf_op jit(solution)/shard_map/ppermute | solution.py:54
  42.2 3.8 %back.1 = (bf16[8,160,128]{2,1,0:T(8,128)(2,1)S(1)}, bf16[8,160,128]{2,1,0:T(8,128)(2,1)S(1)}, bf16[8,160,128]{2,1,0:T(8,128)(2,1)}, bf16[8,160,128]{2,1,0:T(8,128)(2,1)}) custom-call(bf16[160,1024]{1,0:T(8,128)(2,1)S(1)} %multiply_convert_fusion.refs_0_, bf16[160,1024]{1,0:T(8,128)(2,1)S(1)} %collective-permute-done.refs_1_, ...), custom_call_target="tpu_custom_call" | custom-call | flops 1342177280 | bytes 5242880 | tf_op jit(solution)/shard_map/back/pallas_call | solution.py:255
  46.0 1.7 %collective-permute-start.12 = (bf16[8,160,128]{2,1,0:T(8,128)(2,1)S(1)}, bf16[8,160,128]{2,1,0:T(8,128)(2,1)S(1)}, u32[]{:S(2)}, u32[]{:S(2)}) collective-permute-start(bf16[8,160,128]{2,1,0:T(8,128)(2,1)S(1)} %get-tuple-element.56), channel_id=1, source_target_pairs={{0,3},{1,0},{2,1},{3,2},{4,7},{5,4},{6,5},{7,6},{8,11},{9,8},{10,9... | collective-permute-start | bytes 983048 | tf_op jit(solution)/shard_map/ppermute | solution.py:59
  47.7 0.6 collective-permute-start.14
  48.3 2.1 %weight_terms.1 = (bf16[160,1024]{1,0:T(8,128)(2,1)S(1)}, bf16[160,1024]{1,0:T(8,128)(2,1)S(1)}, bf16[160,1024]{1,0:T(8,128)(2,1)S(1)}, bf16[80,1024]{1,0:T(8,12...) custom-call(bf16[1280,128]{1,0:T(8,128)(2,1)S(1)} %copy-done.3, ...), custom_call_target="tpu_custom_call" | custom-call | flops 1342177280 | bytes 6291456 | tf_op jit(solution)/shard_map/weight_terms/pallas_call | solution.py:230
  50.4 0.7 copy-done.4
  51.1 0.7 copy-done.6
  51.8 0.7 copy-done.8
  52.6 0.7 copy-done.10
  53.3 0.7 copy-done.13
  54.0 0.6 copy-done.15
  54.6 0.7 copy-done.17
  55.3 0.7 copy-done.19
  56.0 0.7 copy-done.21
  56.6 2.7 %collective-permute-start.29 = (bf16[80,1024]{1,0:T(8,128)(2,1)}, bf16[80,1024]{1,0:T(8,128)(2,1)S(1)}, u32[]{:S(2)}, u32[]{:S(2)}) collective-permute-start(bf16[80,1024]{1,0:T(8,128)(2,1)} %copy-done.21), channel_id=1, source_target_pairs={{0,28},{1,29},{2,30},{3,31},{4,0},{5,1},{6,2},{7,3},{8,4},{9,5},{1... | collective-permute-start | bytes 491528 | tf_op jit(solution)/shard_map/ppermute | solution.py:54
  59.3 6.1 %collective-permute-done.14.refs_3_ = bf16[8,160,128]{2,1,0:T(8,128)(2,1)S(1)} collective-permute-done((bf16[8,160,128]{2,1,0:T(8,128)(2,1)}, bf16[8,160,128]{2,1,0:T(8,128)(2,1)S(1)}, u32[]{:S(2)}, u32[]{:S(2)}) %collective-permute-start.14) | collective-permute-done | bytes 327712 | tf_op jit(solution)/shard_map/ppermute | solution.py:59
  65.5 0.9 local_terms.1
  66.4 0.9 collective-permute-start.17
  67.3 0.1 collective-permute-start.15
  67.4 1.0 add_convert_fusion.5
  68.7 2.7 %collective-permute-start.30 = (bf16[160,1024]{1,0:T(8,128)(2,1)S(1)}, bf16[160,1024]{1,0:T(8,128)(2,1)S(1)}, u32[]{:S(2)}, u32[]{:S(2)}) collective-permute-start(bf16[160,1024]{1,0:T(8,128)(2,1)S(1)} %pad_maximum_fusion.2), channel_id=1, source_target_pairs={{0,28},{1,29},{2,30},{3,31},{4,0},{5,1},{6,2},{7,3},{8,4},{9,5},{1... | collective-permute-start | bytes 983048 | tf_op jit(solution)/shard_map/ppermute | solution.py:54
  71.4 0.1 fusion.3
  71.5 1.3 %collective-permute-start.18 = (bf16[2,4,160,128]{3,2,1,0:T(8,128)(2,1)S(1)}, bf16[2,4,160,128]{3,2,1,0:T(8,128)(2,1)S(1)}, u32[]{:S(2)}, u32[]{:S(2)}) collective-permute-start(bf16[2,4,160,128]{3,2,1,0:T(8,128)(2,1)S(1)} %fusion.3), channel_id=1, source_target_pairs={{192,0},{224,32},{193,1},{225,33},{194,2},{226,34},{195,3},{227,35... | collective-permute-start | bytes 983048 | tf_op jit(solution)/shard_map/ppermute | solution.py:68
  72.8 0.7 collective-permute-start.20
  73.5 0.1 fusion
  73.6 1.5 %collective-permute-start.16 = (bf16[2,4,160,128]{3,2,1,0:T(8,128)(2,1)S(1)}, bf16[2,4,160,128]{3,2,1,0:T(8,128)(2,1)S(1)}, u32[]{:S(2)}, u32[]{:S(2)}) collective-permute-start(bf16[2,4,160,128]{3,2,1,0:T(8,128)(2,1)S(1)} %fusion), channel_id=1, source_target_pairs={{192,0},{224,32},{193,1},{225,33},{194,2},{226,34},{195,3},{227,35... | collective-permute-start | bytes 983048 | tf_op jit(solution)/shard_map/ppermute | solution.py:68
  75.1 1.6 %base_terms.1.refs_8_ = f32[128,5120]{1,0:T(8,128)S(1)} custom-call(bf16[2,4,160,128]{3,2,1,0:T(8,128)(2,1)S(1)} %get-tuple-element.60.refs_0_, bf16[2,4,160,128]{3,2,1,0:T(8,128)(2,1)S(1)} %get-tuple-element.62.refs_1_, bf16[2,4,160,128]{3,2,1,0:T(8,128)(2,1)S(1)} %collective-permute-done.15.refs_2_, ...), custom_call_target="tpu_custom_call" | custom-call | bytes 8388608 | tf_op jit(solution)/shard_map/base_terms/pallas_call | solution.py:354
  76.7 0.1 collective-permute-done.26
  76.8 0.7 collective-permute-start.19
  77.5 0.1 add_convert_fusion.3
  77.6 1.9 %collective-permute-start.27 = (bf16[160,1024]{1,0:T(8,128)(2,1)S(1)}, bf16[160,1024]{1,0:T(8,128)(2,1)S(1)}, u32[]{:S(2)}, u32[]{:S(2)}) collective-permute-start(bf16[160,1024]{1,0:T(8,128)(2,1)S(1)} %add_convert_fusion.3), channel_id=1, source_target_pairs={{0,4},{1,5},{2,6},{3,7},{4,8},{5,9},{6,10},{7,11},{8,12},{9,13},{1... | collective-permute-start | bytes 983048 | tf_op jit(solution)/shard_map/ppermute | solution.py:54
  79.5 0.1 add_convert_fusion.1
  79.6 1.5 %collective-permute-done.18.refs_1_ = bf16[2,4,160,128]{3,2,1,0:T(8,128)(2,1)S(1)} collective-permute-done((bf16[2,4,160,128]{3,2,1,0:T(8,128)(2,1)S(1)}, bf16[2,4,160,128]{3,2,1,0:T(8,128)(2,1)S(1)}, u32[]{:S(2)}, u32[]{:S(2)}) %collective-permute-start.18) | collective-permute-done | bytes 327712 | tf_op jit(solution)/shard_map/ppermute | solution.py:68
  81.1 0.8 collective-permute-start.31
  81.9 0.1 fusion.7
  82.0 2.6 %collective-permute-start.22 = (bf16[2,4,160,128]{3,2,1,0:T(8,128)(2,1)S(1)}, bf16[2,4,160,128]{3,2,1,0:T(8,128)(2,1)S(1)}, u32[]{:S(2)}, u32[]{:S(2)}) collective-permute-start(bf16[2,4,160,128]{3,2,1,0:T(8,128)(2,1)S(1)} %fusion.7), channel_id=1, source_target_pairs={{0,64},{32,96},{64,0},{96,32},{1,65},{33,97},{65,1},{97,33},{2,66}... | collective-permute-start | bytes 983048 | tf_op jit(solution)/shard_map/ppermute | solution.py:68
  84.6 3.5 %collective-permute-done.16.refs_0_ = bf16[2,4,160,128]{3,2,1,0:T(8,128)(2,1)S(1)} collective-permute-done((bf16[2,4,160,128]{3,2,1,0:T(8,128)(2,1)S(1)}, bf16[2,4,160,128]{3,2,1,0:T(8,128)(2,1)S(1)}, u32[]{:S(2)}, u32[]{:S(2)}) %collective-permute-start.16) | collective-permute-done | bytes 327712 | tf_op jit(solution)/shard_map/ppermute | solution.py:68
  88.1 0.1 fusion.6
  88.2 3.6 %collective-permute-start.21 = (bf16[2,4,160,128]{3,2,1,0:T(8,128)(2,1)S(1)}, bf16[2,4,160,128]{3,2,1,0:T(8,128)(2,1)S(1)}, u32[]{:S(2)}, u32[]{:S(2)}) collective-permute-start(bf16[2,4,160,128]{3,2,1,0:T(8,128)(2,1)S(1)} %fusion.6), channel_id=1, source_target_pairs={{0,64},{32,96},{64,0},{96,32},{1,65},{33,97},{65,1},{97,33},{2,66}... | collective-permute-start | bytes 983048 | tf_op jit(solution)/shard_map/ppermute | solution.py:68
  91.8 0.1 add_convert_fusion.2
  92.0 0.1 add_convert_fusion
  92.2 2.7 %collective-permute-start.32 = (bf16[160,1024]{1,0:T(8,128)(2,1)S(1)}, bf16[160,1024]{1,0:T(8,128)(2,1)S(1)}, u32[]{:S(2)}, u32[]{:S(2)}) collective-permute-start(bf16[160,1024]{1,0:T(8,128)(2,1)S(1)} %add_convert_fusion), channel_id=1, source_target_pairs={{0,28},{1,29},{2,30},{3,31},{4,0},{5,1},{6,2},{7,3},{8,4},{9,5},{1... | collective-permute-start | bytes 983048 | tf_op jit(solution)/shard_map/ppermute | solution.py:54
  94.9 0.2 fusion.5
  95.1 5.7 %collective-permute-start.24 = (bf16[2,4,160,128]{3,2,1,0:T(8,128)(2,1)S(1)}, bf16[2,4,160,128]{3,2,1,0:T(8,128)(2,1)S(1)}, u32[]{:S(2)}, u32[]{:S(2)}) collective-permute-start(bf16[2,4,160,128]{3,2,1,0:T(8,128)(2,1)S(1)} %fusion.5), channel_id=1, source_target_pairs={{0,32},{32,0},{64,96},{96,64},{128,160},{160,128},{192,224},{224,1... | collective-permute-start | bytes 983048 | tf_op jit(solution)/shard_map/ppermute | solution.py:63
  100.7 0.2 fusion.2
  100.9 3.3 %collective-permute-start.23 = (bf16[2,4,160,128]{3,2,1,0:T(8,128)(2,1)S(1)}, bf16[2,4,160,128]{3,2,1,0:T(8,128)(2,1)S(1)}, u32[]{:S(2)}, u32[]{:S(2)}) collective-permute-start(bf16[2,4,160,128]{3,2,1,0:T(8,128)(2,1)S(1)} %fusion.2), channel_id=1, source_target_pairs={{0,32},{32,0},{64,96},{96,64},{128,160},{160,128},{192,224},{224,1... | collective-permute-start | bytes 983048 | tf_op jit(solution)/shard_map/ppermute | solution.py:63
  104.3 1.0 multiply_bitcast_fusion
  105.2 0.3 collective-permute-done.23.refs_6_
  105.5 1.5 %finish.1 = bf16[128,5120]{1,0:T(8,128)(2,1)} custom-call(bf16[2,4,160,128]{3,2,1,0:T(8,128)(2,1)S(1)} %collective-permute-done.16.refs_0_, bf16[2,4,160,128]{3,2,1,0:T(8,128)(2,1)S(1)} %collective-permute-done.18.refs_1_, bf16[2,4,160,128]{3,2,1,0:T(8,128)(2,1)S(1)} %collective-permute-done.19.refs_2_, ...), custom_call_target="tpu_custom_call" | custom-call | bytes 6291456 | tf_op jit(solution)/shard_map/finish/pallas_call | solution.py:391
  (84 shorter events, 0.7 us)
Async XLA Ops:
  2.4 14.9 %collective-permute-start.1 = (bf16[160,1024]{1,0:T(8,128)(2,1)S(1)}, bf16[160,1024]{1,0:T(8,128)(2,1)S(1)}, u32[]{:S(2)}, u32[]{:S(2)}) collective-permute-start(bf16[160,1024]{1,0:T(8,128)(2,1)S(1)} %multiply_convert_fusion.refs_0_), channel_id=1, source_target_pairs={{0,4},{1,5},{2,6},{3,7},{4,8},{5,9},{6,10},{7,11},{8,12},{9,13},{1... | collective-permute-start | bytes 983048 | tf_op jit(solution)/shard_map/ppermute | solution.py:54
  5.0 12.4 %collective-permute-start = (bf16[160,1024]{1,0:T(8,128)(2,1)S(1)}, bf16[160,1024]{1,0:T(8,128)(2,1)S(1)}, u32[]{:S(2)}, u32[]{:S(2)}) collective-permute-start(bf16[160,1024]{1,0:T(8,128)(2,1)S(1)} %multiply_convert_fusion.refs_0_), channel_id=1, source_target_pairs={{0,28},{1,29},{2,30},{3,31},{4,0},{5,1},{6,2},{7,3},{8,4},{9,5},{1... | collective-permute-start | bytes 983048 | tf_op jit(solution)/shard_map/ppermute | solution.py:54
  9.0 11.0 %copy-start.22 = (f32[1,4]{1,0:T(1,128)S(1)}, f32[1,4]{1,0:T(1,128)}, u32[]{:S(2)}) copy-start(f32[1,4]{1,0:T(1,128)} %param.24) | copy-start | bytes 52
  9.0 11.7 %copy-start.23 = (s32[1,128]{1,0:T(1,128)S(1)}, s32[1,128]{1,0:T(1,128)}, u32[]{:S(2)}) copy-start(s32[1,128]{1,0:T(1,128)} %refs_1_.1) | copy-start | bytes 1540
  9.0 11.7 %copy-start.24 = (f32[128]{0:T(128)S(1)}, f32[128]{0:T(128)}, u32[]{:S(2)}) copy-start(f32[128]{0:T(128)} %param.22) | copy-start | bytes 1540
  9.0 11.7 %copy-start.25 = (f32[128]{0:T(128)S(1)}, f32[128]{0:T(128)}, u32[]{:S(2)}) copy-start(f32[128]{0:T(128)} %param.23) | copy-start | bytes 1540
  14.6 27.6 %copy-start.12 = (bf16[1024,128]{1,0:T(8,128)(2,1)S(1)}, bf16[1024,128]{1,0:T(8,128)(2,1)}, u32[]{:S(2)}) copy-start(bf16[1024,128]{1,0:T(8,128)(2,1)} %get-tuple-element.66.refs_8_.cots) | copy-start | bytes 786436
  14.6 18.9 %collective-permute-start.8 = (bf16[2944,128]{1,0:T(8,128)(2,1)}, bf16[2944,128]{1,0:T(8,128)(2,1)S(1)}, u32[]{:S(2)}, u32[]{:S(2)}) collective-permute-start(bf16[2944,128]{1,0:T(8,128)(2,1)} %get-tuple-element.53.refs_5_), channel_id=1, source_target_pairs={{0,1},{1,2},{2,3},{3,0},{4,5},{5,6},{6,7},{7,4},{8,9},{9,10},{10,1... | collective-permute-start | bytes 2261000 | tf_op jit(solution)/shard_map/ppermute | solution.py:59
  15.9 17.7 %collective-permute-start.9 = (bf16[2944,128]{1,0:T(8,128)(2,1)}, bf16[2944,128]{1,0:T(8,128)(2,1)S(1)}, u32[]{:S(2)}, u32[]{:S(2)}) collective-permute-start(bf16[2944,128]{1,0:T(8,128)(2,1)} %get-tuple-element.54.refs_6_), channel_id=1, source_target_pairs={{0,3},{1,0},{2,1},{3,2},{4,7},{5,4},{6,5},{7,6},{8,11},{9,8},{10,9... | collective-permute-start | bytes 2261000 | tf_op jit(solution)/shard_map/ppermute | solution.py:59
  17.3 8.9 %collective-permute-start.2 = (bf16[160,1024]{1,0:T(8,128)(2,1)S(1)}, bf16[160,1024]{1,0:T(8,128)(2,1)S(1)}, u32[]{:S(2)}, u32[]{:S(2)}) collective-permute-start(bf16[160,1024]{1,0:T(8,128)(2,1)S(1)} %collective-permute-done.1.refs_2_), channel_id=1, source_target_pairs={{0,4},{1,5},{2,6},{3,7},{4,8},{5,9},{6,10},{7,11},{8,12},{9,13},{1... | collective-permute-start | bytes 983048 | tf_op jit(solution)/shard_map/ppermute | solution.py:54
  17.4 8.9 %collective-permute-start.3 = (bf16[160,1024]{1,0:T(8,128)(2,1)S(1)}, bf16[160,1024]{1,0:T(8,128)(2,1)S(1)}, u32[]{:S(2)}, u32[]{:S(2)}) collective-permute-start(bf16[160,1024]{1,0:T(8,128)(2,1)S(1)} %collective-permute-done.refs_1_), channel_id=1, source_target_pairs={{0,28},{1,29},{2,30},{3,31},{4,0},{5,1},{6,2},{7,3},{8,4},{9,5},{1... | collective-permute-start | bytes 983048 | tf_op jit(solution)/shard_map/ppermute | solution.py:54
  26.3 10.1 %collective-permute-start.5 = (bf16[160,1024]{1,0:T(8,128)(2,1)S(1)}, bf16[160,1024]{1,0:T(8,128)(2,1)S(1)}, u32[]{:S(2)}, u32[]{:S(2)}) collective-permute-start(bf16[160,1024]{1,0:T(8,128)(2,1)S(1)} %collective-permute-done.2.refs_4_), channel_id=1, source_target_pairs={{0,4},{1,5},{2,6},{3,7},{4,8},{5,9},{6,10},{7,11},{8,12},{9,13},{1... | collective-permute-start | bytes 983048 | tf_op jit(solution)/shard_map/ppermute | solution.py:54
  26.3 10.2 %collective-permute-start.4 = (bf16[160,1024]{1,0:T(8,128)(2,1)S(1)}, bf16[160,1024]{1,0:T(8,128)(2,1)S(1)}, u32[]{:S(2)}, u32[]{:S(2)}) collective-permute-start(bf16[160,1024]{1,0:T(8,128)(2,1)S(1)} %collective-permute-done.3.refs_3_), channel_id=1, source_target_pairs={{0,28},{1,29},{2,30},{3,31},{4,0},{5,1},{6,2},{7,3},{8,4},{9,5},{1... | collective-permute-start | bytes 983048 | tf_op jit(solution)/shard_map/ppermute | solution.py:54
  33.5 8.7 %collective-permute-start.10 = (bf16[1152,128]{1,0:T(8,128)(2,1)S(1)}, bf16[1152,128]{1,0:T(8,128)(2,1)S(1)}, u32[]{:S(2)}, u32[]{:S(2)}) collective-permute-start(bf16[1152,128]{1,0:T(8,128)(2,1)S(1)} %slice.58), channel_id=1, source_target_pairs={{0,1},{1,2},{2,3},{3,0},{4,5},{5,6},{6,7},{7,4},{8,9},{9,10},{10,1... | collective-permute-start | bytes 884744 | tf_op jit(solution)/shard_map/ppermute | solution.py:59
  33.6 8.5 %collective-permute-start.11 = (bf16[1152,128]{1,0:T(8,128)(2,1)S(1)}, bf16[1152,128]{1,0:T(8,128)(2,1)S(1)}, u32[]{:S(2)}, u32[]{:S(2)}) collective-permute-start(bf16[1152,128]{1,0:T(8,128)(2,1)S(1)} %slice.59), channel_id=1, source_target_pairs={{0,3},{1,0},{2,1},{3,2},{4,7},{5,4},{6,5},{7,6},{8,11},{9,8},{10,9... | collective-permute-start | bytes 884744 | tf_op jit(solution)/shard_map/ppermute | solution.py:59
  36.4 5.8 %collective-permute-start.6 = (bf16[80,1024]{1,0:T(8,128)(2,1)S(1)}, bf16[80,1024]{1,0:T(8,128)(2,1)S(1)}, u32[]{:S(2)}, u32[]{:S(2)}) collective-permute-start(bf16[80,1024]{1,0:T(8,128)(2,1)S(1)} %slice.56), channel_id=1, source_target_pairs={{0,4},{1,5},{2,6},{3,7},{4,8},{5,9},{6,10},{7,11},{8,12},{9,13},{1... | collective-permute-start | bytes 491528 | tf_op jit(solution)/shard_map/ppermute | solution.py:54
  36.5 5.6 %collective-permute-start.7 = (bf16[80,1024]{1,0:T(8,128)(2,1)S(1)}, bf16[80,1024]{1,0:T(8,128)(2,1)S(1)}, u32[]{:S(2)}, u32[]{:S(2)}) collective-permute-start(bf16[80,1024]{1,0:T(8,128)(2,1)S(1)} %slice.57), channel_id=1, source_target_pairs={{0,28},{1,29},{2,30},{3,31},{4,0},{5,1},{6,2},{7,3},{8,4},{9,5},{1... | collective-permute-start | bytes 491528 | tf_op jit(solution)/shard_map/ppermute | solution.py:54
  42.2 6.1 %copy-start.3 = (bf16[1280,128]{1,0:T(8,128)(2,1)S(1)}, bf16[1280,128]{1,0:T(8,128)(2,1)}, u32[]{:S(2)}) copy-start(bf16[1280,128]{1,0:T(8,128)(2,1)} %get-tuple-element.59.refs_4_.near) | copy-start | bytes 983044
  46.0 9.9 %collective-permute-start.12 = (bf16[8,160,128]{2,1,0:T(8,128)(2,1)S(1)}, bf16[8,160,128]{2,1,0:T(8,128)(2,1)S(1)}, u32[]{:S(2)}, u32[]{:S(2)}) collective-permute-start(bf16[8,160,128]{2,1,0:T(8,128)(2,1)S(1)} %get-tuple-element.56), channel_id=1, source_target_pairs={{0,3},{1,0},{2,1},{3,2},{4,7},{5,4},{6,5},{7,6},{8,11},{9,8},{10,9... | collective-permute-start | bytes 983048 | tf_op jit(solution)/shard_map/ppermute | solution.py:59
  47.7 11.6 %collective-permute-start.13 = (bf16[8,160,128]{2,1,0:T(8,128)(2,1)}, bf16[8,160,128]{2,1,0:T(8,128)(2,1)S(1)}, u32[]{:S(2)}, u32[]{:S(2)}) collective-permute-start(bf16[8,160,128]{2,1,0:T(8,128)(2,1)} %get-tuple-element.57), channel_id=1, source_target_pairs={{0,2},{1,3},{2,0},{3,1},{4,6},{5,7},{6,4},{7,5},{8,10},{9,11},{10,... | collective-permute-start | bytes 983048 | tf_op jit(solution)/shard_map/ppermute | solution.py:59
  47.7 17.7 %collective-permute-start.14 = (bf16[8,160,128]{2,1,0:T(8,128)(2,1)}, bf16[8,160,128]{2,1,0:T(8,128)(2,1)S(1)}, u32[]{:S(2)}, u32[]{:S(2)}) collective-permute-start(bf16[8,160,128]{2,1,0:T(8,128)(2,1)} %get-tuple-element.58), channel_id=1, source_target_pairs={{0,1},{1,2},{2,3},{3,0},{4,5},{5,6},{6,7},{7,4},{8,9},{9,10},{10,1... | collective-permute-start | bytes 983048 | tf_op jit(solution)/shard_map/ppermute | solution.py:59
  48.3 17.1 %copy-start.1 = (bf16[2944,128]{1,0:T(8,128)(2,1)S(1)}, bf16[2944,128]{1,0:T(8,128)(2,1)}, u32[]{:S(2)}) copy-start(bf16[2944,128]{1,0:T(8,128)(2,1)} %get-tuple-element.53.refs_5_) | copy-start | bytes 2260996
  48.3 17.1 %copy-start.2 = (bf16[2944,128]{1,0:T(8,128)(2,1)S(1)}, bf16[2944,128]{1,0:T(8,128)(2,1)}, u32[]{:S(2)}) copy-start(bf16[2944,128]{1,0:T(8,128)(2,1)} %get-tuple-element.54.refs_6_) | copy-start | bytes 2260996
  50.4 0.7 copy-start.4
  51.1 0.7 copy-start.6
  51.8 0.7 copy-start.8
  52.6 0.7 copy-start.10
  53.3 0.7 copy-start.13
  54.0 0.6 copy-start.15
  54.6 0.7 copy-start.17
  55.3 0.7 copy-start.19
  56.0 0.7 copy-start.21
  56.6 10.8 %collective-permute-start.25 = (bf16[80,1024]{1,0:T(8,128)(2,1)}, bf16[80,1024]{1,0:T(8,128)(2,1)}, u32[]{:S(2)}, u32[]{:S(2)}) collective-permute-start(bf16[80,1024]{1,0:T(8,128)(2,1)} %get-tuple-element.86), channel_id=1, source_target_pairs={{0,4},{1,5},{2,6},{3,7},{4,8},{5,9},{6,10},{7,11},{8,12},{9,13},{1... | collective-permute-start | bytes 491528 | tf_op jit(solution)/shard_map/ppermute | solution.py:54
  56.6 10.8 %copy-start.20 = (bf16[80,1024]{1,0:T(8,128)(2,1)S(1)}, bf16[80,1024]{1,0:T(8,128)(2,1)}, u32[]{:S(2)}) copy-start(bf16[80,1024]{1,0:T(8,128)(2,1)} %copy-done.19) | copy-start | bytes 491524
  56.6 11.8 %copy-start.16 = (bf16[80,1024]{1,0:T(8,128)(2,1)S(1)}, bf16[80,1024]{1,0:T(8,128)(2,1)}, u32[]{:S(2)}) copy-start(bf16[80,1024]{1,0:T(8,128)(2,1)} %copy-done.15) | copy-start | bytes 491524
  56.6 11.9 %copy-start.18 = (bf16[80,1024]{1,0:T(8,128)(2,1)S(1)}, bf16[80,1024]{1,0:T(8,128)(2,1)}, u32[]{:S(2)}) copy-start(bf16[80,1024]{1,0:T(8,128)(2,1)} %copy-done.17) | copy-start | bytes 491524
  56.6 11.9 %collective-permute-start.29 = (bf16[80,1024]{1,0:T(8,128)(2,1)}, bf16[80,1024]{1,0:T(8,128)(2,1)S(1)}, u32[]{:S(2)}, u32[]{:S(2)}) collective-permute-start(bf16[80,1024]{1,0:T(8,128)(2,1)} %copy-done.21), channel_id=1, source_target_pairs={{0,28},{1,29},{2,30},{3,31},{4,0},{5,1},{6,2},{7,3},{8,4},{9,5},{1... | collective-permute-start | bytes 491528 | tf_op jit(solution)/shard_map/ppermute | solution.py:54
  66.4 2.2 %copy-start.14 = (bf16[80,1024]{1,0:T(8,128)(2,1)S(1)}, bf16[80,1024]{1,0:T(8,128)(2,1)}, u32[]{:S(2)}) copy-start(bf16[80,1024]{1,0:T(8,128)(2,1)} %copy-done.13) | copy-start | bytes 491524
  66.4 5.0 %collective-permute-start.17 = (bf16[2,4,160,128]{3,2,1,0:T(8,128)(2,1)S(1)}, bf16[2,4,160,128]{3,2,1,0:T(8,128)(2,1)S(1)}, u32[]{:S(2)}, u32[]{:S(2)}) collective-permute-start(bf16[2,4,160,128]{3,2,1,0:T(8,128)(2,1)S(1)} %get-tuple-element.63.refs_5_), channel_id=1, source_target_pairs={{0,32},{32,0},{64,96},{96,64},{128,160},{160,128},{192,224},{224,1... | collective-permute-start | bytes 983048 | tf_op jit(solution)/shard_map/ppermute | solution.py:63
  67.3 6.1 %collective-permute-start.15 = (bf16[2,4,160,128]{3,2,1,0:T(8,128)(2,1)S(1)}, bf16[2,4,160,128]{3,2,1,0:T(8,128)(2,1)S(1)}, u32[]{:S(2)}, u32[]{:S(2)}) collective-permute-start(bf16[2,4,160,128]{3,2,1,0:T(8,128)(2,1)S(1)} %get-tuple-element.61.refs_4_), channel_id=1, source_target_pairs={{0,32},{32,0},{64,96},{96,64},{128,160},{160,128},{192,224},{224,1... | collective-permute-start | bytes 983048 | tf_op jit(solution)/shard_map/ppermute | solution.py:63
  68.4 8.4 %collective-permute-start.26 = (bf16[160,1024]{1,0:T(8,128)(2,1)S(1)}, bf16[160,1024]{1,0:T(8,128)(2,1)S(1)}, u32[]{:S(2)}, u32[]{:S(2)}) collective-permute-start(bf16[160,1024]{1,0:T(8,128)(2,1)S(1)} %pad_maximum_fusion.1), channel_id=1, source_target_pairs={{0,4},{1,5},{2,6},{3,7},{4,8},{5,9},{6,10},{7,11},{8,12},{9,13},{1... | collective-permute-start | bytes 983048 | tf_op jit(solution)/shard_map/ppermute | solution.py:54
  68.6 6.5 %copy-start = (bf16[128,5120]{1,0:T(8,128)(2,1)S(1)}, bf16[128,5120]{1,0:T(8,128)(2,1)}, u32[]{:S(2)}) copy-start(bf16[128,5120]{1,0:T(8,128)(2,1)} %refs_6_.1) | copy-start | bytes 3932164
  68.7 8.9 %collective-permute-start.30 = (bf16[160,1024]{1,0:T(8,128)(2,1)S(1)}, bf16[160,1024]{1,0:T(8,128)(2,1)S(1)}, u32[]{:S(2)}, u32[]{:S(2)}) collective-permute-start(bf16[160,1024]{1,0:T(8,128)(2,1)S(1)} %pad_maximum_fusion.2), channel_id=1, source_target_pairs={{0,28},{1,29},{2,30},{3,31},{4,0},{5,1},{6,2},{7,3},{8,4},{9,5},{1... | collective-permute-start | bytes 983048 | tf_op jit(solution)/shard_map/ppermute | solution.py:54
  71.5 9.6 %collective-permute-start.18 = (bf16[2,4,160,128]{3,2,1,0:T(8,128)(2,1)S(1)}, bf16[2,4,160,128]{3,2,1,0:T(8,128)(2,1)S(1)}, u32[]{:S(2)}, u32[]{:S(2)}) collective-permute-start(bf16[2,4,160,128]{3,2,1,0:T(8,128)(2,1)S(1)} %fusion.3), channel_id=1, source_target_pairs={{192,0},{224,32},{193,1},{225,33},{194,2},{226,34},{195,3},{227,35... | collective-permute-start | bytes 983048 | tf_op jit(solution)/shard_map/ppermute | solution.py:68
  72.8 9.1 %collective-permute-start.20 = (bf16[2,4,160,128]{3,2,1,0:T(8,128)(2,1)S(1)}, bf16[2,4,160,128]{3,2,1,0:T(8,128)(2,1)S(1)}, u32[]{:S(2)}, u32[]{:S(2)}) collective-permute-start(bf16[2,4,160,128]{3,2,1,0:T(8,128)(2,1)S(1)} %fusion.3), channel_id=1, source_target_pairs={{192,128},{224,160},{128,64},{160,96},{193,129},{225,161},{129,65}... | collective-permute-start | bytes 983048 | tf_op jit(solution)/shard_map/ppermute | solution.py:68
  73.6 14.5 %collective-permute-start.16 = (bf16[2,4,160,128]{3,2,1,0:T(8,128)(2,1)S(1)}, bf16[2,4,160,128]{3,2,1,0:T(8,128)(2,1)S(1)}, u32[]{:S(2)}, u32[]{:S(2)}) collective-permute-start(bf16[2,4,160,128]{3,2,1,0:T(8,128)(2,1)S(1)} %fusion), channel_id=1, source_target_pairs={{192,0},{224,32},{193,1},{225,33},{194,2},{226,34},{195,3},{227,35... | collective-permute-start | bytes 983048 | tf_op jit(solution)/shard_map/ppermute | solution.py:68
  75.1 2.4 %copy-start.11 = (bf16[160,1024]{1,0:T(8,128)(2,1)S(1)}, bf16[160,1024]{1,0:T(8,128)(2,1)}, u32[]{:S(2)}) copy-start(bf16[160,1024]{1,0:T(8,128)(2,1)} %copy-done.10) | copy-start | bytes 983044
  75.1 4.4 %copy-start.9 = (bf16[160,1024]{1,0:T(8,128)(2,1)S(1)}, bf16[160,1024]{1,0:T(8,128)(2,1)}, u32[]{:S(2)}) copy-start(bf16[160,1024]{1,0:T(8,128)(2,1)} %copy-done.8) | copy-start | bytes 983044
  76.8 11.3 %collective-permute-start.19 = (bf16[2,4,160,128]{3,2,1,0:T(8,128)(2,1)S(1)}, bf16[2,4,160,128]{3,2,1,0:T(8,128)(2,1)S(1)}, u32[]{:S(2)}, u32[]{:S(2)}) collective-permute-start(bf16[2,4,160,128]{3,2,1,0:T(8,128)(2,1)S(1)} %fusion), channel_id=1, source_target_pairs={{192,128},{224,160},{128,64},{160,96},{193,129},{225,161},{129,65}... | collective-permute-start | bytes 983048 | tf_op jit(solution)/shard_map/ppermute | solution.py:68
  77.6 14.2 %collective-permute-start.27 = (bf16[160,1024]{1,0:T(8,128)(2,1)S(1)}, bf16[160,1024]{1,0:T(8,128)(2,1)S(1)}, u32[]{:S(2)}, u32[]{:S(2)}) collective-permute-start(bf16[160,1024]{1,0:T(8,128)(2,1)S(1)} %add_convert_fusion.3), channel_id=1, source_target_pairs={{0,4},{1,5},{2,6},{3,7},{4,8},{5,9},{6,10},{7,11},{8,12},{9,13},{1... | collective-permute-start | bytes 983048 | tf_op jit(solution)/shard_map/ppermute | solution.py:54
  79.6 12.2 %copy-start.7 = (bf16[160,1024]{1,0:T(8,128)(2,1)S(1)}, bf16[160,1024]{1,0:T(8,128)(2,1)}, u32[]{:S(2)}) copy-start(bf16[160,1024]{1,0:T(8,128)(2,1)} %copy-done.6) | copy-start | bytes 983044
  81.1 10.9 %collective-permute-start.31 = (bf16[160,1024]{1,0:T(8,128)(2,1)S(1)}, bf16[160,1024]{1,0:T(8,128)(2,1)S(1)}, u32[]{:S(2)}, u32[]{:S(2)}) collective-permute-start(bf16[160,1024]{1,0:T(8,128)(2,1)S(1)} %add_convert_fusion.1), channel_id=1, source_target_pairs={{0,28},{1,29},{2,30},{3,31},{4,0},{5,1},{6,2},{7,3},{8,4},{9,5},{1... | collective-permute-start | bytes 983048 | tf_op jit(solution)/shard_map/ppermute | solution.py:54
  82.0 10.0 %copy-start.5 = (bf16[160,1024]{1,0:T(8,128)(2,1)S(1)}, bf16[160,1024]{1,0:T(8,128)(2,1)}, u32[]{:S(2)}) copy-start(bf16[160,1024]{1,0:T(8,128)(2,1)} %copy-done.4) | copy-start | bytes 983044
  82.0 12.9 %collective-permute-start.22 = (bf16[2,4,160,128]{3,2,1,0:T(8,128)(2,1)S(1)}, bf16[2,4,160,128]{3,2,1,0:T(8,128)(2,1)S(1)}, u32[]{:S(2)}, u32[]{:S(2)}) collective-permute-start(bf16[2,4,160,128]{3,2,1,0:T(8,128)(2,1)S(1)} %fusion.7), channel_id=1, source_target_pairs={{0,64},{32,96},{64,0},{96,32},{1,65},{33,97},{65,1},{97,33},{2,66}... | collective-permute-start | bytes 983048 | tf_op jit(solution)/shard_map/ppermute | solution.py:68
  88.2 12.5 %collective-permute-start.21 = (bf16[2,4,160,128]{3,2,1,0:T(8,128)(2,1)S(1)}, bf16[2,4,160,128]{3,2,1,0:T(8,128)(2,1)S(1)}, u32[]{:S(2)}, u32[]{:S(2)}) collective-permute-start(bf16[2,4,160,128]{3,2,1,0:T(8,128)(2,1)S(1)} %fusion.6), channel_id=1, source_target_pairs={{0,64},{32,96},{64,0},{96,32},{1,65},{33,97},{65,1},{97,33},{2,66}... | collective-permute-start | bytes 983048 | tf_op jit(solution)/shard_map/ppermute | solution.py:68
  91.9 12.3 %collective-permute-start.28 = (bf16[160,1024]{1,0:T(8,128)(2,1)S(1)}, bf16[160,1024]{1,0:T(8,128)(2,1)S(1)}, u32[]{:S(2)}, u32[]{:S(2)}) collective-permute-start(bf16[160,1024]{1,0:T(8,128)(2,1)S(1)} %add_convert_fusion.2), channel_id=1, source_target_pairs={{0,4},{1,5},{2,6},{3,7},{4,8},{5,9},{6,10},{7,11},{8,12},{9,13},{1... | collective-permute-start | bytes 983048 | tf_op jit(solution)/shard_map/ppermute | solution.py:54
  92.2 12.1 %collective-permute-start.32 = (bf16[160,1024]{1,0:T(8,128)(2,1)S(1)}, bf16[160,1024]{1,0:T(8,128)(2,1)S(1)}, u32[]{:S(2)}, u32[]{:S(2)}) collective-permute-start(bf16[160,1024]{1,0:T(8,128)(2,1)S(1)} %add_convert_fusion), channel_id=1, source_target_pairs={{0,28},{1,29},{2,30},{3,31},{4,0},{5,1},{6,2},{7,3},{8,4},{9,5},{1... | collective-permute-start | bytes 983048 | tf_op jit(solution)/shard_map/ppermute | solution.py:54
  95.1 10.2 %collective-permute-start.24 = (bf16[2,4,160,128]{3,2,1,0:T(8,128)(2,1)S(1)}, bf16[2,4,160,128]{3,2,1,0:T(8,128)(2,1)S(1)}, u32[]{:S(2)}, u32[]{:S(2)}) collective-permute-start(bf16[2,4,160,128]{3,2,1,0:T(8,128)(2,1)S(1)} %fusion.5), channel_id=1, source_target_pairs={{0,32},{32,0},{64,96},{96,64},{128,160},{160,128},{192,224},{224,1... | collective-permute-start | bytes 983048 | tf_op jit(solution)/shard_map/ppermute | solution.py:63
  100.9 4.6 %collective-permute-start.23 = (bf16[2,4,160,128]{3,2,1,0:T(8,128)(2,1)S(1)}, bf16[2,4,160,128]{3,2,1,0:T(8,128)(2,1)S(1)}, u32[]{:S(2)}, u32[]{:S(2)}) collective-permute-start(bf16[2,4,160,128]{3,2,1,0:T(8,128)(2,1)S(1)} %fusion.2), channel_id=1, source_target_pairs={{0,32},{32,0},{64,96},{96,64},{128,160},{160,128},{192,224},{224,1... | collective-permute-start | bytes 983048 | tf_op jit(solution)/shard_map/ppermute | solution.py:63
